TPU v7x, 32 devices: a whole 2x2x4 slice. The times are simulated.
32 devices in a mesh: ax: 8 (over z, x), sec: 4 (over y, core).
Axes of the slice: x: 2, y: 2, z: 4, core: 2. Of those that a mesh axis runs over, the one named last changes fastest.
Arguments:
- load: float32 [1024, 6, 1024], P('ax', None, 'sec'), may hold values from -6 to 6
- disp: float32 [1024, 6, 1024], P('ax', None, 'sec'), may hold values from -1.5 to 1.5
- stiff: float32 [1024, 6, 1024], P('ax', None, 'sec'), may hold values from 0.5 to 2
- hole: int32 [1024, 1024], P('ax', 'sec'), may hold values 0 or 1
- section_class: int32 [1024], P('ax'), may hold values from 0 to 3
- class_table: float32 [4, 6], replicated, may hold values from 0.5 to 2
- precond: float32 [6, 6, 1024], replicated, may hold values from -0.5 to 0.5, as said below
Outputs:
- disp_new: float32 [1024, 6, 1024], P('ax', None, 'sec')
- residual_new: float32 [1024, 6, 1024], P('ax', None, 'sec')
- stats: float32 [3], replicated
Inputs may be any that keep to these rules, and one draw needn't show every extreme that they name: `precond`: for each harmonic the matrix over the first two dimensions is symmetric and positive definite.
All inputs are finite; a program needn't handle non-finite values. No bound on the sum of `hole` on one device may be relied on, other than what follows from the above.
Results may differ from a plain program's by a relative error of at most 0.0075.
Values sent between devices are 32-bit elements; how exact they have to be, the bound alone decides.
No kernel may reach another device: no remote copies, remote signals or barrier semaphores. Data moves between devices by JAX's collectives and lax.ppermute only.
A program may use at most 64 MiB of HBM per device.

v0:
```python
import math

import jax
import jax.numpy as jnp
from jax import lax
from jax.sharding import PartitionSpec as P


def with_halo(x, sides, width, wrap):
    for axis, dim in sides:
        size, length = (lax.axis_size(axis), x.shape[dim])
        up = [(i, (i + 1) % size) for i in range(size if wrap else size - 1)]
        down = [(j, i) for i, j in up]
        last = lax.slice_in_dim(x, length - width, length, axis=dim)
        first = lax.slice_in_dim(x, 0, width, axis=dim)
        before = lax.ppermute(last, axis, up)
        after = lax.ppermute(first, axis, down)
        x = jnp.concatenate([before, x, after], axis=dim)
    return x


def swap_radial(field):
    extent = field.shape
    folded = field.reshape(extent[0], extent[1] // 2, 2, extent[2])
    return jnp.flip(folded, axis=2).reshape(extent)


def apply_operator(field, stiffness):
    axial_pad = with_halo(field, (("ax", 0),), 1, False)
    sector_pad = with_halo(field, (("sec", 2),), 1, True)
    beside = axial_pad[2:] + axial_pad[:-2]
    beside = beside + sector_pad[:, :, 2:] + sector_pad[:, :, :-2]
    return (stiffness + 4.5) * field - beside - 0.5 * swap_radial(field)


def harmonic_table(row_index, col_index, length):
    product = row_index[:, None] * col_index[None, :] % length
    angle = 2.0 * math.pi / length * product.astype(jnp.float32)
    return jnp.concatenate([jnp.cos(angle), jnp.sin(angle)], axis=1)


def scale_harmonics(block_inverse, spectrum):
    doubled = jnp.concatenate([block_inverse, block_inverse], axis=2)
    return jnp.sum(doubled[None] * spectrum[:, None], axis=2)


def shards(load, disp, stiff, hole, section_class, class_table, precond):
    slab_count, comp_count, sector_width = disp.shape
    sector_count = lax.axis_size("sec")
    around_cells = sector_width * sector_count
    total_axial = slab_count * lax.axis_size("ax")
    position = lax.axis_index("ax") * slab_count + jnp.arange(slab_count)
    taper = 1.0 + 2.0 * position.astype(jnp.float32) / (total_axial - 1)
    one_hot = (section_class[:, None] == jnp.arange(class_table.shape[0])[None, :]).astype(
        jnp.float32
    )
    factors = jnp.dot(one_hot, class_table, precision=lax.Precision.HIGHEST)
    stiffness = stiff * (factors * taper[:, None])[:, :, None]
    solid = (1 - hole).astype(jnp.float32)[:, None, :]
    residual = solid * (load - apply_operator(disp, stiffness))
    sector = lax.axis_index("sec")
    own_index = sector * sector_width + jnp.arange(sector_width)
    table = harmonic_table(jnp.arange(around_cells), own_index, around_cells)
    own_inverse = lax.dynamic_slice_in_dim(precond, sector * sector_width, sector_width, 2)
    initial = jnp.zeros((slab_count, comp_count, 2 * sector_width), jnp.float32)
    piece = lax.all_gather(residual, "sec", axis=2, tiled=True)
    span = piece.shape[2]
    table_rows = table
    flat = piece.reshape(-1, span)
    spectrum = jnp.dot(flat, table_rows, precision=lax.Precision.HIGHEST).reshape(initial.shape)
    scaled = scale_harmonics(own_inverse, spectrum).reshape(-1, 2 * sector_width)
    table_rows = table
    shares = lax.psum_scatter(
        lax.dot_general(
            table_rows, scaled, (((1,), (1,)), ((), ())), precision=lax.Precision.HIGHEST
        )
        / around_cells,
        "sec",
        scatter_dimension=0,
        tiled=True,
    )
    smoothed = shares.T.reshape(slab_count, comp_count, sector_width)
    prec = solid * smoothed
    image = solid * apply_operator(prec, stiffness)
    cell_total = slab_count * lax.axis_size("ax") * comp_count * around_cells
    inner_rz = lax.psum(jnp.sum(residual * prec), ("ax", "sec")) / cell_total
    inner_zq = lax.psum(jnp.sum(prec * image), ("ax", "sec")) / cell_total
    alpha = inner_rz / inner_zq
    residual_new = residual - alpha * image
    square_new = lax.psum(jnp.sum(residual_new * residual_new), ("ax", "sec")) / cell_total
    disp_new = disp + alpha * prec
    return (disp_new, residual_new, jnp.stack([inner_rz, inner_zq, square_new]))


def solution(mesh):
    in_specs = (
        P("ax", None, "sec"),
        P("ax", None, "sec"),
        P("ax", None, "sec"),
        P("ax", "sec"),
        P("ax"),
        P(),
        P(),
    )
    out_specs = (P("ax", None, "sec"), P("ax", None, "sec"), P())
    return jax.shard_map(shards, mesh=mesh, in_specs=in_specs, out_specs=out_specs, check_vma=False)
```

profile of v0, /device:TPU:0, one launch (start us, length us, event | category | flops | bytes accessed | tf_op | source)
XLA Modules:
  0.0 225.0 jit_solution(3334305938467696507)
XLA Ops:
  7.2 0.0 copy-start
  7.2 0.0 copy-start.1
  7.2 0.0 copy-start.6
  7.2 0.0 all-gather.2.cloned.1.call-start
  7.3 2.3 %fusion.30 = (f32[128,6,1]{2,0,1:T(8,128)}, f32[128,6,1]{2,0,1:T(8,128)}) fusion(f32[128,6,256]{2,0,1:T(8,128)} %param.8), kind=kLoop, calls=%fused_computation.61 | loop fusion | bytes 12288 | tf_op jit(solution)/shard_map/slice | solution.py:15
  9.5 2.4 %collective-permute-start.2 = (f32[128,6,1]{2,0,1:T(8,128)}, f32[128,6,1]{2,0,1:T(8,128)S(1)}, u32[]{:S(2)}, u32[]{:S(2)}) collective-permute-start(f32[128,6,1]{2,0,1:T(8,128)} %get-tuple-element.16), channel_id=1, source_target_pairs={{1,0},{2,1},{3,2},{0,3},{5,4},{6,5},{7,6},{4,7},{9,8},{10,9},{11,1... | collective-permute-start | bytes 9224 | tf_op jit(solution)/shard_map/ppermute | solution.py:17
  11.9 0.8 fusion.29
  12.8 1.3 collective-permute-start
  14.1 4.5 %collective-permute-start.1 = (f32[1,6,256]{2,0,1:T(1,128)S(1)}, f32[1,6,256]{2,0,1:T(1,128)S(1)}, u32[]{:S(2)}, u32[]{:S(2)}) collective-permute-start(f32[1,6,256]{2,0,1:T(1,128)S(1)} %get-tuple-element.15), channel_id=1, source_target_pairs={{0,4},{4,8},{8,12},{12,16},{16,20},{20,24},{24,28},{1,5},{5,9},{9,... | collective-permute-start | bytes 18440 | tf_op jit(solution)/shard_map/ppermute | solution.py:16
  18.6 0.9 subtract_convert_fusion
  19.6 0.9 convolution_multiply_fusion.1
  20.4 0.1 reverse_multiply_fusion.1
  20.6 1.2 collective-permute-done.2
  21.7 0.9 collective-permute-done.3
  22.7 0.0 collective-permute-done
  22.7 1.6 fusion.18
  24.2 0.0 all-gather.2.cloned.1.call-update
  24.3 0.0 reduce-scatter.2.cloned.1.call-start
  24.4 4.1 %fusion.22 = (f32[1024,256]{1,0:T(8,128)S(1)}, f32[1024,256]{1,0:T(8,128)S(1)}) fusion(s32[256]{0:T(256)S(1)} %iota_add_fusion), kind=kLoop, calls=%fused_computation.47 | loop fusion | flops 3670016 | bytes 2098176 | tf_op jit(solution)/shard_map/cos | solution.py:39
  28.5 25.6 %all-gather.2.cloned.1.call-done = f32[128,6,1024]{2,0,1:T(8,128)} async-done(((f32[128,6,256]{2,0,1:T(8,128)}), f32[128,6,1024]{2,0,1:T(8,128)}) %all-gather.2.cloned.1.call-update) | async-done | bytes 3145744 | tf_op jit(solution)/shard_map/all_gather | solution.py:66
  54.1 7.0 %fusion = f32[128,6,512]{2,0,1:T(8,128)S(1)} fusion(f32[128,6,1024]{2,0,1:T(8,128)} %all-gather.2.cloned.1.call-done, f32[1024,256]{1,0:T(8,128)S(1)} %get-tuple-element.19, f32[1024,256]{1,0:T(8,128)S(1)} %get-tuple-element.18), kind=kOutput, calls=%fused_computation.2 | convolution fusion | flops 4832362496 | bytes 6815744 | tf_op jit(solution)/shard_map/dot_general | solution.py:70
  61.1 0.7 multiply_reduce_fusion
  61.8 2.3 %copy.24 = f32[128,6,512]{2,1,0:T(8,128)} copy(f32[128,6,512]{2,0,1:T(8,128)S(1)} %multiply_reduce_fusion) | data formatting | bytes 3145728 | tf_op jit(solution)/shard_map/reduce_sum | solution.py:44
  64.1 2.6 %reshape.48 = f32[768,512]{1,0:T(8,128)} reshape(f32[128,6,512]{2,1,0:T(8,128)} %copy.24) | data formatting | bytes 3145728 | tf_op jit(solution)/shard_map/reshape | solution.py:71
  66.6 8.3 %convolution_multiply_fusion = f32[1024,768]{1,0:T(8,128)} fusion(f32[768,512]{1,0:T(8,128)} %reshape.48, f32[1024,256]{1,0:T(8,128)S(1)} %get-tuple-element.19, f32[1024,256]{1,0:T(8,128)S(1)} %get-tuple-element.18), kind=kOutput, calls=%fused_computation.4 | convolution fusion | flops 4833148928 | bytes 6815744 | tf_op jit(solution)/shard_map/dot_general | solution.py:74
  74.9 0.0 reduce-scatter.2.cloned.1.call-update
  74.9 38.1 %reduce-scatter.2.cloned.1.call-done = f32[256,768]{1,0:T(8,128)} async-done(((f32[1024,768]{1,0:T(8,128)}), f32[256,768]{1,0:T(8,128)}) %reduce-scatter.2.cloned.1.call-update) | async-done | bytes 786448 | tf_op jit(solution)/shard_map/reduce_scatter | solution.py:73
  113.0 1.4 copy.25
  114.5 0.1 reshape.49
  114.6 0.3 copy_multiply_fusion.1
  114.8 0.0 copy-start.3
  114.8 1.0 fusion.28
  115.9 0.0 copy-start.2
  115.9 2.6 %reshape.50 = f32[128,3,2,256]{3,2,1,0:T(2,128)} reshape(f32[768,256]{1,0:T(8,128)} %copy-done.5) | data formatting | bytes 1572864 | tf_op jit(solution)/shard_map/reshape | solution.py:82
  118.5 0.5 collective-permute-start.7
  119.0 1.3 collective-permute-start.4
  120.3 4.5 %collective-permute-start.5 = (f32[1,6,256]{2,0,1:T(1,128)S(1)}, f32[1,6,256]{2,0,1:T(1,128)S(1)}, u32[]{:S(2)}, u32[]{:S(2)}) collective-permute-start(f32[1,6,256]{2,0,1:T(1,128)S(1)} %get-tuple-element.11), channel_id=1, source_target_pairs={{0,4},{4,8},{8,12},{12,16},{16,20},{20,24},{24,28},{1,5},{5,9},{9,... | collective-permute-start | bytes 18440 | tf_op jit(solution)/shard_map/ppermute | solution.py:16
  124.8 1.2 copy_multiply_fusion
  126.1 0.1 reverse_multiply_fusion
  126.1 1.5 collective-permute-done.6
  127.7 2.1 collective-permute-done.7
  129.8 2.2 multiply_reduce_fusion.2
  132.0 39.9 %all-reduce = (f32[]{:T(128)}, f32[]{:T(128)}) all-reduce(f32[]{:T(128)} %get-tuple-element.4, f32[]{:T(128)} %get-tuple-element.3), channel_id=1, replica_groups=mesh['ax'=8,'sec'=4] {'ax','sec'}, use_global_device_ids=true, to_apply=%region_3.4 | all-reduce | flops 2 | bytes 16 | tf_op jit(solution)/shard_map/psum | solution.py:86
  173.3 0.0 copy-start.8
  173.3 1.2 multiply_add_fusion
  174.4 1.6 multiply_reduce_fusion.1
  176.1 40.9 %psum.23 = f32[]{:T(128)} all-reduce(f32[]{:T(128)} %get-tuple-element.7), channel_id=1, replica_groups=mesh['ax'=8,'sec'=4] {'ax','sec'}, use_global_device_ids=true, to_apply=%region_7.8 | all-reduce | flops 1 | bytes 8 | tf_op jit(solution)/shard_map/psum | solution.py:90
  217.6 0.6 pad_maximum_fusion.12
  (24 shorter events, 0.1 us)
Async XLA Ops:
  7.2 17.2 %copy-start = (f32[6,6,1024]{2,1,0:T(8,128)S(1)}, f32[6,6,1024]{2,1,0:T(8,128)}, u32[]{:S(2)}) copy-start(f32[6,6,1024]{2,1,0:T(8,128)} %param.13) | copy-start | bytes 442372
  7.2 13.3 %copy-start.1 = (f32[128,6,256]{2,0,1:T(8,128)S(1)}, f32[128,6,256]{2,0,1:T(8,128)}, u32[]{:S(2)}) copy-start(f32[128,6,256]{2,0,1:T(8,128)} %param.8) | copy-start | bytes 2359300
  7.2 15.5 %copy-start.9 = (f32[128,6,256]{2,0,1:T(8,128)S(1)}, f32[128,6,256]{2,0,1:T(8,128)}, u32[]{:S(2)}) copy-start(f32[128,6,256]{2,0,1:T(8,128)} %param.7) | copy-start | bytes 2359300
  7.2 15.5 %copy-start.6 = (f32[128,6,256]{2,0,1:T(8,128)S(1)}, f32[128,6,256]{2,0,1:T(8,128)}, u32[]{:S(2)}) copy-start(f32[128,6,256]{2,0,1:T(8,128)} %param.9) | copy-start | bytes 2359300
  7.2 46.9 %all-gather.2.cloned.1.call-start = ((), (), s32[]{:S(2)}) async-start(), calls=%async_computation.1 | async-start | bytes 3932160 | tf_op jit(solution)/shard_map/all_gather | solution.py:66
  9.5 12.2 %collective-permute-start.2 = (f32[128,6,1]{2,0,1:T(8,128)}, f32[128,6,1]{2,0,1:T(8,128)S(1)}, u32[]{:S(2)}, u32[]{:S(2)}) collective-permute-start(f32[128,6,1]{2,0,1:T(8,128)} %get-tuple-element.16), channel_id=1, source_target_pairs={{1,0},{2,1},{3,2},{0,3},{5,4},{6,5},{7,6},{4,7},{9,8},{10,9},{11,1... | collective-permute-start | bytes 9224 | tf_op jit(solution)/shard_map/ppermute | solution.py:17
  11.9 10.7 %collective-permute-start.3 = (f32[128,6,1]{2,0,1:T(8,128)}, f32[128,6,1]{2,0,1:T(8,128)S(1)}, u32[]{:S(2)}, u32[]{:S(2)}) collective-permute-start(f32[128,6,1]{2,0,1:T(8,128)} %get-tuple-element.17), channel_id=1, source_target_pairs={{0,1},{1,2},{2,3},{3,0},{4,5},{5,6},{6,7},{7,4},{8,9},{9,10},{10,1... | collective-permute-start | bytes 9224 | tf_op jit(solution)/shard_map/ppermute | solution.py:16
  12.8 9.9 %collective-permute-start = (f32[1,6,256]{2,0,1:T(1,128)S(1)}, f32[1,6,256]{2,0,1:T(1,128)S(1)}, u32[]{:S(2)}, u32[]{:S(2)}) collective-permute-start(f32[1,6,256]{2,0,1:T(1,128)S(1)} %get-tuple-element.14), channel_id=1, source_target_pairs={{4,0},{8,4},{12,8},{16,12},{20,16},{24,20},{28,24},{5,1},{9,5},{13... | collective-permute-start | bytes 18440 | tf_op jit(solution)/shard_map/ppermute | solution.py:17
  14.1 8.6 %collective-permute-start.1 = (f32[1,6,256]{2,0,1:T(1,128)S(1)}, f32[1,6,256]{2,0,1:T(1,128)S(1)}, u32[]{:S(2)}, u32[]{:S(2)}) collective-permute-start(f32[1,6,256]{2,0,1:T(1,128)S(1)} %get-tuple-element.15), channel_id=1, source_target_pairs={{0,4},{4,8},{8,12},{12,16},{16,20},{20,24},{24,28},{1,5},{5,9},{9,... | collective-permute-start | bytes 18440 | tf_op jit(solution)/shard_map/ppermute | solution.py:16
  24.3 88.8 %reduce-scatter.2.cloned.1.call-start = ((), (), s32[]{:S(2)}) async-start(), calls=%async_computation.2 | async-start | bytes 3932160 | tf_op jit(solution)/shard_map/reduce_scatter | solution.py:73
  114.4 1.4 copy-start.5
  114.8 1.1 copy-start.3
  115.9 13.9 %copy-start.2 = (f32[128,6,256]{2,0,1:T(8,128)S(1)}, f32[128,6,256]{2,0,1:T(8,128)}, u32[]{:S(2)}) copy-start(f32[128,6,256]{2,0,1:T(8,128)} %fusion.18) | copy-start | bytes 2359300
  118.5 11.3 %copy-start.4 = (f32[128,6,256]{2,0,1:T(8,128)S(1)}, f32[128,6,256]{2,0,1:T(8,128)}, u32[]{:S(2)}) copy-start(f32[128,6,256]{2,0,1:T(8,128)} %copy-done.3) | copy-start | bytes 2359300
  118.5 11.3 %copy-start.7 = (f32[128,6,256]{2,0,1:T(8,128)S(1)}, f32[128,6,256]{2,0,1:T(8,128)}, u32[]{:S(2)}) copy-start(f32[128,6,256]{2,0,1:T(8,128)} %param.9) | copy-start | bytes 2359300
  118.5 9.2 %collective-permute-start.6 = (f32[128,6,1]{2,0,1:T(8,128)}, f32[128,6,1]{2,0,1:T(8,128)S(1)}, u32[]{:S(2)}, u32[]{:S(2)}) collective-permute-start(f32[128,6,1]{2,0,1:T(8,128)} %get-tuple-element.12), channel_id=1, source_target_pairs={{1,0},{2,1},{3,2},{0,3},{5,4},{6,5},{7,6},{4,7},{9,8},{10,9},{11,1... | collective-permute-start | bytes 9224 | tf_op jit(solution)/shard_map/ppermute | solution.py:17
  118.5 11.3 %collective-permute-start.7 = (f32[128,6,1]{2,0,1:T(8,128)S(1)}, f32[128,6,1]{2,0,1:T(8,128)S(1)}, u32[]{:S(2)}, u32[]{:S(2)}) collective-permute-start(f32[128,6,1]{2,0,1:T(8,128)S(1)} %get-tuple-element.13), channel_id=1, source_target_pairs={{0,1},{1,2},{2,3},{3,0},{4,5},{5,6},{6,7},{7,4},{8,9},{9,10},{10,1... | collective-permute-start | bytes 9224 | tf_op jit(solution)/shard_map/ppermute | solution.py:16
  119.0 10.8 %collective-permute-start.4 = (f32[1,6,256]{2,0,1:T(1,128)S(1)}, f32[1,6,256]{2,0,1:T(1,128)S(1)}, u32[]{:S(2)}, u32[]{:S(2)}) collective-permute-start(f32[1,6,256]{2,0,1:T(1,128)S(1)} %get-tuple-element.10), channel_id=1, source_target_pairs={{4,0},{8,4},{12,8},{16,12},{20,16},{24,20},{28,24},{5,1},{9,5},{13... | collective-permute-start | bytes 18440 | tf_op jit(solution)/shard_map/ppermute | solution.py:17
  120.3 9.5 %collective-permute-start.5 = (f32[1,6,256]{2,0,1:T(1,128)S(1)}, f32[1,6,256]{2,0,1:T(1,128)S(1)}, u32[]{:S(2)}, u32[]{:S(2)}) collective-permute-start(f32[1,6,256]{2,0,1:T(1,128)S(1)} %get-tuple-element.11), channel_id=1, source_target_pairs={{0,4},{4,8},{8,12},{12,16},{16,20},{20,24},{24,28},{1,5},{5,9},{9,... | collective-permute-start | bytes 18440 | tf_op jit(solution)/shard_map/ppermute | solution.py:16
  173.3 1.2 copy-start.8
Sparse Core Ops, SparseCore 0:
  24.4 29.6 all-gather.1
  75.0 37.9 reduce-scatter.1
where the time goes:
time: 226 us; the launch traced here: 225 us
  blocking collectives  80.8 us (36%)
  waiting for transfers between devices  69.5 us (31%)
  between operations  16.3 us (7%)
  matrix products  16.1 us (7%)
  starting transfers between devices  14.7 us (7%)
  other arithmetic  14.5 us (6%)
  local copies, waits for them, and re-layouts  13.1 us (6%)
    psum x1, blocking collectives, shards(): lax.psum(jnp.sum(residual_new * residual_new), ('ax', 'sec')) / cell_total  40.9 us
    psum x1, blocking collectives, shards(): inner_rz = lax.psum(jnp.sum(residual * prec), ('ax', 'sec')) / cell_total  39.9 us
    reduce_scatter x1, waiting for transfers between devices, shards(): lax.psum_scatter(lax.dot_general(table_rows, scaled, (((1,), (1,)), ((),...  38.1 us
    all_gather x1, waiting for transfers between devices, shards(): piece = lax.all_gather(residual, 'sec', axis=2, tiled=True)  25.6 us
    ppermute x4, starting transfers between devices, with_halo(): before = lax.ppermute(last, axis, up)  9.6 us
    dot_general x1, matrix products, shards(): lax.dot_general(table_rows, scaled, (((1,), (1,)), ((), ())), precision=l...  8.26 us
    dot_general x1, matrix products, shards(): jnp.dot(flat, table_rows, precision=lax.Precision.HIGHEST)  6.96 us
    ppermute x4, starting transfers between devices, with_halo(): after = lax.ppermute(first, axis, down)  4.98 us
  transfers between devices with their start and end apart: 10, of which 6 were waited for; matrix products, arithmetic and copies ran while one was open for 4% of the time, Pallas kernels for 0%

commit v1 on v0

v1 whole, which is shorter than its diff:
```python
import functools

import jax
import jax.numpy as jnp
import ml_dtypes
import numpy as np
from jax import lax
from jax.experimental import pallas as pl
from jax.experimental.pallas import tpu as pltpu
from jax.sharding import PartitionSpec as P

F32 = jnp.float32
BF16 = jnp.bfloat16
SECTORS = 4
TILE = 8
LANES = 128


def two_parts(table):
    high = table.astype(ml_dtypes.bfloat16)
    low = (table - high.astype(np.float64)).astype(ml_dtypes.bfloat16)
    return high, low


def three_terms(table):
    high, low = two_parts(table)
    return np.concatenate([high, high, low], axis=0)


@functools.lru_cache(maxsize=None)
def harmonic_tables(width):
    around = SECTORS * width
    half = width // 2
    zero = [("c", 4 * q) for q in range(half + 1)] + [("s", 4 * q) for q in range(1, half)]
    two = [(f, 4 * q + 2) for f in "cs" for q in range(half)]
    one = [(f, 4 * q + 1) for f in "cs" for q in range(width)]
    columns = zero + two + one
    harmonic = np.array([k for _, k in columns], dtype=np.int64)
    is_sin = np.array([f == "s" for f, _ in columns])

    def wave(place, k, shift):
        return np.cos(2.0 * np.pi / around * ((place[:, None] * k[None, :]) % around) - shift)

    place = np.arange(width)
    shift = np.where(is_sin, np.pi / 2, 0.0)[None, :]
    direct = wave(place, harmonic, shift)
    ones = slice(2 * width, 4 * width)
    quarter = wave(place, harmonic[ones], shift[:, ones] - np.pi / 2)
    forward_zero = three_terms(direct[:, :width])
    forward_two = three_terms(direct[:, width : 2 * width])
    forward_one = three_terms(np.concatenate([direct[:, ones], quarter], axis=0))
    targets = np.concatenate([place, np.full(LANES, width)])
    targets[-1] = around - 1
    inverse = wave(targets, harmonic, shift).T
    inverse[:, width + 1 : -1] = 0.0
    fold = np.zeros((around, around))
    fold[harmonic, np.arange(around)] += 1.0 / around
    mirror = (around - harmonic) % around
    apart = mirror != harmonic
    fold[mirror[apart], np.arange(around)[apart]] += 1.0 / around
    return (
        forward_zero,
        forward_two,
        forward_one,
        three_terms(inverse),
        fold.astype(ml_dtypes.bfloat16),
    )


def split(x):
    high = x.astype(BF16)
    return high, (x - high.astype(F32)).astype(BF16)


def lanes_of(shape):
    return lax.broadcasted_iota(jnp.int32, shape, len(shape) - 1)


def rows_of(shape):
    return lax.broadcasted_iota(jnp.int32, shape, len(shape) - 2)


def shifted(x, before, after):
    lane = lanes_of(x.shape)
    size = x.shape[-1]
    left = jnp.where(lane == 0, before, pltpu.roll(x, 1, x.ndim - 1))
    right = jnp.where(lane == size - 1, after, pltpu.roll(x, size - 1, x.ndim - 1))
    return left, right


def stacked(x, before, after):
    row = rows_of(x.shape)
    size = x.shape[-2]
    up = jnp.where(row == 0, before, pltpu.roll(x, 1, x.ndim - 2))
    down = jnp.where(row == size - 1, after, pltpu.roll(x, size - 1, x.ndim - 2))
    return up, down


def fold_kernel(precond_ref, fold_ref, out_ref):
    value = precond_ref[...]
    high = value.astype(BF16)
    rest = value - high.astype(F32)
    middle = rest.astype(BF16)
    low = (rest - middle.astype(F32)).astype(BF16)
    terms = [jnp.dot(t, fold_ref[...], preferred_element_type=F32) for t in (high, middle, low)]
    out_ref[...] = terms[0] + (terms[1] + terms[2])


def local_kernel(
    cuts, comps, position_ref, table_ref, class_ref, load_ref, disp_ref, stiff_ref, hole_ref,
    first_ref, second_ref, ends_ref, factor_ref, up_ref, down_ref,
):
    slab, width = hole_ref.shape
    a, b, c = cuts
    classes = class_ref[...]
    position = position_ref[0] + lanes_of(classes.shape)
    taper = 1.0 + 2.0 * position.astype(F32) / (position_ref[1] - 1).astype(F32)
    rows = []
    for q in range(comps):
        value = jnp.zeros(classes.shape, F32)
        for kind in range(table_ref.shape[0]):
            value = jnp.where(classes == kind, table_ref[kind, q], value)
        rows.append(value * taper)
    rows.append(jnp.zeros((LANES - comps, slab), F32))
    factor_ref[...] = jnp.concatenate(rows, axis=0).T
    solid = (1 - hole_ref[...]).astype(F32)
    edge_left, edge_right = [], []
    for q in range(comps):
        field = disp_ref[q]
        left, right = shifted(field, 0.0, 0.0)
        up, down = stacked(field, 0.0, 0.0)
        stiffness = stiff_ref[q] * factor_ref[:, q : q + 1]
        image = (stiffness + 4.5) * field - (up + down + left + right) - 0.5 * disp_ref[q ^ 1]
        part = solid * (load_ref[q] - image)
        first_ref[pl.ds(q * (b - a), b - a), :] = part[a:b]
        second_ref[pl.ds(q * (c - b), c - b), :] = part[b:c]
        ends_ref[pl.ds(q * (a + slab - c), a), :] = part[:a]
        ends_ref[pl.ds(q * (a + slab - c) + a, slab - c), :] = part[c:]
        for ref, row in ((up_ref, slab - 1), (down_ref, 0)):
            ref[q : q + 1, :] = part[row : row + 1]
            ref[TILE + q : TILE + q + 1, :] = field[row : row + 1]
        edge_left.append(field[:, 0:1])
        edge_right.append(field[:, width - 1 : width])
    for ref, row in ((up_ref, slab - 1), (down_ref, 0)):
        ref[comps : TILE, :] = jnp.broadcast_to(solid[row : row + 1], (TILE - comps, width))
        ref[TILE + comps :, :] = jnp.zeros((TILE - comps, width), F32)
    edge_left += [solid[:, 0:1]] * (TILE - comps)
    edge_right += [solid[:, width - 1 : width]] * (TILE - comps)
    edges = jnp.concatenate(edge_left + edge_right + [jnp.zeros((slab, LANES - 2 * TILE), F32)], axis=1).T
    first_ref[pl.ds(comps * (b - a), TILE), :] = jnp.concatenate(
        [edges[:TILE], edges[TILE : 2 * TILE]], axis=1
    )


def ends_kernel(comps, ends_ref, up_ref, down_ref, before_ref, after_ref, out_ref):
    rows = ends_ref.shape[0] // comps
    width = ends_ref.shape[1]
    row = rows_of((rows, width))
    spare = rows_of((TILE, width))
    solid_before = before_ref[comps : comps + 1]
    solid_after = after_ref[comps : comps + 1]
    for q in range(comps):
        disp_before = before_ref[TILE + q : TILE + q + 1]
        disp_after = after_ref[TILE + q : TILE + q + 1]
        part = ends_ref[pl.ds(q * rows, rows), :]
        part = part + jnp.where(row == 0, down_ref[comps : comps + 1] * disp_before, 0.0)
        part = part + jnp.where(row == rows - 1, up_ref[comps : comps + 1] * disp_after, 0.0)
        out_ref[pl.ds(q * (rows + TILE), rows), :] = part
        res_before = before_ref[q : q + 1] + solid_before * down_ref[TILE + q : TILE + q + 1]
        res_after = after_ref[q : q + 1] + solid_after * up_ref[TILE + q : TILE + q + 1]
        beyond = jnp.zeros((TILE, width), F32)
        for i, value in enumerate((res_before, res_after, disp_before, disp_after, solid_before, solid_after)):
            beyond = jnp.where(spare == i, value, beyond)
        out_ref[pl.ds(q * (rows + TILE) + rows, TILE), :] = beyond


def in_order(odd, own, core, across, both):
    return own, jnp.where(odd, both, core), across, jnp.where(odd, core, both)


def butterfly(x0, x1, x2, x3):
    even, other = x0 + x2, x1 + x3
    return even + other, even - other, x0 - x2, x1 - x3


def edge_table(odd, blocks):
    tiles = in_order(odd, *blocks)
    left = [t[:, :LANES] for t in tiles]
    right = [t[:, LANES:] for t in tiles]
    solid = TILE - 1
    at_left = [left[s][solid:] * right[s - 1] for s in range(SECTORS)]
    at_right = [right[s][solid:] * left[(s + 1) % SECTORS] for s in range(SECTORS)]
    stack = []
    for one, other in zip(butterfly(*at_left), butterfly(*at_right)):
        stack += [one, other]
    stack += [at_left[0], at_right[0], right[3], left[1]]
    stack.append(jnp.zeros((LANES - len(stack) * TILE, LANES), F32))
    return jnp.concatenate(stack, axis=0).T


def transform_kernel(
    comps, rows_at, spare, make_edge, odd_ref, own_ref, core_ref, across_ref, both_ref, *refs,
):
    refs = list(refs)
    edge_in = None if make_edge else refs.pop(0)
    zero_ref, two_ref, one_ref, inverse_ref, weight_ref, hole_ref = refs[:6]
    refs = refs[6:]
    edge_ref = refs.pop(0) if make_edge else edge_in
    prec_ref, residual_ref, left_ref, spectrum_ref, scaled_ref = refs
    width = own_ref.shape[1]
    odd = odd_ref[0] == 1
    sign = jnp.where(odd, -1.0, 1.0)
    main = sum(size for _, size in rows_at)
    rows = main + spare
    total = comps * rows
    sources = (own_ref, core_ref, across_ref, both_ref)
    if make_edge:
        edge_ref[...] = edge_table(odd, [r[total : total + TILE] for r in sources])
    solid = jnp.concatenate([(1 - hole_ref[pl.ds(at, size)]).astype(F32) for at, size in rows_at], axis=0)
    edge = jnp.concatenate([edge_ref[pl.ds(at, size)] for at, size in rows_at], axis=0)
    lane = lanes_of((main, LANES))
    first = lane == 0
    last = lane == LANES - 1

    def with_edges(x, array, q):
        column = array * 2 * TILE + q
        head = x[:, :LANES] + jnp.where(first, edge[:, column : column + 1], 0.0)
        tail = x[:, -LANES:] + jnp.where(last, edge[:, column + TILE : column + TILE + 1], 0.0)
        middle = [x[:, LANES:-LANES]] if width > 2 * LANES else []
        return jnp.concatenate([head] + middle + [tail], axis=1)

    masks = []
    for q in range(comps):
        at = q * rows
        own, core, across, both = [r[pl.ds(at, main), :] for r in sources]
        arrays = butterfly(own, core, across, both)
        arrays = arrays[:3] + (sign * arrays[3],)
        arrays = [with_edges(x, i, q) for i, x in enumerate(arrays)]
        residual_ref[q] = with_edges(own, 4, q)
        if spare:
            tiles = in_order(odd, *[r[pl.ds(at + main, spare), :] for r in sources])
            disp = [pltpu.roll(t, spare - 2, 0) for t in tiles]
            holes = [pltpu.roll(t, spare - 4, 0) for t in tiles]
            place = lanes_of((spare, width))
            fixed = []
            for s in range(SECTORS):
                beside = jnp.where(place == 0, pltpu.roll(disp[s - 1], 1, 1), 0.0)
                beside = beside + jnp.where(
                    place == width - 1, pltpu.roll(disp[(s + 1) % SECTORS], width - 1, 1), 0.0
                )
                value = tiles[s] + holes[s] * beside
                fixed.append(jnp.where(rows_of((spare, width)) < 2, value, 0.0))
            masks.append(holes[0])
            more = butterfly(*fixed)
            arrays = [jnp.concatenate(pair, axis=0) for pair in zip(arrays, more)]
        for i, x in enumerate(arrays):
            high, low = split(x)
            left_ref[pl.ds(at, rows), 2 * i * width : (2 * i + 1) * width] = high
            left_ref[pl.ds(at, rows), (2 * i + 1) * width : (2 * i + 2) * width] = low

    def column(i):
        return left_ref[:, i * width : (i + 1) * width]

    def product(parts, table):
        return jnp.dot(jnp.concatenate(parts, axis=1), table[...], preferred_element_type=F32)

    spectrum_ref[:, :width] = product([column(0), column(1), column(0)], zero_ref)
    spectrum_ref[:, width : 2 * width] = product([column(2), column(3), column(2)], two_ref)
    spectrum_ref[:, 2 * width :] = product(
        [column(4), column(6), column(5), column(7), column(4), column(6)], one_ref
    )

    around = SECTORS * width

    def scale(step, carry):
        at = pl.multiple_of(step * LANES, LANES)
        parts = [spectrum_ref[pl.ds(p * rows, rows), pl.ds(at, LANES)] for p in range(comps)]
        for q in range(comps):
            value = parts[0] * weight_ref[q * comps : q * comps + 1, pl.ds(at, LANES)]
            for p in range(1, comps):
                value = value + parts[p] * weight_ref[q * comps + p : q * comps + p + 1, pl.ds(at, LANES)]
            high, low = split(value)
            scaled_ref[pl.ds(q * rows, rows), pl.ds(at, LANES)] = high
            scaled_ref[pl.ds(q * rows, rows), pl.ds(pl.multiple_of(around + at, LANES), LANES)] = low
        return carry

    lax.fori_loop(0, around // LANES, scale, 0)
    high = scaled_ref[:, :around]
    result = product([high, scaled_ref[:, around:], high], inverse_ref)
    for q in range(comps):
        at = q * rows
        part = result[at : at + main]
        prec_ref[q, :main] = jnp.concatenate([part[:, :width] * solid, part[:, width:]], axis=1)
        if spare:
            more = result[at + main : at + rows, :width] * masks[q]
            prec_ref[q, main:] = jnp.concatenate([more, jnp.zeros((spare, LANES), F32)], axis=1)


def whole(refs, q, cuts, slab, columns):
    a, b, c = cuts
    first, second, ends = refs
    return jnp.concatenate(
        [ends[q, :a, columns], first[q, :, columns], second[q, :, columns], ends[q, a : a + slab - c, columns]],
        axis=0,
    )


def image_kernel(
    cuts, comps, stiff_ref, hole_ref, factor_ref, edge_ref,
    p0_ref, p1_ref, p2_ref, r0_ref, r1_ref, r2_ref, image_ref, sums_ref,
):
    slab, width = hole_ref.shape
    a, _, c = cuts
    spare = a + slab - c
    precs = (p0_ref, p1_ref, p2_ref)
    solid = (1 - hole_ref[...]).astype(F32)
    own = slice(0, width)
    solid_before = edge_ref[:, 11 * TILE - 1 : 11 * TILE]
    solid_after = edge_ref[:, 12 * TILE - 1 : 12 * TILE]
    fields = [whole(precs, q, cuts, slab, own) for q in range(comps)]
    sums = [jnp.zeros((TILE, width), F32) for _ in range(5)]
    for q in range(comps):
        field = fields[q]
        tile = whole(precs, q, cuts, slab, slice(width, width + LANES))
        left, right = shifted(field, tile[:, LANES - 1 :] * solid_before, tile[:, :1] * solid_after)
        up, down = stacked(field, p2_ref[q, spare : spare + 1, own], p2_ref[q, spare + 1 : spare + 2, own])
        stiffness = stiff_ref[q] * factor_ref[:, q : q + 1]
        image = (stiffness + 4.5) * field - (up + down + left + right) - 0.5 * fields[q ^ 1]
        image = solid * image
        image_ref[q] = image
        residual = whole((r0_ref, r1_ref, r2_ref), q, cuts, slab, own)
        pairs = ((residual, field), (field, image), (residual, residual), (residual, image), (image, image))
        for i, (x, y) in enumerate(pairs):
            sums[i] = sums[i] + jnp.sum((x * y).reshape(slab // TILE, TILE, width), axis=0)
    lane = lanes_of(sums_ref.shape)
    row = jnp.zeros(sums_ref.shape, F32)
    for i, value in enumerate(sums):
        row = jnp.where(lane == i, jnp.sum(value), row)
    sums_ref[...] = row


def update_kernel(
    cuts, comps, cell_total, disp_ref, image_ref, gathered_ref,
    p0_ref, p1_ref, p2_ref, r0_ref, r1_ref, r2_ref, disp_out, residual_out, stats_out,
):
    slab, width = disp_ref.shape[1:]
    lane = lanes_of(gathered_ref.shape)
    values = gathered_ref[...] * (1.0 / cell_total)
    rz, zq, rr, ri, ii = [jnp.sum(jnp.where(lane == i, values, 0.0)) for i in range(5)]
    spot = lanes_of((1, LANES))
    top = jnp.where(spot >= 0, rz, 0.0)
    alpha_row = top / jnp.where(spot >= 0, zq, 0.0)
    square = rr + alpha_row * (alpha_row * ii - 2.0 * ri)
    stats_out[...] = jnp.where(spot == 0, rz, jnp.where(spot == 1, zq, square))
    alpha = alpha_row[:, :1]
    own = slice(0, width)
    for q in range(comps):
        disp_out[q] = disp_ref[q] + alpha * whole((p0_ref, p1_ref, p2_ref), q, cuts, slab, own)
        residual_out[q] = whole((r0_ref, r1_ref, r2_ref), q, cuts, slab, own) - alpha * image_ref[q]


VMEM = pl.BlockSpec(memory_space=pltpu.VMEM)
SMEM = pl.BlockSpec(memory_space=pltpu.SMEM)


def call(kernel, name, out_shapes, in_specs, flops, moved, scratch=()):
    return pl.pallas_call(
        kernel,
        out_shape=[jax.ShapeDtypeStruct(s, F32) for s in out_shapes],
        in_specs=in_specs,
        out_specs=[VMEM] * len(out_shapes),
        scratch_shapes=list(scratch),
        compiler_params=pltpu.CompilerParams(vmem_limit_bytes=32 * 1024 * 1024),
        cost_estimate=pl.CostEstimate(flops=flops, bytes_accessed=moved, transcendentals=0),
        name=name,
    )


def shards(load, disp, stiff, hole, section_class, class_table, precond):
    slab, comps, width = disp.shape
    ax, sec = lax.axis_size("ax"), lax.axis_size("sec")
    around = width * sec
    cell_total = slab * ax * comps * around
    cuts = (slab // 8, slab // 2, slab - slab // 8)
    a, b, c = cuts
    ends = a + slab - c
    load, disp, stiff = [x.transpose(1, 0, 2) for x in (load, disp, stiff)]
    zero, two, one, inverse, fold = harmonic_tables(width)
    block = 4 * comps * slab * width
    odd = (lax.axis_index("sec") % 2).astype(jnp.int32).reshape(1)
    position = jnp.stack([lax.axis_index("ax") * slab, jnp.int32(ax * slab)]).astype(jnp.int32)

    first, second, edge_rows, factor, up, down = call(
        functools.partial(local_kernel, cuts, comps), "local",
        [(comps * (b - a) + TILE, width), (comps * (c - b), width), (comps * ends, width),
         (slab, LANES), (2 * TILE, width), (2 * TILE, width)],
        [SMEM, SMEM] + [VMEM] * 5, 20 * comps * slab * width, 4 * block,
    )(position, class_table, section_class.reshape(1, slab), load, disp, stiff, hole)

    def across(x):
        return lax.ppermute(x, "sec", [(i, (i + sec // 2) % sec) for i in range(sec)])

    def beside(x):
        return lax.ppermute(x, "sec", [(i, i ^ 1) for i in range(sec)])

    def gather(x):
        far = across(x)
        return x, beside(x), far, beside(far)

    first = gather(first)
    before = lax.ppermute(up, "ax", [(i, i + 1) for i in range(ax - 1)])
    after = lax.ppermute(down, "ax", [(i + 1, i) for i in range(ax - 1)])
    second = gather(second)
    (last,) = call(
        functools.partial(ends_kernel, comps), "ends",
        [(comps * (ends + TILE), width)], [VMEM] * 5, comps * ends * width, 8 * comps * ends * width,
    )(edge_rows, up, down, before, after)
    last = gather(last)
    (weight,) = call(
        fold_kernel, "fold", [(comps * comps, around)], [VMEM] * 2,
        6 * comps * comps * around * around, 2 * around * around,
    )(precond.reshape(comps * comps, around), fold)

    def transform(blocks, rows_at, spare, edge):
        main = sum(size for _, size in rows_at)
        rows = main + spare
        total = comps * rows
        out_shapes = [(comps, rows, width + LANES), (comps, main, width)]
        if edge is None:
            out_shapes = [(slab, LANES)] + out_shapes
        operands = list(blocks) + ([] if edge is None else [edge]) + [zero, two, one, inverse, weight, hole]
        return call(
            functools.partial(transform_kernel, comps, rows_at, spare, edge is None), "transform",
            out_shapes, [SMEM] + [VMEM] * len(operands),
            2 * total * 3 * around * (width + 2 * width), 4 * total * width * 8,
            [pltpu.VMEM((total, 8 * width), BF16), pltpu.VMEM((total, around), F32),
             pltpu.VMEM((total, 2 * around), BF16)],
        )(odd, *operands)

    edge, prec0, res0 = transform(first, ((a, b - a),), 0, None)
    prec1, res1 = transform(second, ((b, c - b),), 0, edge)
    prec2, res2 = transform(last, ((0, a), (c, slab - c)), TILE, edge)

    image, sums = call(
        functools.partial(image_kernel, cuts, comps), "image",
        [(comps, slab, width), (ax * sec, LANES)], [VMEM] * 10, 30 * comps * slab * width, 5 * block,
    )(stiff, hole, factor, edge, prec0, prec1, prec2, res0, res1, res2)
    gathered = lax.all_to_all(sums, ("ax", "sec"), 0, 0, tiled=True)
    disp_new, residual_new, stats = call(
        functools.partial(update_kernel, cuts, comps, cell_total), "update",
        [(comps, slab, width), (comps, slab, width), (1, LANES)], [VMEM] * 9,
        4 * comps * slab * width, 6 * block,
    )(disp, image, gathered, prec0, prec1, prec2, res0, res1, res2)
    return disp_new.transpose(1, 0, 2), residual_new.transpose(1, 0, 2), stats[0, :3]


def solution(mesh):
    in_specs = (
        P("ax", None, "sec"),
        P("ax", None, "sec"),
        P("ax", None, "sec"),
        P("ax", "sec"),
        P("ax"),
        P(),
        P(),
    )
    out_specs = (P("ax", None, "sec"), P("ax", None, "sec"), P())
    return jax.shard_map(shards, mesh=mesh, in_specs=in_specs, out_specs=out_specs, check_vma=False)
```

time: 226 us -> 67.8 us (0.30)
  blocking collectives: 80.8 us -> 12.4 us
  waiting for transfers between devices: 69.5 us -> 12.6 us
  Pallas kernels: 0 us -> 18.7 us
  matrix products: 16.1 us -> 0 us
  between operations: 16.3 us -> 0.85 us
  other arithmetic: 14.5 us -> 0.08 us
  starting transfers between devices: 14.7 us -> 11 us
    psum x2 -> x0, blocking collectives: 80.8 us -> none  [the longest x1 40.9 us: shards(): lax.psum(jnp.sum(residual_new * residual_new), ('ax', 'sec')) / cell_total]
    reduce_scatter x1 -> x0, waiting for transfers between devices: 38.1 us -> none  [shards(): lax.psum_scatter(lax.dot_general(table_rows, scaled, (((1,), (1,)), ((),...]
    all_gather x1 -> x0, waiting for transfers between devices: 25.6 us -> none  [shards(): piece = lax.all_gather(residual, 'sec', axis=2, tiled=True)]
    pallas_call x0 -> x8, Pallas kernels: none -> 18.7 us  [the longest x3 12.2 us: transform(): call(functools.partial(transform_kernel, comps, rows_at, spare, edge is N...]
    dot_general x3 -> x0, matrix products: 16.1 us -> none  [the longest x1 8.26 us: shards(): lax.dot_general(table_rows, scaled, (((1,), (1,)), ((), ())), precision=l...]
    all_to_all x0 -> x1, blocking collectives: none -> 12.4 us  [shards(): gathered = lax.all_to_all(sums, ('ax', 'sec'), 0, 0, tiled=True)]
    unnamed x20 -> x34, local copies, waits for them, and re-layouts: 0.06 us -> 9.59 us
    ppermute x8 -> x11, waiting for transfers between devices: 5.73 us -> 12.6 us  [the longest x3 8.26 us: across(): lax.ppermute(x, 'sec', [(i, (i + sec // 2) % sec) for i in range(sec)])]
  transfers between devices with their start and end apart: 10 -> 11, of which waited for: 6 -> 3; matrix products, arithmetic and copies ran while one was open for 4% -> 2% of each run, Pallas kernels for 0% -> 14%
where the time goes in v1:
time: 67.8 us; the launch traced here: 67.3 us
  Pallas kernels  18.7 us (28%)
  waiting for transfers between devices  12.6 us (19%)
  blocking collectives  12.4 us (18%)
  local copies, waits for them, and re-layouts  11.7 us (17%)
  starting transfers between devices  11 us (16%)
  between operations  0.85 us (1%)
    all_to_all x1, blocking collectives, shards(): gathered = lax.all_to_all(sums, ('ax', 'sec'), 0, 0, tiled=True)  12.4 us
    pallas_call x3, Pallas kernels, transform(): call(functools.partial(transform_kernel, comps, rows_at, spare, edge is N...  12.2 us
    unnamed x34, local copies, waits for them, and re-layouts  9.59 us
    ppermute x3, waiting for transfers between devices, across(): lax.ppermute(x, 'sec', [(i, (i + sec // 2) % sec) for i in range(sec)])  8.26 us
    ppermute x3, starting transfers between devices, across(): lax.ppermute(x, 'sec', [(i, (i + sec // 2) % sec) for i in range(sec)])  4.7 us
    ppermute x1, waiting for transfers between devices, shards(): after = lax.ppermute(down, 'ax', [(i + 1, i) for i in range(ax - 1)])  4.21 us
    ppermute x1, starting transfers between devices, shards(): before = lax.ppermute(up, 'ax', [(i, i + 1) for i in range(ax - 1)])  3.92 us
    pallas_call x1, Pallas kernels, shards(): call(functools.partial(local_kernel, cuts, comps), 'local', [(comps * (b...  2.39 us
  transfers between devices with their start and end apart: 11, of which 3 were waited for; matrix products, arithmetic and copies ran while one was open for 2% of the time, Pallas kernels for 14%

profile of v1, /device:TPU:0, one launch (start us, length us, event | category | flops | bytes accessed | tf_op | source)
XLA Modules:
  0.0 67.3 jit_solution(6871712992935092626)
XLA Ops:
  0.6 0.1 pad_add_fusion.position_ref
  0.7 0.9 %copy-done.4 = s32[128,256]{1,0:T(8,128)S(1)} copy-done((s32[128,256]{1,0:T(8,128)S(1)}, s32[128,256]{1,0:T(8,128)}, u32[]{:S(2)}) %copy-start.4) | copy-done | bytes 131096
  1.6 1.1 %copy-done.6 = f32[128,6,256]{2,0,1:T(8,128)S(1)} copy-done((f32[128,6,256]{2,0,1:T(8,128)S(1)}, f32[128,6,256]{2,0,1:T(8,128)}, u32[]{:S(2)}) %copy-start.6) | copy-done | bytes 786456
  2.8 1.1 %copy-done.8 = f32[128,6,256]{2,0,1:T(8,128)S(1)} copy-done((f32[128,6,256]{2,0,1:T(8,128)S(1)}, f32[128,6,256]{2,0,1:T(8,128)}, u32[]{:S(2)}) %copy-start.8) | copy-done | bytes 786456
  3.9 1.1 %copy-done.11 = f32[128,6,256]{2,0,1:T(8,128)S(1)} copy-done((f32[128,6,256]{2,0,1:T(8,128)S(1)}, f32[128,6,256]{2,0,1:T(8,128)}, u32[]{:S(2)}) %copy-start.11) | copy-done | bytes 786456
  5.0 0.7 %copy-done.15 = f32[4,6]{1,0:T(4,128)S(1)} copy-done((f32[4,6]{1,0:T(4,128)S(1)}, f32[4,6]{1,0:T(4,128)}, u32[]{:S(2)}) %copy-start.15) | copy-done | bytes 120
  5.7 0.7 copy-done.16
  6.4 2.4 %local.1 = (f32[296,256]{1,0:T(8,128)}, f32[288,256]{1,0:T(8,128)}, f32[192,256]{1,0:T(8,128)S(1)}, f32[128,128]{1,0:T(8,128)S(1)}, f32[16,256]{1,0:T(8,128)S(1)}, /*index=5*/f32[16,256]{1,0:T(8,128)S(1)}) custom-call(s32[2]{0:T(128)S(1)} %pad_add_fusion.position_ref, f32[4,6]{1,0:T(4,128)S(1)} %copy-done.15, s32[1,128]{1,0:T(1,128)S(1)} %bitcast.21, ...), custom_call_target="tpu_custom_call" | custom-call | flops 3932160 | bytes 3145728 | tf_op jit(solution)/shard_map/local/pallas_call | solution.py:393
  8.8 0.0 copy-start.3
  8.8 0.0 copy-start.5
  8.8 3.0 %collective-permute-start.1 = (f32[296,256]{1,0:T(8,128)}, f32[296,256]{1,0:T(8,128)}, u32[]{:S(2)}, u32[]{:S(2)}) collective-permute-start(f32[296,256]{1,0:T(8,128)} %get-tuple-element.22.own_ref), channel_id=1, source_target_pairs={{0,2},{1,3},{2,0},{3,1},{4,6},{5,7},{6,4},{7,5},{8,10},{9,11},{10,... | collective-permute-start | bytes 909320 | tf_op jit(solution)/shard_map/ppermute | solution.py:401
  11.8 0.1 collective-permute-start.4
  11.9 0.0 collective-permute-start
  11.9 8.2 %collective-permute-done.1.across_ref = f32[296,256]{1,0:T(8,128)} collective-permute-done((f32[296,256]{1,0:T(8,128)}, f32[296,256]{1,0:T(8,128)}, u32[]{:S(2)}, u32[]{:S(2)}) %collective-permute-start.1) | collective-permute-done | bytes 303136 | tf_op jit(solution)/shard_map/ppermute | solution.py:401
  20.1 0.0 collective-permute-start.2
  20.1 3.9 %collective-permute-start.6 = (f32[16,256]{1,0:T(8,128)S(1)}, f32[16,256]{1,0:T(8,128)S(1)}, u32[]{:S(2)}, u32[]{:S(2)}) collective-permute-start(f32[16,256]{1,0:T(8,128)S(1)} %get-tuple-element.28.up_ref), channel_id=1, source_target_pairs={{0,4},{4,8},{8,12},{12,16},{16,20},{20,24},{24,28},{1,5},{5,9},{9,... | collective-permute-start | bytes 49160 | tf_op jit(solution)/shard_map/ppermute | solution.py:411
  24.1 1.3 %collective-permute-start.7 = (f32[16,256]{1,0:T(8,128)S(1)}, f32[16,256]{1,0:T(8,128)S(1)}, u32[]{:S(2)}, u32[]{:S(2)}) collective-permute-start(f32[16,256]{1,0:T(8,128)S(1)} %get-tuple-element.29.down_ref), channel_id=1, source_target_pairs={{4,0},{8,4},{12,8},{16,12},{20,16},{24,20},{28,24},{5,1},{9,5},{13... | collective-permute-start | bytes 49160 | tf_op jit(solution)/shard_map/ppermute | solution.py:412
  25.4 0.1 collective-permute-done.6.before_ref
  25.5 4.2 %collective-permute-done.7.after_ref = f32[16,256]{1,0:T(8,128)S(1)} collective-permute-done((f32[16,256]{1,0:T(8,128)S(1)}, f32[16,256]{1,0:T(8,128)S(1)}, u32[]{:S(2)}, u32[]{:S(2)}) %collective-permute-start.7) | collective-permute-done | bytes 16416 | tf_op jit(solution)/shard_map/ppermute | solution.py:412
  29.8 0.0 copy-done.13
  29.8 1.6 %collective-permute-start.9 = (f32[240,256]{1,0:T(8,128)S(1)}, f32[240,256]{1,0:T(8,128)}, u32[]{:S(2)}, u32[]{:S(2)}) collective-permute-start(f32[240,256]{1,0:T(8,128)S(1)} %ends.1.own_ref), channel_id=1, source_target_pairs={{0,2},{1,3},{2,0},{3,1},{4,6},{5,7},{6,4},{7,5},{8,10},{9,11},{10,... | collective-permute-start | bytes 737288 | tf_op jit(solution)/shard_map/ppermute | solution.py:401
  31.4 0.0 collective-permute-start.3
  31.4 0.0 collective-permute-done.4.across_ref
  31.4 0.5 collective-permute-start.5
  31.9 1.6 %reshape.19.precond_ref = f32[36,1024]{1,0:T(8,128)} reshape(f32[6,6,1024]{2,1,0:T(8,128)} %param.18) | data formatting | bytes 294912 | tf_op jit(solution)/shard_map/reshape | solution.py:422
  33.5 1.6 %copy-done.10 = bf16[1024,1024]{1,0:T(8,128)(2,1)S(1)} copy-done((bf16[1024,1024]{1,0:T(8,128)(2,1)S(1)}, bf16[1024,1024]{1,0:T(8,128)(2,1)}, u32[]{:S(2)}) %copy-start.10) | copy-done | bytes 2097176
  35.1 0.9 %copy-done.12 = f32[36,1024]{1,0:T(8,128)S(1)} copy-done((f32[36,1024]{1,0:T(8,128)S(1)}, f32[36,1024]{1,0:T(8,128)}, u32[]{:S(2)}) %copy-start.12) | copy-done | bytes 147480
  36.0 1.2 %fold.1.refs_4_.refs_5_ = f32[36,1024]{1,0:T(8,128)S(1)} custom-call(f32[36,1024]{1,0:T(8,128)S(1)} %copy-done.12, bf16[1024,1024]{1,0:T(8,128)(2,1)S(1)} %copy-done.10), custom_call_target="tpu_custom_call" | custom-call | flops 226492416 | bytes 2097152 | tf_op jit(solution)/shard_map/fold/pallas_call | solution.py:419
  37.2 0.0 collective-permute-done.9.across_ref
  37.2 0.1 collective-permute-start.8
  37.3 0.0 collective-permute-done.core_ref
  37.3 0.5 collective-permute-start.10
  37.8 0.0 collective-permute-done.2.both_ref
  37.8 0.0 copy-start.1
  37.8 1.4 %copy-done.1 = bf16[1536,512]{1,0:T(8,128)(2,1)S(1)} copy-done((bf16[1536,512]{1,0:T(8,128)(2,1)S(1)}, bf16[1536,512]{1,0:T(8,128)(2,1)}, u32[]{:S(2)}) %copy-start.1) | copy-done | bytes 1572888
  39.2 4.3 %transform.3 = (f32[128,128]{1,0:T(8,128)S(1)}, f32[6,48,384]{2,1,0:T(8,128)S(1)}, f32[6,48,256]{2,1,0:T(8,128)S(1)}) custom-call(s32[1]{0:T(128)} %bitcast.5.odd_ref, f32[296,256]{1,0:T(8,128)} %get-tuple-element.22.own_ref, f32[296,256]{1,0:T(8,128)} %collective-permute-done.core_ref, f32[296,256]{1,0:T(8,128)} %collective-permute-done.1.across_ref, ...), custom_call_target="tpu_custom_call" | custom-call | flops 1358954496 | bytes 2359296 | tf_op jit(solution)/shard_map/transform/pallas_call | solution.py:432
  43.5 0.0 collective-permute-done.3.core_ref
  43.5 0.0 collective-permute-done.5.both_ref
  43.5 4.2 %transform.4 = (f32[6,48,384]{2,1,0:T(8,128)S(1)}, f32[6,48,256]{2,1,0:T(8,128)S(1)}) custom-call(s32[1]{0:T(128)} %bitcast.5.odd_ref, f32[288,256]{1,0:T(8,128)} %get-tuple-element.25.own_ref, f32[288,256]{1,0:T(8,128)} %collective-permute-done.3.core_ref, f32[288,256]{1,0:T(8,128)} %collective-permute-done.4.across_ref, ...), custom_call_target="tpu_custom_call" | custom-call | flops 1358954496 | bytes 2359296 | tf_op jit(solution)/shard_map/transform/pallas_call | solution.py:432
  47.7 0.0 copy-start.9
  47.8 0.0 collective-permute-done.8.core_ref
  47.8 0.0 collective-permute-done.10.both_ref
  47.8 3.6 %transform.5 = (f32[6,40,384]{2,1,0:T(8,128)S(1)}, f32[6,32,256]{2,1,0:T(8,128)S(1)}) custom-call(s32[1]{0:T(128)} %bitcast.5.odd_ref, f32[240,256]{1,0:T(8,128)S(1)} %ends.1.own_ref, f32[240,256]{1,0:T(8,128)S(1)} %collective-permute-done.8.core_ref, f32[240,256]{1,0:T(8,128)} %collective-permute-done.9.across_ref, ...), custom_call_target="tpu_custom_call" | custom-call | flops 1132462080 | bytes 1966080 | tf_op jit(solution)/shard_map/transform/pallas_call | solution.py:432
  51.4 0.0 copy-start.7
  51.5 1.4 %image.1 = (f32[6,128,256]{2,1,0:T(8,128)S(1)}, f32[32,128]{1,0:T(8,128)S(1)}) custom-call(f32[6,128,256]{2,1,0:T(8,128)S(1)} %bitcast.17, s32[128,256]{1,0:T(8,128)S(1)} %copy-done.5, f32[128,128]{1,0:T(8,128)S(1)} %copy-done.14, f32[128,128]{1,0:T(8,128)S(1)} %get-tuple-element.23.refs_0_.edge_ref, f32[6,48,384]{2,1,0:T(8,128)S(1)} %get-tuple-element.24.p0_ref, ...), custom_call_target="tpu_custom_call" | custom-call | flops 5898240 | bytes 3932160 | tf_op jit(solution)/shard_map/image/pallas_call | solution.py:444
  52.9 12.4 %all_to_all.11 = f32[32,1,128]{2,1,0:T(1,128)S(1)} all-to-all(f32[32,1,128]{2,1,0:T(1,128)S(1)} %bitcast.20), channel_id=1, replica_groups=mesh['ax'=8,'sec'=4] {'ax','sec'}, dimensions={0} | all-to-all | bytes 32768 | tf_op jit(solution)/shard_map/all_to_all | solution.py:448
  65.2 1.5 %update.1 = (f32[6,128,256]{2,1,0:T(8,128)}, f32[6,128,256]{2,1,0:T(8,128)}, f32[1,128]{1,0:T(1,128)S(1)}) custom-call(f32[6,128,256]{2,1,0:T(8,128)S(1)} %bitcast.15, f32[6,128,256]{2,1,0:T(8,128)S(1)} %get-tuple-element.34.image_ref, f32[32,128]{1,0:T(8,128)S(1)} %bitcast.19, f32[6,48,384]{2,1,0:T(8,128)S(1)} %get-tuple-element.24.p0_ref, ...), custom_call_target="tpu_custom_call" | custom-call | flops 786432 | bytes 4718592 | tf_op jit(solution)/shard_map/update/pallas_call | solution.py:449
  66.8 0.5 slice_bitcast_fusion
  (20 shorter events, 0.1 us)
Async XLA Ops:
  0.7 0.9 %copy-start.4 = (s32[128,256]{1,0:T(8,128)S(1)}, s32[128,256]{1,0:T(8,128)}, u32[]{:S(2)}) copy-start(s32[128,256]{1,0:T(8,128)} %hole_ref.3) | copy-start | bytes 393220
  1.6 1.1 %copy-start.6 = (f32[128,6,256]{2,0,1:T(8,128)S(1)}, f32[128,6,256]{2,0,1:T(8,128)}, u32[]{:S(2)}) copy-start(f32[128,6,256]{2,0,1:T(8,128)} %param.13) | copy-start | bytes 2359300
  2.8 1.1 %copy-start.8 = (f32[128,6,256]{2,0,1:T(8,128)S(1)}, f32[128,6,256]{2,0,1:T(8,128)}, u32[]{:S(2)}) copy-start(f32[128,6,256]{2,0,1:T(8,128)} %param.14) | copy-start | bytes 2359300
  3.9 1.1 %copy-start.11 = (f32[128,6,256]{2,0,1:T(8,128)S(1)}, f32[128,6,256]{2,0,1:T(8,128)}, u32[]{:S(2)}) copy-start(f32[128,6,256]{2,0,1:T(8,128)} %param.12) | copy-start | bytes 2359300
  5.0 0.7 %copy-start.15 = (f32[4,6]{1,0:T(4,128)S(1)}, f32[4,6]{1,0:T(4,128)}, u32[]{:S(2)}) copy-start(f32[4,6]{1,0:T(4,128)} %table_ref.1) | copy-start | bytes 292
  5.7 0.7 copy-start.16
  8.7 21.0 %copy-start.13 = (f32[128,128]{1,0:T(8,128)}, f32[128,128]{1,0:T(8,128)S(1)}, u32[]{:S(2)}) copy-start(f32[128,128]{1,0:T(8,128)S(1)} %get-tuple-element.21.factor_ref) | copy-start | bytes 196612
  8.8 29.0 %copy-start = (bf16[3072,384]{1,0:T(8,128)(2,1)S(1)}, bf16[3072,384]{1,0:T(8,128)(2,1)}, u32[]{:S(2)}) copy-start(bf16[3072,384]{1,0:T(8,128)(2,1)} %constant.40.clone.refs_3_.refs_4_) | copy-start | bytes 7077892
  8.8 29.0 %copy-start.2 = (bf16[768,256]{1,0:T(8,128)(2,1)S(1)}, bf16[768,256]{1,0:T(8,128)(2,1)}, u32[]{:S(2)}) copy-start(bf16[768,256]{1,0:T(8,128)(2,1)} %constant.38.clone.refs_1_.refs_2_) | copy-start | bytes 1179652
  8.8 29.0 %copy-start.3 = (bf16[768,256]{1,0:T(8,128)(2,1)S(1)}, bf16[768,256]{1,0:T(8,128)(2,1)}, u32[]{:S(2)}) copy-start(bf16[768,256]{1,0:T(8,128)(2,1)} %constant.37.clone.refs_0_.refs_1_) | copy-start | bytes 1179652
  8.8 29.0 %copy-start.5 = (s32[128,256]{1,0:T(8,128)S(1)}, s32[128,256]{1,0:T(8,128)}, u32[]{:S(2)}) copy-start(s32[128,256]{1,0:T(8,128)} %hole_ref.3) | copy-start | bytes 393220
  8.8 11.4 %collective-permute-start.1 = (f32[296,256]{1,0:T(8,128)}, f32[296,256]{1,0:T(8,128)}, u32[]{:S(2)}, u32[]{:S(2)}) collective-permute-start(f32[296,256]{1,0:T(8,128)} %get-tuple-element.22.own_ref), channel_id=1, source_target_pairs={{0,2},{1,3},{2,0},{3,1},{4,6},{5,7},{6,4},{7,5},{8,10},{9,11},{10,... | collective-permute-start | bytes 909320 | tf_op jit(solution)/shard_map/ppermute | solution.py:401
  11.8 19.5 %collective-permute-start.4 = (f32[288,256]{1,0:T(8,128)}, f32[288,256]{1,0:T(8,128)}, u32[]{:S(2)}, u32[]{:S(2)}) collective-permute-start(f32[288,256]{1,0:T(8,128)} %get-tuple-element.25.own_ref), channel_id=1, source_target_pairs={{0,2},{1,3},{2,0},{3,1},{4,6},{5,7},{6,4},{7,5},{8,10},{9,11},{10,... | collective-permute-start | bytes 884744 | tf_op jit(solution)/shard_map/ppermute | solution.py:401
  11.9 25.4 %collective-permute-start = (f32[296,256]{1,0:T(8,128)}, f32[296,256]{1,0:T(8,128)}, u32[]{:S(2)}, u32[]{:S(2)}) collective-permute-start(f32[296,256]{1,0:T(8,128)} %get-tuple-element.22.own_ref), channel_id=1, source_target_pairs={{0,1},{1,0},{2,3},{3,2},{4,5},{5,4},{6,7},{7,6},{8,9},{9,8},{10,11... | collective-permute-start | bytes 909320 | tf_op jit(solution)/shard_map/ppermute | solution.py:404
  20.1 17.6 %collective-permute-start.2 = (f32[296,256]{1,0:T(8,128)}, f32[296,256]{1,0:T(8,128)}, u32[]{:S(2)}, u32[]{:S(2)}) collective-permute-start(f32[296,256]{1,0:T(8,128)} %collective-permute-done.1.across_ref), channel_id=1, source_target_pairs={{0,1},{1,0},{2,3},{3,2},{4,5},{5,4},{6,7},{7,6},{8,9},{9,8},{10,11... | collective-permute-start | bytes 909320 | tf_op jit(solution)/shard_map/ppermute | solution.py:404
  20.1 5.4 %collective-permute-start.6 = (f32[16,256]{1,0:T(8,128)S(1)}, f32[16,256]{1,0:T(8,128)S(1)}, u32[]{:S(2)}, u32[]{:S(2)}) collective-permute-start(f32[16,256]{1,0:T(8,128)S(1)} %get-tuple-element.28.up_ref), channel_id=1, source_target_pairs={{0,4},{4,8},{8,12},{12,16},{16,20},{20,24},{24,28},{1,5},{5,9},{9,... | collective-permute-start | bytes 49160 | tf_op jit(solution)/shard_map/ppermute | solution.py:411
  24.1 5.6 %collective-permute-start.7 = (f32[16,256]{1,0:T(8,128)S(1)}, f32[16,256]{1,0:T(8,128)S(1)}, u32[]{:S(2)}, u32[]{:S(2)}) collective-permute-start(f32[16,256]{1,0:T(8,128)S(1)} %get-tuple-element.29.down_ref), channel_id=1, source_target_pairs={{4,0},{8,4},{12,8},{16,12},{20,16},{24,20},{28,24},{5,1},{9,5},{13... | collective-permute-start | bytes 49160 | tf_op jit(solution)/shard_map/ppermute | solution.py:412
  29.8 7.4 %collective-permute-start.9 = (f32[240,256]{1,0:T(8,128)S(1)}, f32[240,256]{1,0:T(8,128)}, u32[]{:S(2)}, u32[]{:S(2)}) collective-permute-start(f32[240,256]{1,0:T(8,128)S(1)} %ends.1.own_ref), channel_id=1, source_target_pairs={{0,2},{1,3},{2,0},{3,1},{4,6},{5,7},{6,4},{7,5},{8,10},{9,11},{10,... | collective-permute-start | bytes 737288 | tf_op jit(solution)/shard_map/ppermute | solution.py:401
  31.4 12.2 %collective-permute-start.3 = (f32[288,256]{1,0:T(8,128)}, f32[288,256]{1,0:T(8,128)}, u32[]{:S(2)}, u32[]{:S(2)}) collective-permute-start(f32[288,256]{1,0:T(8,128)} %get-tuple-element.25.own_ref), channel_id=1, source_target_pairs={{0,1},{1,0},{2,3},{3,2},{4,5},{5,4},{6,7},{7,6},{8,9},{9,8},{10,11... | collective-permute-start | bytes 884744 | tf_op jit(solution)/shard_map/ppermute | solution.py:404
  31.4 12.2 %collective-permute-start.5 = (f32[288,256]{1,0:T(8,128)}, f32[288,256]{1,0:T(8,128)}, u32[]{:S(2)}, u32[]{:S(2)}) collective-permute-start(f32[288,256]{1,0:T(8,128)} %collective-permute-done.4.across_ref), channel_id=1, source_target_pairs={{0,1},{1,0},{2,3},{3,2},{4,5},{5,4},{6,7},{7,6},{8,9},{9,8},{10,11... | collective-permute-start | bytes 884744 | tf_op jit(solution)/shard_map/ppermute | solution.py:404
  33.5 1.6 %copy-start.10 = (bf16[1024,1024]{1,0:T(8,128)(2,1)S(1)}, bf16[1024,1024]{1,0:T(8,128)(2,1)}, u32[]{:S(2)}) copy-start(bf16[1024,1024]{1,0:T(8,128)(2,1)} %constant.36.clone.fold_ref) | copy-start | bytes 6291460
  35.1 0.9 %copy-start.12 = (f32[36,1024]{1,0:T(8,128)S(1)}, f32[36,1024]{1,0:T(8,128)}, u32[]{:S(2)}) copy-start(f32[36,1024]{1,0:T(8,128)} %reshape.19.precond_ref) | copy-start | bytes 442372
  37.2 10.6 %collective-permute-start.8 = (f32[240,256]{1,0:T(8,128)S(1)}, f32[240,256]{1,0:T(8,128)S(1)}, u32[]{:S(2)}, u32[]{:S(2)}) collective-permute-start(f32[240,256]{1,0:T(8,128)S(1)} %ends.1.own_ref), channel_id=1, source_target_pairs={{0,1},{1,0},{2,3},{3,2},{4,5},{5,4},{6,7},{7,6},{8,9},{9,8},{10,11... | collective-permute-start | bytes 737288 | tf_op jit(solution)/shard_map/ppermute | solution.py:404
  37.3 10.5 %collective-permute-start.10 = (f32[240,256]{1,0:T(8,128)}, f32[240,256]{1,0:T(8,128)S(1)}, u32[]{:S(2)}, u32[]{:S(2)}) collective-permute-start(f32[240,256]{1,0:T(8,128)} %collective-permute-done.9.across_ref), channel_id=1, source_target_pairs={{0,1},{1,0},{2,3},{3,2},{4,5},{5,4},{6,7},{7,6},{8,9},{9,8},{10,11... | collective-permute-start | bytes 737288 | tf_op jit(solution)/shard_map/ppermute | solution.py:404
  37.8 1.4 %copy-start.1 = (bf16[1536,512]{1,0:T(8,128)(2,1)S(1)}, bf16[1536,512]{1,0:T(8,128)(2,1)}, u32[]{:S(2)}) copy-start(bf16[1536,512]{1,0:T(8,128)(2,1)} %constant.39.clone.refs_2_.refs_3_) | copy-start | bytes 4718596
  47.7 3.7 %copy-start.9 = (f32[128,6,256]{2,0,1:T(8,128)S(1)}, f32[128,6,256]{2,0,1:T(8,128)}, u32[]{:S(2)}) copy-start(f32[128,6,256]{2,0,1:T(8,128)} %param.14) | copy-start | bytes 2359300
  47.8 3.7 %copy-start.14 = (f32[128,128]{1,0:T(8,128)S(1)}, f32[128,128]{1,0:T(8,128)}, u32[]{:S(2)}) copy-start(f32[128,128]{1,0:T(8,128)} %copy-done.13) | copy-start | bytes 196612
  51.4 13.8 %copy-start.7 = (f32[128,6,256]{2,0,1:T(8,128)S(1)}, f32[128,6,256]{2,0,1:T(8,128)}, u32[]{:S(2)}) copy-start(f32[128,6,256]{2,0,1:T(8,128)} %param.13) | copy-start | bytes 2359300

commit v2 on v1

v2 whole, which is shorter than its diff:
```python
import functools

import jax
import jax.numpy as jnp
import ml_dtypes
import numpy as np
from jax import lax
from jax.experimental import pallas as pl
from jax.experimental.pallas import tpu as pltpu
from jax.sharding import PartitionSpec as P

F32 = jnp.float32
BF16 = jnp.bfloat16
SECTORS = 4
TILE = 8
LANES = 128


def three_terms(table):
    high = table.astype(ml_dtypes.bfloat16)
    low = (table - high.astype(np.float64)).astype(ml_dtypes.bfloat16)
    return np.concatenate([high, high, low], axis=0)


@functools.lru_cache(maxsize=None)
def harmonic_tables(width):
    around = SECTORS * width
    half = width // 2
    zero = [("c", 4 * q) for q in range(half + 1)] + [("s", 4 * q) for q in range(1, half)]
    two = [(f, 4 * q + 2) for f in "cs" for q in range(half)]
    one = [(f, 8 * q + 1) for f in "cs" for q in range(half)]
    five = [(f, 8 * q + 5) for f in "cs" for q in range(half)]
    columns = zero + two + one + five
    harmonic = np.array([k for _, k in columns], dtype=np.int64)
    is_sin = np.array([f == "s" for f, _ in columns])

    def wave(place, shift):
        angle = 2.0 * np.pi / around * ((place[:, None] * harmonic[None, :]) % around)
        return np.cos(angle - shift)

    place = np.arange(width)
    shift = np.where(is_sin, np.pi / 2, 0.0)[None, :]
    direct = wave(place, shift)
    turned = np.concatenate([direct[:half], wave(place[:half], shift - np.pi / 2)], axis=0)
    forward = [direct[:, :width], direct[:, width : 2 * width]]
    forward += [turned[:, 2 * width : 3 * width], turned[:, 3 * width :]]
    beyond = np.zeros((TILE, around), np.float32)
    beyond[:2] = wave(np.array([around - 1, width]), shift)
    fold = np.zeros((around, around))
    fold[harmonic, np.arange(around)] += 1.0 / around
    mirror = (around - harmonic) % around
    apart = mirror != harmonic
    fold[mirror[apart], np.arange(around)[apart]] += 1.0 / around
    return (
        np.concatenate([three_terms(t) for t in forward], axis=0),
        three_terms(direct.T),
        beyond,
        fold.astype(ml_dtypes.bfloat16),
    )


def split(x):
    high = x.astype(BF16)
    return high, (x - high.astype(F32)).astype(BF16)


def lanes_of(shape):
    return lax.broadcasted_iota(jnp.int32, shape, len(shape) - 1)


def rows_of(shape):
    return lax.broadcasted_iota(jnp.int32, shape, len(shape) - 2)


def beside_sum(x, before, after):
    lane = lanes_of(x.shape)
    size = x.shape[-1]
    left = jnp.where(lane == 0, before, pltpu.roll(x, 1, x.ndim - 1))
    right = jnp.where(lane == size - 1, after, pltpu.roll(x, size - 1, x.ndim - 1))
    return left + right


def stacked_sum(x, before=0.0, after=0.0):
    row = rows_of(x.shape)
    size = x.shape[0]
    up = jnp.where(row == 0, before, pltpu.roll(x, 1, 0))
    down = jnp.where(row == size - 1, after, pltpu.roll(x, size - 1, 0))
    return up + down


def fold_kernel(precond_ref, fold_ref, out_ref):
    value = jnp.concatenate([precond_ref[q] for q in range(precond_ref.shape[0])], axis=0)
    high = value.astype(BF16)
    rest = value - high.astype(F32)
    middle = rest.astype(BF16)
    low = (rest - middle.astype(F32)).astype(BF16)
    terms = [jnp.dot(t, fold_ref[...], preferred_element_type=F32) for t in (high, middle, low)]
    out_ref[...] = terms[0] + (terms[1] + terms[2])


def factor_columns(table_ref, class_ref, ax_size, comps):
    classes = class_ref[...]
    slab = classes.shape[1]
    position = lax.axis_index("ax") * slab + lanes_of(classes.shape)
    taper = 1.0 + 2.0 * position.astype(F32) / F32(ax_size * slab - 1)
    rows = []
    for q in range(comps):
        value = jnp.zeros(classes.shape, F32)
        for kind in range(table_ref.shape[0]):
            value = jnp.where(classes == kind, table_ref[kind, q], value)
        rows.append(value * taper)
    rows.append(jnp.zeros((LANES - comps, slab), F32))
    return jnp.concatenate(rows, axis=0).T


def copies(pairs, sems):
    started = [pltpu.make_async_copy(src, dst, sems.at[i]) for i, (src, dst) in enumerate(pairs)]
    for copy in started:
        copy.start()
    return started


def local_part(q, low, high, slab, solid, factor, load, stiff, disp_ref):
    start, stop = max(low - TILE, 0), min(high + TILE, slab)
    inner = slice(low - start, high - start)
    block = disp_ref[q, start:stop]
    field = block[inner]
    beside = stacked_sum(block)[inner] + beside_sum(field, 0.0, 0.0)
    stiffness = stiff * factor[low:high, q : q + 1]
    image = (stiffness + 4.5) * field - beside - 0.5 * disp_ref[q ^ 1, low:high]
    return solid[low:high] * (load - image)


def first_kernel(
    cuts, comps, ax_size, table_ref, class_ref, load_ref, disp_ref, stiff_ref, hole_ref,
    first_ref, load_in, disp_in, stiff_in, hole_in, sems,
):
    slab, width = hole_ref.shape
    a, b, _ = cuts
    moving = copies(
        [(hole_ref, hole_in)]
        + [(disp_ref.at[q], disp_in.at[q]) for q in range(comps)]
        + [(load_ref.at[q, pl.ds(a, b - a)], load_in.at[q]) for q in range(comps)]
        + [(stiff_ref.at[q, pl.ds(a, b - a)], stiff_in.at[q]) for q in range(comps)],
        sems,
    )
    factor = factor_columns(table_ref, class_ref, ax_size, comps)
    for copy in moving[: 1 + comps]:
        copy.wait()
    solid = (1 - hole_in[...]).astype(F32)
    spare = TILE - comps
    edge_left = [disp_in[q, :, 0:1] for q in range(comps)] + [solid[:, 0:1]] * spare
    edge_right = [disp_in[q, :, width - 1 : width] for q in range(comps)]
    edge_right += [solid[:, width - 1 : width]] * spare
    rest = [jnp.zeros((slab, LANES - 2 * TILE), F32)]
    edges = jnp.concatenate(edge_left + edge_right + rest, axis=1).T
    first_ref[pl.ds(comps * (b - a), TILE), :] = jnp.concatenate(
        [edges[:TILE], edges[TILE : 2 * TILE]], axis=1
    )
    for q in range(comps):
        moving[1 + comps + q].wait()
        moving[1 + 2 * comps + q].wait()
        first_ref[pl.ds(q * (b - a), b - a), :] = local_part(
            q, a, b, slab, solid, factor, load_in[q], stiff_in[q], disp_in
        )


def second_kernel(
    cuts, comps, ax_size, table_ref, class_ref, load_ref, disp_ref, stiff_ref, hole_ref,
    second_ref, ends_ref, factor_ref, up_ref, down_ref, load_in, disp_in, stiff_in, hole_in, sems,
):
    slab, width = hole_ref.shape
    a, b, c = cuts
    pairs = [(hole_ref, hole_in)] + [(disp_ref.at[q], disp_in.at[q]) for q in range(comps)]
    for q in range(comps):
        for src, dst in ((load_ref, load_in), (stiff_ref, stiff_in)):
            pairs.append((src.at[q, pl.ds(0, a)], dst.at[q, pl.ds(0, a)]))
            pairs.append((src.at[q, pl.ds(b, slab - b)], dst.at[q, pl.ds(a, slab - b)]))
    moving = copies(pairs, sems)
    factor_ref[...] = factor_columns(table_ref, class_ref, ax_size, comps)
    for copy in moving[: 1 + comps]:
        copy.wait()
    factor = factor_ref[...]
    solid = (1 - hole_in[...]).astype(F32)
    ends = a + slab - c
    for q in range(comps):
        for copy in moving[1 + comps + 4 * q : 5 + comps + 4 * q]:
            copy.wait()
        part = local_part(
            q, b, slab, slab, solid, factor, load_in[q, a:], stiff_in[q, a:], disp_in
        )
        top = local_part(q, 0, a, slab, solid, factor, load_in[q, :a], stiff_in[q, :a], disp_in)
        second_ref[pl.ds(q * (c - b), c - b), :] = part[: c - b]
        ends_ref[pl.ds(q * ends, a), :] = top
        ends_ref[pl.ds(q * ends + a, slab - c), :] = part[c - b :]
        up_ref[q : q + 1, :] = part[slab - b - 1 :]
        down_ref[q : q + 1, :] = top[:1]
        up_ref[TILE + q : TILE + q + 1, :] = disp_in[q, slab - 1 :]
        down_ref[TILE + q : TILE + q + 1, :] = disp_in[q, :1]
    spare = TILE - comps
    for ref, row in ((up_ref, slab - 1), (down_ref, 0)):
        ref[comps:TILE, :] = jnp.broadcast_to(solid[row : row + 1], (spare, width))
        ref[TILE + comps :, :] = jnp.zeros((spare, width), F32)


def ends_kernel(comps, ends_ref, up_ref, down_ref, before_ref, after_ref, out_ref):
    rows = ends_ref.shape[0] // comps
    width = ends_ref.shape[1]
    row = rows_of((rows, width))
    spare = rows_of((TILE, width))
    solid_before = before_ref[comps : comps + 1]
    solid_after = after_ref[comps : comps + 1]
    for q in range(comps):
        disp_before = before_ref[TILE + q : TILE + q + 1]
        disp_after = after_ref[TILE + q : TILE + q + 1]
        part = ends_ref[pl.ds(q * rows, rows), :]
        part = part + jnp.where(row == 0, down_ref[comps : comps + 1] * disp_before, 0.0)
        part = part + jnp.where(row == rows - 1, up_ref[comps : comps + 1] * disp_after, 0.0)
        out_ref[pl.ds(q * (rows + TILE), rows), :] = part
        res_before = before_ref[q : q + 1] + solid_before * down_ref[TILE + q : TILE + q + 1]
        res_after = after_ref[q : q + 1] + solid_after * up_ref[TILE + q : TILE + q + 1]
        beyond = jnp.zeros((TILE, width), F32)
        for i, value in enumerate((res_before, res_after, disp_before, disp_after, solid_before, solid_after)):
            beyond = jnp.where(spare == i, value, beyond)
        out_ref[pl.ds(q * (rows + TILE) + rows, TILE), :] = beyond


def in_order(odd, own, core, across, both):
    return own, jnp.where(odd, both, core), across, jnp.where(odd, core, both)


def butterfly(x0, x1, x2, x3):
    even, other = x0 + x2, x1 + x3
    return even + other, even - other, x0 - x2, x1 - x3


def edge_table(odd, blocks):
    tiles = in_order(odd, *blocks)
    left = [t[:, :LANES] for t in tiles]
    right = [t[:, LANES:] for t in tiles]
    solid = TILE - 1
    at_left = [left[s][solid:] * right[s - 1] for s in range(SECTORS)]
    at_right = [right[s][solid:] * left[(s + 1) % SECTORS] for s in range(SECTORS)]
    stack = []
    for one, other in zip(butterfly(*at_left), butterfly(*at_right)):
        stack += [one, other]
    stack += [at_left[0], at_right[0], right[3], left[1]]
    stack.append(jnp.zeros((LANES - len(stack) * TILE, LANES), F32))
    return jnp.concatenate(stack, axis=0).T


def transform_kernel(comps, rows_at, spare, make_edge, own_ref, core_ref, across_ref, both_ref, *refs):
    refs = list(refs)
    edge_in = None if make_edge else refs.pop(0)
    forward_ref, inverse_ref, beyond_ref, weight_ref, hole_ref = refs[:5]
    refs = refs[5:]
    edge_ref = refs.pop(0) if make_edge else edge_in
    prec_ref, residual_ref, left_ref, spectrum_ref, scaled_ref, halo_ref = refs
    width = own_ref.shape[1]
    half = width // 2
    odd = lax.axis_index("sec") % 2 == 1
    sign = jnp.where(odd, -1.0, 1.0)
    main = sum(size for _, size in rows_at)
    rows = main + spare
    total = comps * rows
    group = 1 if rows % 16 == 0 else 2
    sources = (own_ref, core_ref, across_ref, both_ref)
    if make_edge:
        edge_ref[...] = edge_table(odd, [r[total : total + TILE] for r in sources])
    solid = jnp.concatenate([(1 - hole_ref[pl.ds(at, size)]).astype(F32) for at, size in rows_at], axis=0)
    edge = jnp.concatenate([edge_ref[pl.ds(at, size)] for at, size in rows_at], axis=0)
    lane = lanes_of((main, LANES))
    first = lane == 0
    last = lane == LANES - 1

    def with_edges(x, array, q):
        column = array * 2 * TILE + q
        head = x[:, :LANES] + jnp.where(first, edge[:, column : column + 1], 0.0)
        tail = x[:, -LANES:] + jnp.where(last, edge[:, column + TILE : column + TILE + 1], 0.0)
        middle = [x[:, LANES:-LANES]] if width > 2 * LANES else []
        return jnp.concatenate([head] + middle + [tail], axis=1)

    def arrays_of(q):
        at = q * rows
        own, core, across, both = [r[pl.ds(at, main), :] for r in sources]
        arrays = butterfly(own, core, across, both)
        arrays = arrays[:3] + (sign * arrays[3],)
        arrays = [with_edges(x, i, q) for i, x in enumerate(arrays)]
        residual_ref[q] = with_edges(own, 4, q)
        mask = None
        if spare:
            tiles = in_order(odd, *[r[pl.ds(at + main, spare), :] for r in sources])
            disp = [pltpu.roll(t, spare - 2, 0) for t in tiles]
            holes = [pltpu.roll(t, spare - 4, 0) for t in tiles]
            place = lanes_of((spare, width))
            fixed = []
            for s in range(SECTORS):
                beside = jnp.where(place == 0, pltpu.roll(disp[s - 1], 1, 1), 0.0)
                beside = beside + jnp.where(
                    place == width - 1, pltpu.roll(disp[(s + 1) % SECTORS], width - 1, 1), 0.0
                )
                value = tiles[s] + holes[s] * beside
                fixed.append(jnp.where(rows_of((spare, width)) < 2, value, 0.0))
            mask = holes[0]
            arrays = [jnp.concatenate(pair, axis=0) for pair in zip(arrays, butterfly(*fixed))]
        y0, y2, real, imag = arrays
        turned_real = (real[:, half:] - imag[:, half:]) * F32(np.sqrt(0.5))
        turned_imag = (real[:, half:] + imag[:, half:]) * F32(np.sqrt(0.5))
        plus = jnp.concatenate([real[:, :half] + turned_real, imag[:, :half] + turned_imag], axis=1)
        minus = jnp.concatenate([real[:, :half] - turned_real, imag[:, :half] - turned_imag], axis=1)
        return (y0, y2, plus, minus), mask

    masks = []
    for start in range(0, comps, group):
        found = [arrays_of(q) for q in range(start, start + group)]
        masks += [mask for _, mask in found]
        at = pl.ds(start * rows, group * rows)
        for i in range(4):
            high, low = split(jnp.concatenate([arrays[i] for arrays, _ in found], axis=0))
            left_ref[at, 2 * i * width : (2 * i + 1) * width] = high
            left_ref[at, (2 * i + 1) * width : (2 * i + 2) * width] = low

    for i in range(4):
        high = left_ref[:, 2 * i * width : (2 * i + 1) * width]
        low = left_ref[:, (2 * i + 1) * width : (2 * i + 2) * width]
        spectrum_ref[:, i * width : (i + 1) * width] = jnp.dot(
            jnp.concatenate([high, low, high], axis=1),
            forward_ref[pl.ds(3 * i * width, 3 * width), :],
            preferred_element_type=F32,
        )

    around = SECTORS * width
    block = rows if group > 1 else 16

    def scale(step, carry):
        def at(q, count):
            return pl.ds(pl.multiple_of(q * rows + step * block, TILE), count)

        halo = [[jnp.zeros((block, LANES), F32) for _ in range(2)] for _ in range(comps)]
        for lanes in range(0, around, LANES):
            here = slice(lanes, lanes + LANES)
            parts = [spectrum_ref[at(p, block), here] for p in range(comps)]
            for start in range(0, comps, group):
                values = []
                for q in range(start, start + group):
                    value = parts[0] * weight_ref[q * comps : q * comps + 1, here]
                    for p in range(1, comps):
                        value = value + parts[p] * weight_ref[q * comps + p : q * comps + p + 1, here]
                    for i in range(2):
                        halo[q][i] = halo[q][i] + value * beyond_ref[i : i + 1, here]
                    values.append(value)
                high, low = split(jnp.concatenate(values, axis=0))
                scaled_ref[at(start, group * block), here] = high
                scaled_ref[at(start, group * block), around + lanes : around + lanes + LANES] = low
        for q in range(comps):
            before, after = [jnp.sum(x, axis=1, keepdims=True) for x in halo[q]]
            halo_ref[at(q, block), :] = jnp.where(lanes_of((block, LANES)) == 0, before, after)
        return carry

    lax.fori_loop(0, rows // block, scale, 0)
    high = scaled_ref[:, :around]
    result = jnp.dot(
        jnp.concatenate([high, scaled_ref[:, around:], high], axis=1),
        inverse_ref[...],
        preferred_element_type=F32,
    )
    for q in range(comps):
        at = q * rows
        prec_ref[q, :main, :width] = result[at : at + main] * solid
        prec_ref[q, :, width:] = halo_ref[pl.ds(at, rows), :]
        if spare:
            prec_ref[q, main:, :width] = result[at + main : at + rows] * masks[q]


def image_rows(q, fields, tiles, edge, stiff, solid, factor, before, after, inner):
    field = fields[q][inner]
    solid_before = edge[:, 11 * TILE - 1 : 11 * TILE]
    solid_after = edge[:, 12 * TILE - 1 : 12 * TILE]
    beside = beside_sum(field, tiles[q][:, :1] * solid_before, tiles[q][:, 1:2] * solid_after)
    beside = beside + stacked_sum(fields[q], before, after)[inner]
    stiffness = stiff * factor[:, q : q + 1]
    return field, solid * ((stiffness + 4.5) * field - beside - 0.5 * fields[q ^ 1][inner])


def add_sums(sums, residual, field, image):
    rows, width = field.shape
    pairs = ((residual, field), (field, image), (residual, residual), (residual, image), (image, image))
    return [
        total + jnp.sum((x * y).reshape(rows // TILE, TILE, width), axis=0)
        for total, (x, y) in zip(sums, pairs)
    ]


def middle_kernel(
    cuts, comps, stiff_ref, hole_ref, factor_ref, edge_ref, p0_ref, p1_ref, r0_ref, r1_ref, image_ref, sums_ref,
):
    slab, width = hole_ref.shape
    a, b, c = cuts
    low, high = a + TILE, c - TILE
    fields = [jnp.concatenate([p0_ref[q, :, :width], p1_ref[q, :, :width]], axis=0) for q in range(comps)]
    solid = (1 - hole_ref[low:high]).astype(F32)
    factor, edge = factor_ref[low:high], edge_ref[low:high]
    sums = [jnp.zeros((TILE, width), F32) for _ in range(5)]
    for q in range(comps):
        tile = jnp.concatenate([p0_ref[q, TILE:, width:], p1_ref[q, :-TILE, width:]], axis=0)
        field, image = image_rows(
            q, fields, {q: tile}, edge, stiff_ref[q, low:high], solid, factor, 0.0, 0.0, slice(TILE, -TILE)
        )
        image_ref[q] = image
        residual = jnp.concatenate([r0_ref[q, TILE:], r1_ref[q, :-TILE]], axis=0)
        sums = add_sums(sums, residual, field, image)
    for i, total in enumerate(sums):
        sums_ref[pl.ds(i * TILE, TILE), :] = total


def outer_kernel(
    cuts, comps, stiff_ref, hole_ref, factor_ref, edge_ref, p0_ref, p1_ref, p2_ref,
    r0_ref, r1_ref, r2_ref, partial_ref, image_ref, sums_ref,
):
    slab, width = hole_ref.shape
    a, b, c = cuts
    own, side = slice(0, width), slice(width, width + LANES)
    reach = a + TILE
    spare = a + slab - c
    sums = [partial_ref[pl.ds(i * TILE, TILE), :] for i in range(5)]
    tops = [jnp.concatenate([p2_ref[q, :a, own], p0_ref[q, : 2 * TILE, own]], axis=0) for q in range(comps)]
    bottoms = [jnp.concatenate([p1_ref[q, -2 * TILE :, own], p2_ref[q, a:spare, own]], axis=0) for q in range(comps)]
    solid = (1 - hole_ref[...]).astype(F32)
    factor, edge = factor_ref[...], edge_ref[...]
    for q in range(comps):
        tile = jnp.concatenate([p2_ref[q, :a, side], p0_ref[q, :TILE, side]], axis=0)
        rows = slice(0, reach)
        field, image = image_rows(
            q, tops, {q: tile}, edge[rows], stiff_ref[q, rows], solid[rows], factor[rows],
            p2_ref[q, spare : spare + 1, own], 0.0, slice(0, reach),
        )
        image_ref[q, :reach] = image
        residual = jnp.concatenate([r2_ref[q, :a], r0_ref[q, :TILE]], axis=0)
        sums = add_sums(sums, residual, field, image)
        tile = jnp.concatenate([p1_ref[q, -TILE:, side], p2_ref[q, a:spare, side]], axis=0)
        rows = slice(c - TILE, slab)
        field, image = image_rows(
            q, bottoms, {q: tile}, edge[rows], stiff_ref[q, rows], solid[rows], factor[rows],
            0.0, p2_ref[q, spare + 1 : spare + 2, own], slice(TILE, None),
        )
        image_ref[q, reach:] = image
        residual = jnp.concatenate([r1_ref[q, -TILE:], r2_ref[q, a:]], axis=0)
        sums = add_sums(sums, residual, field, image)
    row = jnp.zeros((1, LANES), F32)
    spot = lanes_of((1, LANES))
    for i, value in enumerate(sums):
        value = jnp.sum(jnp.sum(value, axis=0, keepdims=True), axis=1, keepdims=True)
        row = jnp.where(spot == i, value, row)
    sums_ref[...] = jnp.broadcast_to(row, sums_ref.shape)


def update_kernel(
    cuts, comps, cell_total, disp_ref, middle_ref, outer_ref, gathered_ref,
    p0_ref, p1_ref, p2_ref, r0_ref, r1_ref, r2_ref, disp_out, residual_out, stats_out,
):
    slab, width = disp_ref.shape[1:]
    a, b, c = cuts
    values = jnp.sum(gathered_ref[...], axis=0, keepdims=True) * F32(1.0 / cell_total)
    rz, zq, rr, ri, ii = [values[:, i : i + 1] for i in range(5)]
    alpha = rz / zq
    square = rr + alpha * (alpha * ii - 2.0 * ri)
    stats_out[...] = jnp.concatenate([rz, zq, square], axis=1)
    own = slice(0, width)
    reach = a + TILE
    for q in range(comps):
        disp_out[q, :a] = disp_ref[q, :a] + alpha * p2_ref[q, :a, own]
        disp_out[q, a:b] = disp_ref[q, a:b] + alpha * p0_ref[q, :, own]
        disp_out[q, b:c] = disp_ref[q, b:c] + alpha * p1_ref[q, :, own]
        disp_out[q, c:] = disp_ref[q, c:] + alpha * p2_ref[q, a : a + slab - c, own]
        image = jnp.concatenate([outer_ref[q, :reach], middle_ref[q], outer_ref[q, reach:]], axis=0)
        residual_out[q, :a] = r2_ref[q, :a] - alpha * image[:a]
        residual_out[q, a:b] = r0_ref[q] - alpha * image[a:b]
        residual_out[q, b:c] = r1_ref[q] - alpha * image[b:c]
        residual_out[q, c:] = r2_ref[q, a:] - alpha * image[c:]


VMEM = pl.BlockSpec(memory_space=pltpu.VMEM)
SMEM = pl.BlockSpec(memory_space=pltpu.SMEM)
HBM = pl.BlockSpec(memory_space=pltpu.HBM)
FULL = 62


def call(kernel, name, out_shapes, in_specs, flops, moved, scratch=(), grant=32):
    return pl.pallas_call(
        kernel,
        out_shape=[jax.ShapeDtypeStruct(s, F32) for s in out_shapes],
        in_specs=in_specs,
        out_specs=[VMEM] * len(out_shapes),
        scratch_shapes=list(scratch),
        compiler_params=pltpu.CompilerParams(vmem_limit_bytes=grant * 1024 * 1024),
        cost_estimate=pl.CostEstimate(flops=flops, bytes_accessed=moved, transcendentals=0),
        name=name,
    )


def transform_call(blocks, edge, tables, hole, rows_at, spare, comps, width, slab):
    forward, inverse, beyond, weight = tables
    around = SECTORS * width
    main = sum(size for _, size in rows_at)
    rows = main + spare
    total = comps * rows
    out_shapes = [(comps, rows, width + LANES), (comps, main, width)]
    if edge is None:
        out_shapes = [(slab, LANES)] + out_shapes
    operands = list(blocks) + ([] if edge is None else [edge]) + [forward, inverse, beyond, weight, hole]
    return call(
        functools.partial(transform_kernel, comps, rows_at, spare, edge is None), "transform",
        out_shapes, [VMEM] * len(operands),
        2 * total * 3 * around * 2 * width, 4 * total * width * 8,
        [pltpu.VMEM((total, 8 * width), BF16), pltpu.VMEM((total, around), F32),
         pltpu.VMEM((total, 2 * around), BF16), pltpu.VMEM((total, LANES), F32)],
    )(*operands)


def after_all(x, *others):
    return lax.optimization_barrier((x, *others))[0]


def shards(load, disp, stiff, hole, section_class, class_table, precond):
    slab, comps, width = disp.shape
    ax, sec = lax.axis_size("ax"), lax.axis_size("sec")
    around = width * sec
    cell_total = slab * ax * comps * around
    cuts = (slab // 16, slab // 16 * 9, slab - slab // 16)
    a, b, c = cuts
    ends = a + slab - c
    load, disp, stiff = [x.transpose(1, 0, 2) for x in (load, disp, stiff)]
    forward, inverse, beyond, fold = harmonic_tables(width)
    block = 4 * comps * slab * width
    classes = section_class.reshape(1, slab)

    def inputs(rows, count):
        return [pltpu.VMEM((comps, rows, width), F32), pltpu.VMEM((comps, slab, width), F32),
                pltpu.VMEM((comps, rows, width), F32), pltpu.VMEM((slab, width), jnp.int32),
                pltpu.SemaphoreType.DMA((count,))]

    specs = [SMEM, VMEM] + [HBM] * 4
    arguments = (class_table, classes, load, disp, stiff, hole)
    (first,) = call(
        functools.partial(first_kernel, cuts, comps, ax), "first",
        [(comps * (b - a) + TILE, width)], specs, 10 * comps * slab * width, 2 * block,
        inputs(b - a, 1 + 3 * comps), FULL,
    )(*arguments)
    second, edge_rows, factor, up, down = call(
        functools.partial(second_kernel, cuts, comps, ax), "second",
        [(comps * (c - b), width), (comps * ends, width), (slab, LANES), (2 * TILE, width), (2 * TILE, width)],
        specs, 10 * comps * slab * width, 2 * block,
        inputs(a + slab - b, 1 + 5 * comps), FULL,
    )(*arguments)

    def across(x):
        return lax.ppermute(x, "sec", [(i, (i + sec // 2) % sec) for i in range(sec)])

    def beside(x):
        return lax.ppermute(x, "sec", [(i, i ^ 1) for i in range(sec)])

    far0 = across(first)
    far1 = across(second)
    before = lax.ppermute(up, "ax", [(i, i + 1) for i in range(ax - 1)])
    after = lax.ppermute(down, "ax", [(i + 1, i) for i in range(ax - 1)])
    (weight,) = call(
        fold_kernel, "fold", [(comps * comps, around)], [VMEM] * 2,
        6 * comps * comps * around * around, 2 * around * around,
    )(precond, fold)
    (last,) = call(
        functools.partial(ends_kernel, comps), "ends",
        [(comps * (ends + TILE), width)], [VMEM] * 5, comps * ends * width, 8 * comps * ends * width,
    )(edge_rows, up, down, before, after)
    far2 = across(last)
    tables = (forward, inverse, beyond, weight)

    far0 = after_all(far0, second, last)
    edge, prec0, res0 = transform_call(
        (first, beside(first), far0, beside(far0)), None, tables, hole, ((a, b - a),), 0, comps, width, slab
    )
    far1 = after_all(far1, prec0)
    prec1, res1 = transform_call(
        (second, beside(second), far1, beside(far1)), edge, tables, hole, ((b, c - b),), 0, comps, width, slab
    )
    far2 = after_all(far2, prec1)
    image, partial = call(
        functools.partial(middle_kernel, cuts, comps), "middle",
        [(comps, c - a - 2 * TILE, width), (5 * TILE, width)], [VMEM] * 8, 30 * comps * slab * width, 4 * block,
    )(stiff, hole, factor, edge, prec0, prec1, res0, res1)
    prec2, res2 = transform_call(
        (last, beside(last), far2, beside(far2)), edge, tables, hole, ((0, a), (c, slab - c)), TILE, comps, width, slab
    )
    image_ends, sums = call(
        functools.partial(outer_kernel, cuts, comps), "outer",
        [(comps, ends + 2 * TILE, width), (ax * sec, LANES)], [VMEM] * 11, 8 * comps * slab * width, block,
    )(stiff, hole, factor, edge, prec0, prec1, prec2, res0, res1, res2, partial)
    gathered = lax.all_to_all(sums, ("ax", "sec"), 0, 0, tiled=True)
    disp_new, residual_new, stats = call(
        functools.partial(update_kernel, cuts, comps, cell_total), "update",
        [(comps, slab, width), (comps, slab, width), (1, 3)], [VMEM] * 10,
        4 * comps * slab * width, 6 * block,
    )(disp, image, image_ends, gathered, prec0, prec1, prec2, res0, res1, res2)
    return disp_new.transpose(1, 0, 2), residual_new.transpose(1, 0, 2), stats.reshape(3)


def solution(mesh):
    in_specs = (
        P("ax", None, "sec"),
        P("ax", None, "sec"),
        P("ax", None, "sec"),
        P("ax", "sec"),
        P("ax"),
        P(),
        P(),
    )
    out_specs = (P("ax", None, "sec"), P("ax", None, "sec"), P())
    return jax.shard_map(shards, mesh=mesh, in_specs=in_specs, out_specs=out_specs, check_vma=False)
```

time: 67.8 us -> 57.6 us (0.85)
  local copies, waits for them, and re-layouts: 11.7 us -> 4.89 us
  waiting for transfers between devices: 12.6 us -> 5.87 us
  Pallas kernels: 18.7 us -> 22 us
    ppermute x3, waiting for transfers between devices: 8.26 us -> 0.95 us  [across(): lax.ppermute(x, 'sec', [(i, (i + sec // 2) % sec) for i in range(sec)])]
    unnamed x34 -> x28, local copies, waits for them, and re-layouts: 9.59 us -> 4.89 us
    pallas_call x5 -> x7, Pallas kernels: 15.9 us -> 19.5 us  [the longest x3 10.3 us: transform_call(): call(functools.partial(transform_kernel, comps, rows_at, spare, edge is N...]
    reshape x1 -> x0, local copies, waits for them, and re-layouts: 1.6 us -> none  [shards(): precond.reshape(comps * comps, around)]
  transfers between devices with their start and end apart: 11 -> 11, of which waited for: 3 -> 4; matrix products, arithmetic and copies ran while one was open for 2% -> 0% of each run, Pallas kernels for 14% -> 26%
where the time goes in v2:
time: 57.6 us; the launch traced here: 57.1 us
  Pallas kernels  22 us (38%)
  blocking collectives  12.8 us (22%)
  starting transfers between devices  10.7 us (19%)
  waiting for transfers between devices  5.87 us (10%)
  local copies, waits for them, and re-layouts  4.89 us (8%)
  between operations  0.87 us (2%)
    all_to_all x1, blocking collectives, shards(): gathered = lax.all_to_all(sums, ('ax', 'sec'), 0, 0, tiled=True)  12.8 us
    pallas_call x3, Pallas kernels, transform_call(): call(functools.partial(transform_kernel, comps, rows_at, spare, edge is N...  10.3 us
    ppermute x3, starting transfers between devices, across(): lax.ppermute(x, 'sec', [(i, (i + sec // 2) % sec) for i in range(sec)])  5.12 us
    unnamed x28, local copies, waits for them, and re-layouts  4.89 us
    ppermute x1, waiting for transfers between devices, shards(): after = lax.ppermute(down, 'ax', [(i + 1, i) for i in range(ax - 1)])  4.21 us
    pallas_call x1, Pallas kernels, shards(): call(functools.partial(first_kernel, cuts, comps, ax), 'first', [(comps *...  3.96 us
    pallas_call x1, Pallas kernels, shards(): call(functools.partial(second_kernel, cuts, comps, ax), 'second', [(comps...  3.87 us
    ppermute x1, starting transfers between devices, shards(): before = lax.ppermute(up, 'ax', [(i, i + 1) for i in range(ax - 1)])  3.53 us
  transfers between devices with their start and end apart: 11, of which 4 were waited for; matrix products, arithmetic and copies ran while one was open for 0% of the time, Pallas kernels for 26%

profile of v2, /device:TPU:0, one launch (start us, length us, event | category | flops | bytes accessed | tf_op | source)
XLA Modules:
  0.0 57.1 jit_solution(11357754511166041001)
XLA Ops:
  0.6 4.0 %first.1.own_ref = f32[392,256]{1,0:T(8,128)} custom-call(f32[4,6]{1,0:T(4,128)} %table_ref.3, s32[1,128]{1,0:T(1,128)} %bitcast.22, f32[6,128,256]{2,1,0:T(8,128)} %bitcast.20, f32[6,128,256]{2,1,0:T(8,128)} %bitcast.15, f32[6,128,256]{2,1,0:T(8,128)} %bitcast.11, s32[128,256]{1,0:T(8,128)} %hole_ref.7), custom_call_target="tpu_custom_call" | custom-call | flops 1966080 | bytes 1572864 | tf_op jit(solution)/shard_map/first/pallas_call | solution.py:544
  4.6 0.0 copy-start.6
  4.6 3.0 %collective-permute-start.1 = (f32[392,256]{1,0:T(8,128)}, f32[392,256]{1,0:T(8,128)}, u32[]{:S(2)}, u32[]{:S(2)}) collective-permute-start(f32[392,256]{1,0:T(8,128)} %first.1.own_ref), channel_id=1, source_target_pairs={{0,2},{1,3},{2,0},{3,1},{4,6},{5,7},{6,4},{7,5},{8,10},{9,11},{10,... | collective-permute-start | bytes 1204232 | tf_op jit(solution)/shard_map/ppermute | solution.py:557
  7.6 3.9 %second.1 = (f32[288,256]{1,0:T(8,128)}, f32[96,256]{1,0:T(8,128)}, f32[128,128]{1,0:T(8,128)}, f32[16,256]{1,0:T(8,128)}, f32[16,256]{1,0:T(8,128)}) custom-call(f32[4,6]{1,0:T(4,128)} %table_ref.3, s32[1,128]{1,0:T(1,128)} %bitcast.23, f32[6,128,256]{2,1,0:T(8,128)} %bitcast.21, f32[6,128,256]{2,1,0:T(8,128)} %bitcast.16, f32[6,128,256]{2,1,0:T(8,128)} %bitcast.12, ...), custom_call_target="tpu_custom_call" | custom-call | flops 1966080 | bytes 1572864 | tf_op jit(solution)/shard_map/second/pallas_call | solution.py:549
  11.5 0.0 copy-start
  11.5 0.0 copy-start.4
  11.6 3.5 %collective-permute-start.2 = (f32[16,256]{1,0:T(8,128)}, f32[16,256]{1,0:T(8,128)S(1)}, u32[]{:S(2)}, u32[]{:S(2)}) collective-permute-start(f32[16,256]{1,0:T(8,128)} %get-tuple-element.28.up_ref), channel_id=1, source_target_pairs={{0,4},{4,8},{8,12},{12,16},{16,20},{20,24},{24,28},{1,5},{5,9},{9,... | collective-permute-start | bytes 49160 | tf_op jit(solution)/shard_map/ppermute | solution.py:564
  15.1 1.3 %collective-permute-start.3 = (f32[16,256]{1,0:T(8,128)}, f32[16,256]{1,0:T(8,128)S(1)}, u32[]{:S(2)}, u32[]{:S(2)}) collective-permute-start(f32[16,256]{1,0:T(8,128)} %get-tuple-element.29.down_ref), channel_id=1, source_target_pairs={{4,0},{8,4},{12,8},{16,12},{20,16},{24,20},{28,24},{5,1},{9,5},{13... | collective-permute-start | bytes 49160 | tf_op jit(solution)/shard_map/ppermute | solution.py:565
  16.4 0.0 copy-done.6
  16.4 0.1 collective-permute-start
  16.5 0.2 collective-permute-done.2.before_ref
  16.7 4.2 %collective-permute-done.3.after_ref = f32[16,256]{1,0:T(8,128)S(1)} collective-permute-done((f32[16,256]{1,0:T(8,128)}, f32[16,256]{1,0:T(8,128)S(1)}, u32[]{:S(2)}, u32[]{:S(2)}) %collective-permute-start.3) | collective-permute-done | bytes 16416 | tf_op jit(solution)/shard_map/ppermute | solution.py:565
  20.9 0.9 %copy-done.11 = f32[96,256]{1,0:T(8,128)S(1)} copy-done((f32[96,256]{1,0:T(8,128)S(1)}, f32[96,256]{1,0:T(8,128)}, u32[]{:S(2)}) %copy-start.11) | copy-done | bytes 98328
  21.8 0.7 %copy-done.12 = f32[16,256]{1,0:T(8,128)S(1)} copy-done((f32[16,256]{1,0:T(8,128)S(1)}, f32[16,256]{1,0:T(8,128)}, u32[]{:S(2)}) %copy-start.12) | copy-done | bytes 16408
  22.5 0.7 %copy-done.13 = f32[16,256]{1,0:T(8,128)S(1)} copy-done((f32[16,256]{1,0:T(8,128)S(1)}, f32[16,256]{1,0:T(8,128)}, u32[]{:S(2)}) %copy-start.13) | copy-done | bytes 16408
  23.3 0.0 collective-permute-done.1.across_ref
  23.3 0.1 collective-permute-start.4
  23.4 0.6 %collective-permute-start.6 = (f32[288,256]{1,0:T(8,128)}, f32[288,256]{1,0:T(8,128)S(1)}, u32[]{:S(2)}, u32[]{:S(2)}) collective-permute-start(f32[288,256]{1,0:T(8,128)} %get-tuple-element.26.own_ref), channel_id=1, source_target_pairs={{0,2},{1,3},{2,0},{3,1},{4,6},{5,7},{6,4},{7,5},{8,10},{9,11},{10,... | collective-permute-start | bytes 884744 | tf_op jit(solution)/shard_map/ppermute | solution.py:557
  24.0 0.2 collective-permute-start.5
  24.1 1.6 %copy-done.5 = bf16[1024,1024]{1,0:T(8,128)(2,1)S(1)} copy-done((bf16[1024,1024]{1,0:T(8,128)(2,1)S(1)}, bf16[1024,1024]{1,0:T(8,128)(2,1)}, u32[]{:S(2)}) %copy-start.5) | copy-done | bytes 2097176
  25.7 0.9 %copy-done.10 = f32[6,6,1024]{2,1,0:T(8,128)S(1)} copy-done((f32[6,6,1024]{2,1,0:T(8,128)S(1)}, f32[6,6,1024]{2,1,0:T(8,128)}, u32[]{:S(2)}) %copy-start.10) | copy-done | bytes 147480
  26.6 1.2 %fold.1.refs_3_.refs_4_ = f32[36,1024]{1,0:T(8,128)S(1)} custom-call(f32[6,6,1024]{2,1,0:T(8,128)S(1)} %copy-done.10, bf16[1024,1024]{1,0:T(8,128)(2,1)S(1)} %copy-done.5), custom_call_target="tpu_custom_call" | custom-call | flops 226492416 | bytes 2097152 | tf_op jit(solution)/shard_map/fold/pallas_call | solution.py:566
  27.8 0.0 collective-permute-done.core_ref
  27.8 0.0 collective-permute-done.4.both_ref
  27.9 0.0 copy-done.1
  27.9 0.0 copy-done.7
  27.9 0.0 copy-done
  27.9 0.0 copy-done.4
  27.9 5.6 %transform.3 = (f32[128,128]{1,0:T(8,128)S(1)}, f32[6,64,384]{2,1,0:T(8,128)S(1)}, f32[6,64,256]{2,1,0:T(8,128)S(1)}) custom-call(f32[392,256]{1,0:T(8,128)S(1)} %copy-done.6, f32[392,256]{1,0:T(8,128)S(1)} %collective-permute-done.core_ref, f32[392,256]{1,0:T(8,128)} %collective-permute-done.1.across_ref, f32[392,256]{1,0:T(8,128)S(1)} %collective-permute-done.4.both_ref, ...), custom_call_target="tpu_custom_call" | custom-call | flops 1207959552 | bytes 3145728 | tf_op jit(solution)/shard_map/transform/pallas_call | solution.py:511
  33.5 0.0 collective-permute-done.6.across_ref
  33.5 0.4 collective-permute-start.7
  33.9 1.5 %collective-permute-start.9 = (f32[144,256]{1,0:T(8,128)S(1)}, f32[144,256]{1,0:T(8,128)S(1)}, u32[]{:S(2)}, u32[]{:S(2)}) collective-permute-start(f32[144,256]{1,0:T(8,128)S(1)} %ends.1.own_ref), channel_id=1, source_target_pairs={{0,2},{1,3},{2,0},{3,1},{4,6},{5,7},{6,4},{7,5},{8,10},{9,11},{10,... | collective-permute-start | bytes 442376 | tf_op jit(solution)/shard_map/ppermute | solution.py:557
  35.4 0.0 collective-permute-start.8
  35.4 0.0 collective-permute-done.5.core_ref
  35.4 0.0 collective-permute-done.7.both_ref
  35.4 0.0 copy-done.8
  35.4 0.0 copy-start.2
  35.4 3.4 %transform.4 = (f32[6,48,384]{2,1,0:T(8,128)S(1)}, f32[6,48,256]{2,1,0:T(8,128)S(1)}) custom-call(f32[288,256]{1,0:T(8,128)S(1)} %copy-done.8, f32[288,256]{1,0:T(8,128)S(1)} %collective-permute-done.5.core_ref, f32[288,256]{1,0:T(8,128)S(1)} %collective-permute-done.6.across_ref, f32[288,256]{1,0:T(8,128)S(1)} %collective-permute-done.7.both_ref, ...), custom_call_target="tpu_custom_call" | custom-call | flops 905969664 | bytes 2359296 | tf_op jit(solution)/shard_map/transform/pallas_call | solution.py:511
  38.9 0.9 %collective-permute-done.9.across_ref = f32[144,256]{1,0:T(8,128)S(1)} collective-permute-done((f32[144,256]{1,0:T(8,128)S(1)}, f32[144,256]{1,0:T(8,128)S(1)}, u32[]{:S(2)}, u32[]{:S(2)}) %collective-permute-start.9) | collective-permute-done | bytes 147488 | tf_op jit(solution)/shard_map/ppermute | solution.py:557
  39.8 0.0 collective-permute-start.10
  39.8 0.9 %middle.1 = (f32[6,96,256]{2,1,0:T(8,128)S(1)}, f32[40,256]{1,0:T(8,128)S(1)}) custom-call(f32[6,128,256]{2,1,0:T(8,128)S(1)} %bitcast.13, s32[128,256]{1,0:T(8,128)S(1)} %copy-done.4, f32[128,128]{1,0:T(8,128)S(1)} %copy-done.9, f32[128,128]{1,0:T(8,128)S(1)} %get-tuple-element.31.refs_0_.edge_ref, f32[6,64,384]{2,1,0:T(8,128)S(1)} %get-tuple-element.32.p0_ref, ...), custom_call_target="tpu_custom_call" | custom-call | flops 5898240 | bytes 3145728 | tf_op jit(solution)/shard_map/middle/pallas_call | solution.py:586
  40.7 0.0 collective-permute-done.8.core_ref
  40.7 0.5 collective-permute-done.10.both_ref
  41.2 1.3 %transform.5 = (f32[6,24,384]{2,1,0:T(8,128)S(1)}, f32[6,16,256]{2,1,0:T(8,128)S(1)}) custom-call(f32[144,256]{1,0:T(8,128)S(1)} %ends.1.own_ref, f32[144,256]{1,0:T(8,128)S(1)} %collective-permute-done.8.core_ref, f32[144,256]{1,0:T(8,128)S(1)} %collective-permute-done.9.across_ref, f32[144,256]{1,0:T(8,128)S(1)} %collective-permute-done.10.both_ref, ...), custom_call_target="tpu_custom_call" | custom-call | flops 452984832 | bytes 1179648 | tf_op jit(solution)/shard_map/transform/pallas_call | solution.py:511
  42.5 0.0 copy-start.3
  42.5 0.4 outer.1
  43.0 12.8 %all_to_all.11 = f32[32,1,128]{2,1,0:T(1,128)S(1)} all-to-all(f32[32,1,128]{2,1,0:T(1,128)S(1)} %bitcast.19), channel_id=1, replica_groups=mesh['ax'=8,'sec'=4] {'ax','sec'}, dimensions={0} | all-to-all | bytes 32768 | tf_op jit(solution)/shard_map/all_to_all | solution.py:597
  55.7 1.3 %update.1 = (f32[6,128,256]{2,1,0:T(8,128)}, f32[6,128,256]{2,1,0:T(8,128)}, f32[1,3]{1,0:T(1,128)}) custom-call(f32[6,128,256]{2,1,0:T(8,128)S(1)} %bitcast.17, f32[6,96,256]{2,1,0:T(8,128)S(1)} %get-tuple-element.37.middle_ref, f32[6,32,256]{2,1,0:T(8,128)S(1)} %get-tuple-element.42.outer_ref, f32[32,128]{1,0:T(8,128)S(1)} %bitcast.18, ...), custom_call_target="tpu_custom_call" | custom-call | flops 786432 | bytes 4718592 | tf_op jit(solution)/shard_map/update/pallas_call | solution.py:598
  (13 shorter events, 0.1 us)
Async XLA Ops:
  4.6 11.8 %copy-start.6 = (f32[392,256]{1,0:T(8,128)S(1)}, f32[392,256]{1,0:T(8,128)}, u32[]{:S(2)}) copy-start(f32[392,256]{1,0:T(8,128)} %first.1.own_ref) | copy-start | bytes 1204228
  4.6 18.7 %collective-permute-start.1 = (f32[392,256]{1,0:T(8,128)}, f32[392,256]{1,0:T(8,128)}, u32[]{:S(2)}, u32[]{:S(2)}) collective-permute-start(f32[392,256]{1,0:T(8,128)} %first.1.own_ref), channel_id=1, source_target_pairs={{0,2},{1,3},{2,0},{3,1},{4,6},{5,7},{6,4},{7,5},{8,10},{9,11},{10,... | collective-permute-start | bytes 1204232 | tf_op jit(solution)/shard_map/ppermute | solution.py:557
  7.6 20.2 %copy-start.1 = (bf16[3072,256]{1,0:T(8,128)(2,1)S(1)}, bf16[3072,256]{1,0:T(8,128)(2,1)}, u32[]{:S(2)}) copy-start(bf16[3072,256]{1,0:T(8,128)(2,1)} %constant.9.clone.refs_0_.refs_1_) | copy-start | bytes 4718596
  7.6 20.2 %copy-start.7 = (f32[8,1024]{1,0:T(8,128)S(1)}, f32[8,1024]{1,0:T(8,128)}, u32[]{:S(2)}) copy-start(f32[8,1024]{1,0:T(8,128)} %constant.11.clone.refs_2_.refs_3_) | copy-start | bytes 98308
  11.5 16.4 %copy-start = (bf16[3072,256]{1,0:T(8,128)(2,1)S(1)}, bf16[3072,256]{1,0:T(8,128)(2,1)}, u32[]{:S(2)}) copy-start(bf16[3072,256]{1,0:T(8,128)(2,1)} %constant.10.clone.refs_1_.refs_2_) | copy-start | bytes 4718596
  11.5 16.3 %copy-start.4 = (s32[128,256]{1,0:T(8,128)S(1)}, s32[128,256]{1,0:T(8,128)}, u32[]{:S(2)}) copy-start(s32[128,256]{1,0:T(8,128)} %hole_ref.7) | copy-start | bytes 393220
  11.6 5.2 %collective-permute-start.2 = (f32[16,256]{1,0:T(8,128)}, f32[16,256]{1,0:T(8,128)S(1)}, u32[]{:S(2)}, u32[]{:S(2)}) collective-permute-start(f32[16,256]{1,0:T(8,128)} %get-tuple-element.28.up_ref), channel_id=1, source_target_pairs={{0,4},{4,8},{8,12},{12,16},{16,20},{20,24},{24,28},{1,5},{5,9},{9,... | collective-permute-start | bytes 49160 | tf_op jit(solution)/shard_map/ppermute | solution.py:564
  15.1 5.8 %collective-permute-start.3 = (f32[16,256]{1,0:T(8,128)}, f32[16,256]{1,0:T(8,128)S(1)}, u32[]{:S(2)}, u32[]{:S(2)}) collective-permute-start(f32[16,256]{1,0:T(8,128)} %get-tuple-element.29.down_ref), channel_id=1, source_target_pairs={{4,0},{8,4},{12,8},{16,12},{20,16},{24,20},{28,24},{5,1},{9,5},{13... | collective-permute-start | bytes 49160 | tf_op jit(solution)/shard_map/ppermute | solution.py:565
  16.4 11.4 %collective-permute-start = (f32[392,256]{1,0:T(8,128)S(1)}, f32[392,256]{1,0:T(8,128)S(1)}, u32[]{:S(2)}, u32[]{:S(2)}) collective-permute-start(f32[392,256]{1,0:T(8,128)S(1)} %copy-done.6), channel_id=1, source_target_pairs={{0,1},{1,0},{2,3},{3,2},{4,5},{5,4},{6,7},{7,6},{8,9},{9,8},{10,11... | collective-permute-start | bytes 1204232 | tf_op jit(solution)/shard_map/ppermute | solution.py:560
  20.9 0.9 %copy-start.11 = (f32[96,256]{1,0:T(8,128)S(1)}, f32[96,256]{1,0:T(8,128)}, u32[]{:S(2)}) copy-start(f32[96,256]{1,0:T(8,128)} %get-tuple-element.27.ends_ref) | copy-start | bytes 294916
  21.8 0.7 %copy-start.12 = (f32[16,256]{1,0:T(8,128)S(1)}, f32[16,256]{1,0:T(8,128)}, u32[]{:S(2)}) copy-start(f32[16,256]{1,0:T(8,128)} %get-tuple-element.28.up_ref) | copy-start | bytes 49156
  22.5 0.7 %copy-start.13 = (f32[16,256]{1,0:T(8,128)S(1)}, f32[16,256]{1,0:T(8,128)}, u32[]{:S(2)}) copy-start(f32[16,256]{1,0:T(8,128)} %get-tuple-element.29.down_ref) | copy-start | bytes 49156
  23.3 4.5 %collective-permute-start.4 = (f32[392,256]{1,0:T(8,128)}, f32[392,256]{1,0:T(8,128)S(1)}, u32[]{:S(2)}, u32[]{:S(2)}) collective-permute-start(f32[392,256]{1,0:T(8,128)} %collective-permute-done.1.across_ref), channel_id=1, source_target_pairs={{0,1},{1,0},{2,3},{3,2},{4,5},{5,4},{6,7},{7,6},{8,9},{9,8},{10,11... | collective-permute-start | bytes 1204232 | tf_op jit(solution)/shard_map/ppermute | solution.py:560
  23.4 10.1 %collective-permute-start.6 = (f32[288,256]{1,0:T(8,128)}, f32[288,256]{1,0:T(8,128)S(1)}, u32[]{:S(2)}, u32[]{:S(2)}) collective-permute-start(f32[288,256]{1,0:T(8,128)} %get-tuple-element.26.own_ref), channel_id=1, source_target_pairs={{0,2},{1,3},{2,0},{3,1},{4,6},{5,7},{6,4},{7,5},{8,10},{9,11},{10,... | collective-permute-start | bytes 884744 | tf_op jit(solution)/shard_map/ppermute | solution.py:557
  24.0 11.4 %collective-permute-start.5 = (f32[288,256]{1,0:T(8,128)}, f32[288,256]{1,0:T(8,128)S(1)}, u32[]{:S(2)}, u32[]{:S(2)}) collective-permute-start(f32[288,256]{1,0:T(8,128)} %get-tuple-element.26.own_ref), channel_id=1, source_target_pairs={{0,1},{1,0},{2,3},{3,2},{4,5},{5,4},{6,7},{7,6},{8,9},{9,8},{10,11... | collective-permute-start | bytes 884744 | tf_op jit(solution)/shard_map/ppermute | solution.py:560
  24.1 1.6 %copy-start.5 = (bf16[1024,1024]{1,0:T(8,128)(2,1)S(1)}, bf16[1024,1024]{1,0:T(8,128)(2,1)}, u32[]{:S(2)}) copy-start(bf16[1024,1024]{1,0:T(8,128)(2,1)} %constant.8.clone.fold_ref) | copy-start | bytes 6291460
  25.7 0.9 %copy-start.10 = (f32[6,6,1024]{2,1,0:T(8,128)S(1)}, f32[6,6,1024]{2,1,0:T(8,128)}, u32[]{:S(2)}) copy-start(f32[6,6,1024]{2,1,0:T(8,128)} %precond_ref.1) | copy-start | bytes 442372
  27.8 7.6 %copy-start.8 = (f32[288,256]{1,0:T(8,128)S(1)}, f32[288,256]{1,0:T(8,128)}, u32[]{:S(2)}) copy-start(f32[288,256]{1,0:T(8,128)} %get-tuple-element.26.own_ref) | copy-start | bytes 884740
  33.5 1.9 %collective-permute-start.7 = (f32[288,256]{1,0:T(8,128)S(1)}, f32[288,256]{1,0:T(8,128)S(1)}, u32[]{:S(2)}, u32[]{:S(2)}) collective-permute-start(f32[288,256]{1,0:T(8,128)S(1)} %collective-permute-done.6.across_ref), channel_id=1, source_target_pairs={{0,1},{1,0},{2,3},{3,2},{4,5},{5,4},{6,7},{7,6},{8,9},{9,8},{10,11... | collective-permute-start | bytes 884744 | tf_op jit(solution)/shard_map/ppermute | solution.py:560
  33.9 5.9 %collective-permute-start.9 = (f32[144,256]{1,0:T(8,128)S(1)}, f32[144,256]{1,0:T(8,128)S(1)}, u32[]{:S(2)}, u32[]{:S(2)}) collective-permute-start(f32[144,256]{1,0:T(8,128)S(1)} %ends.1.own_ref), channel_id=1, source_target_pairs={{0,2},{1,3},{2,0},{3,1},{4,6},{5,7},{6,4},{7,5},{8,10},{9,11},{10,... | collective-permute-start | bytes 442376 | tf_op jit(solution)/shard_map/ppermute | solution.py:557
  35.4 5.3 %collective-permute-start.8 = (f32[144,256]{1,0:T(8,128)S(1)}, f32[144,256]{1,0:T(8,128)S(1)}, u32[]{:S(2)}, u32[]{:S(2)}) collective-permute-start(f32[144,256]{1,0:T(8,128)S(1)} %ends.1.own_ref), channel_id=1, source_target_pairs={{0,1},{1,0},{2,3},{3,2},{4,5},{5,4},{6,7},{7,6},{8,9},{9,8},{10,11... | collective-permute-start | bytes 442376 | tf_op jit(solution)/shard_map/ppermute | solution.py:560
  35.4 4.4 %copy-start.2 = (f32[128,6,256]{2,0,1:T(8,128)S(1)}, f32[128,6,256]{2,0,1:T(8,128)}, u32[]{:S(2)}) copy-start(f32[128,6,256]{2,0,1:T(8,128)} %param.13) | copy-start | bytes 2359300
  35.4 4.4 %copy-start.9 = (f32[128,128]{1,0:T(8,128)S(1)}, f32[128,128]{1,0:T(8,128)}, u32[]{:S(2)}) copy-start(f32[128,128]{1,0:T(8,128)} %get-tuple-element.25.factor_ref) | copy-start | bytes 196612
  39.8 1.4 %collective-permute-start.10 = (f32[144,256]{1,0:T(8,128)S(1)}, f32[144,256]{1,0:T(8,128)S(1)}, u32[]{:S(2)}, u32[]{:S(2)}) collective-permute-start(f32[144,256]{1,0:T(8,128)S(1)} %collective-permute-done.9.across_ref), channel_id=1, source_target_pairs={{0,1},{1,0},{2,3},{3,2},{4,5},{5,4},{6,7},{7,6},{8,9},{9,8},{10,11... | collective-permute-start | bytes 442376 | tf_op jit(solution)/shard_map/ppermute | solution.py:560
  42.5 13.2 %copy-start.3 = (f32[128,6,256]{2,0,1:T(8,128)S(1)}, f32[128,6,256]{2,0,1:T(8,128)}, u32[]{:S(2)}) copy-start(f32[128,6,256]{2,0,1:T(8,128)} %param.12) | copy-start | bytes 2359300

commit v3 on v2

v3 whole, which is shorter than its diff:
```python
import functools

import jax
import jax.numpy as jnp
import ml_dtypes
import numpy as np
from jax import lax
from jax.experimental import pallas as pl
from jax.experimental.pallas import tpu as pltpu
from jax.sharding import PartitionSpec as P

F32 = jnp.float32
BF16 = jnp.bfloat16
SECTORS = 4
TILE = 8
LANES = 128


def three_terms(table):
    high = table.astype(ml_dtypes.bfloat16)
    low = (table - high.astype(np.float64)).astype(ml_dtypes.bfloat16)
    return np.concatenate([high, high, low], axis=0)


@functools.lru_cache(maxsize=None)
def harmonic_tables(width):
    around = SECTORS * width
    half = width // 2
    zero = [("c", 4 * q) for q in range(half + 1)] + [("s", 4 * q) for q in range(1, half)]
    two = [(f, 4 * q + 2) for f in "cs" for q in range(half)]
    one = [(f, 8 * q + 1) for f in "cs" for q in range(half)]
    five = [(f, 8 * q + 5) for f in "cs" for q in range(half)]
    columns = zero + two + one + five
    harmonic = np.array([k for _, k in columns], dtype=np.int64)
    is_sin = np.array([f == "s" for f, _ in columns])

    def wave(place, shift):
        angle = 2.0 * np.pi / around * ((place[:, None] * harmonic[None, :]) % around)
        return np.cos(angle - shift)

    place = np.arange(width)
    shift = np.where(is_sin, np.pi / 2, 0.0)[None, :]
    direct = wave(place, shift)
    turned = np.concatenate([direct[:half], wave(place[:half], shift - np.pi / 2)], axis=0)
    forward = [direct[:, :width], direct[:, width : 2 * width]]
    forward += [turned[:, 2 * width : 3 * width], turned[:, 3 * width :]]
    beyond = wave(np.array([around - 1, width]), shift).astype(np.float32)
    beyond = np.repeat(beyond[:, None, :], TILE, axis=1)
    fold = np.zeros((around, 4 * half))
    kinds = [4 * np.arange(half), 4 * np.arange(half) + 2, 8 * np.arange(half) + 1, 8 * np.arange(half) + 5]
    for column, k in enumerate(np.concatenate(kinds)):
        for place in {k, (around - k) % around}:
            fold[place, column] = 1.0 / around
    return (
        np.concatenate([three_terms(t) for t in forward], axis=0),
        three_terms(direct.T),
        beyond,
        fold.astype(ml_dtypes.bfloat16),
    )


def split(x):
    high = x.astype(BF16)
    return high, (x - high.astype(F32)).astype(BF16)


def lanes_of(shape):
    return lax.broadcasted_iota(jnp.int32, shape, len(shape) - 1)


def rows_of(shape):
    return lax.broadcasted_iota(jnp.int32, shape, len(shape) - 2)


def beside_sum(x, before, after):
    lane = lanes_of(x.shape)
    size = x.shape[-1]
    left = jnp.where(lane == 0, before, pltpu.roll(x, 1, x.ndim - 1))
    right = jnp.where(lane == size - 1, after, pltpu.roll(x, size - 1, x.ndim - 1))
    return left + right


def stacked_sum(x, before=0.0, after=0.0):
    row = rows_of(x.shape)
    size = x.shape[0]
    up = jnp.where(row == 0, before, pltpu.roll(x, 1, 0))
    down = jnp.where(row == size - 1, after, pltpu.roll(x, size - 1, 0))
    return up + down


def fold_kernel(precond_ref, fold_ref, out_ref):
    comps = precond_ref.shape[0]
    value = jnp.concatenate([precond_ref[q] for q in range(comps)], axis=0)
    pairs, around = value.shape
    high = value.astype(BF16)
    rest = value - high.astype(F32)
    middle = rest.astype(BF16)
    low = (rest - middle.astype(F32)).astype(BF16)
    terms = [jnp.dot(t, fold_ref[...], preferred_element_type=F32) for t in (high, middle, low)]
    folded = terms[0] + (terms[1] + terms[2])
    half = folded.shape[1] // 4
    zero = folded[:, :half]
    top = value[:, around // 2 : around // 2 + 1] * F32(1.0 / around)
    other = jnp.where(lanes_of(zero.shape) == 0, top, zero)
    folded = jnp.concatenate([zero, other, folded[:, half:]], axis=1)
    for i in range(pairs):
        out_ref[i] = jnp.broadcast_to(folded[i : i + 1], out_ref.shape[1:])


def factor_columns(table_ref, class_ref, ax_size, comps):
    classes = class_ref[...]
    slab = classes.shape[1]
    position = lax.axis_index("ax") * slab + lanes_of(classes.shape)
    taper = 1.0 + 2.0 * position.astype(F32) / F32(ax_size * slab - 1)
    rows = []
    for q in range(comps):
        value = jnp.zeros(classes.shape, F32)
        for kind in range(table_ref.shape[0]):
            value = jnp.where(classes == kind, table_ref[kind, q], value)
        rows.append(value * taper)
    rows.append(jnp.zeros((LANES - comps, slab), F32))
    return jnp.concatenate(rows, axis=0).T


def local_part(q, block, inner, solid, factor, load, stiff, other):
    field = block[inner]
    beside = stacked_sum(block)[inner] + beside_sum(field, 0.0, 0.0)
    stiffness = stiff * factor[:, q : q + 1]
    image = (stiffness + 4.5) * field - beside - 0.5 * other[inner]
    return solid * (load - image)


def edge_rows(fields, solid):
    rows, width = solid.shape
    sources = fields + [solid] * (TILE - len(fields))
    columns = [x[:, :1] for x in sources] + [x[:, width - 1 :] for x in sources]
    table = jnp.concatenate(columns + [jnp.zeros((rows, LANES - 2 * TILE), F32)], axis=1)
    if rows < LANES:
        table = jnp.concatenate([table, jnp.zeros((LANES - rows, LANES), F32)], axis=0)
    table = table.T
    return table[:TILE], table[TILE : 2 * TILE]


def first_kernel(
    cuts, comps, ax_size, table_ref, class_ref, load_ref, disp_ref, stiff_ref, hole_ref,
    first_ref, ends_ref, factor_ref, up_ref, down_ref,
    table_in, class_in, load_in, disp_in, stiff_in, hole_in, first_out, ends_out, factor_out, up_out, down_out,
    in_sems, out_sems,
):
    slab, width = hole_ref.shape
    a, b, c = cuts
    top, bottom = b + TILE, slab - c + TILE

    def copy(src, dst, sems, i):
        moving = pltpu.make_async_copy(src, dst, sems.at[i])
        moving.start()
        return moving

    def two(src, dst, i):
        return [
            copy(src.at[pl.ds(0, top)], dst.at[pl.ds(0, top)], in_sems, i),
            copy(src.at[pl.ds(slab - bottom, bottom)], dst.at[pl.ds(top, bottom)], in_sems, i + 1),
        ]

    small = [copy(class_ref, class_in, in_sems, 0), copy(table_ref, table_in, in_sems, 1)]
    hole_moving = two(hole_ref, hole_in, 2)
    moving = []
    for q in range(comps):
        moving.append([])
        for k, (src, dst) in enumerate(((disp_ref, disp_in), (load_ref, load_in), (stiff_ref, stiff_in))):
            moving[q] += two(src.at[q], dst.at[q], 4 + 6 * q + 2 * k)
    for one in small:
        one.wait()
    factor_out[...] = factor_columns(table_in, class_in, ax_size, comps)
    leaving = [copy(factor_out, factor_ref, out_sems, 0)]
    for one in hole_moving:
        one.wait()
    solid = (1 - hole_in[...]).astype(F32)
    factor = factor_out[...]
    ends = a + slab - c
    stride = b - a
    for q in range(comps):
        if q % 2 == 0:
            for one in moving[q] + moving[q + 1]:
                one.wait()
        high = disp_in[q, :top]
        low = disp_in[q, top:]
        upper = local_part(
            q, high, slice(0, b), solid[:b], factor[:b], load_in[q, :b], stiff_in[q, :b], disp_in[q ^ 1, :top]
        )
        lower = local_part(
            q, low, slice(TILE, bottom), solid[top + TILE :], factor[c:],
            load_in[q, top + TILE :], stiff_in[q, top + TILE :], disp_in[q ^ 1, top:],
        )
        first_out[pl.ds(q * stride, stride), :] = upper[a:]
        leaving.append(
            copy(first_out.at[pl.ds(q * stride, stride)], first_ref.at[pl.ds(q * stride, stride)], out_sems, 1 + q)
        )
        ends_out[pl.ds(q * ends, a), :] = upper[:a]
        ends_out[pl.ds(q * ends + a, slab - c), :] = lower
        up_out[q : q + 1, :] = lower[slab - c - 1 :]
        down_out[q : q + 1, :] = upper[:1]
        up_out[TILE + q : TILE + q + 1, :] = low[bottom - 1 :]
        down_out[TILE + q : TILE + q + 1, :] = high[:1]
    spare = TILE - comps
    for ref, row in ((up_out, top + bottom - 1), (down_out, 0)):
        ref[comps:TILE, :] = jnp.broadcast_to(solid[row : row + 1], (spare, width))
        ref[TILE + comps :, :] = jnp.zeros((spare, width), F32)
    leaving.append(copy(up_out, up_ref, out_sems, 1 + comps))
    leaving.append(copy(down_out, down_ref, out_sems, 2 + comps))

    def chosen(x):
        return jnp.concatenate([x[a:b], x[:a], x[top + TILE :]], axis=0)

    left, right = edge_rows([chosen(disp_in[q]) for q in range(comps)], chosen(solid))
    first_out[pl.ds(comps * stride, TILE), :] = jnp.concatenate([left, right], axis=1)
    left, right = [pltpu.roll(x, LANES - stride, 1) for x in (left, right)]
    ends_out[pl.ds(comps * ends, TILE), :] = jnp.concatenate([left, right], axis=1)
    tail = pl.ds(comps * stride, TILE)
    leaving.append(copy(first_out.at[tail], first_ref.at[tail], out_sems, 3 + comps))
    leaving.append(copy(ends_out, ends_ref, out_sems, 4 + comps))
    for one in leaving:
        one.wait()


def second_kernel(cuts, comps, load_ref, disp_ref, stiff_ref, hole_ref, factor_ref, second_ref):
    _, b, c = cuts
    solid = (1 - hole_ref[b:c]).astype(F32)
    factor = factor_ref[b:c]
    rows = c - b
    around = slice(b - TILE, c + TILE)
    for q in range(comps):
        second_ref[pl.ds(q * rows, rows), :] = local_part(
            q, disp_ref[q, around], slice(TILE, TILE + rows), solid, factor,
            load_ref[q, b:c], stiff_ref[q, b:c], disp_ref[q ^ 1, around],
        )
    left, right = edge_rows([disp_ref[q, b:c] for q in range(comps)], solid)
    second_ref[pl.ds(comps * rows, TILE), :] = jnp.concatenate([left, right], axis=1)


def ends_kernel(comps, ends_ref, up_ref, down_ref, before_ref, after_ref, out_ref):
    rows = (ends_ref.shape[0] - TILE) // comps
    width = ends_ref.shape[1]
    row = rows_of((rows, width))
    spare = rows_of((TILE, width))
    solid_before = before_ref[comps : comps + 1]
    solid_after = after_ref[comps : comps + 1]
    for q in range(comps):
        disp_before = before_ref[TILE + q : TILE + q + 1]
        disp_after = after_ref[TILE + q : TILE + q + 1]
        part = ends_ref[pl.ds(q * rows, rows), :]
        part = part + jnp.where(row == 0, down_ref[comps : comps + 1] * disp_before, 0.0)
        part = part + jnp.where(row == rows - 1, up_ref[comps : comps + 1] * disp_after, 0.0)
        out_ref[pl.ds(q * (rows + TILE), rows), :] = part
        res_before = before_ref[q : q + 1] + solid_before * down_ref[TILE + q : TILE + q + 1]
        res_after = after_ref[q : q + 1] + solid_after * up_ref[TILE + q : TILE + q + 1]
        beyond = jnp.zeros((TILE, width), F32)
        for i, value in enumerate((res_before, res_after, disp_before, disp_after, solid_before, solid_after)):
            beyond = jnp.where(spare == i, value, beyond)
        out_ref[pl.ds(q * (rows + TILE) + rows, TILE), :] = beyond
    out_ref[pl.ds(comps * (rows + TILE), TILE), :] = ends_ref[pl.ds(comps * rows, TILE), :]


def in_order(odd, own, core, across, both):
    return own, jnp.where(odd, both, core), across, jnp.where(odd, core, both)


def butterfly(x0, x1, x2, x3):
    even, other = x0 + x2, x1 + x3
    return even + other, even - other, x0 - x2, x1 - x3


def edge_table(odd, blocks):
    tiles = in_order(odd, *blocks)
    left = [t[:, :LANES] for t in tiles]
    right = [t[:, LANES:] for t in tiles]
    solid = TILE - 1
    at_left = [left[s][solid:] * right[s - 1] for s in range(SECTORS)]
    at_right = [right[s][solid:] * left[(s + 1) % SECTORS] for s in range(SECTORS)]
    stack = []
    for one, other in zip(butterfly(*at_left), butterfly(*at_right)):
        stack += [one, other]
    stack += [at_left[0], at_right[0], right[3], left[1]]
    stack.append(jnp.zeros((LANES - len(stack) * TILE, LANES), F32))
    return jnp.concatenate(stack, axis=0).T


def transform_kernel(
    comps, rows_at, spare, own_ref, core_ref, across_ref, both_ref,
    forward_ref, inverse_ref, beyond_ref, weight_ref, hole_ref,
    prec_ref, residual_ref, left_ref, spectrum_ref, scaled_ref, halo_ref,
):
    width = own_ref.shape[1]
    half = width // 2
    odd = lax.axis_index("sec") % 2 == 1
    sign = jnp.where(odd, -1.0, 1.0)
    main = sum(size for _, size in rows_at)
    rows = main + spare
    total = comps * rows
    group = 1 if rows % 16 == 0 else 2
    sources = (own_ref, core_ref, across_ref, both_ref)
    solid = jnp.concatenate([(1 - hole_ref[pl.ds(at, size)]).astype(F32) for at, size in rows_at], axis=0)
    edge = edge_table(odd, [r[total : total + TILE] for r in sources])[:main]
    lane = lanes_of((main, LANES))
    first = lane == 0
    last = lane == LANES - 1

    def with_edges(x, array, q):
        column = array * 2 * TILE + q
        head = x[:, :LANES] + jnp.where(first, edge[:, column : column + 1], 0.0)
        tail = x[:, -LANES:] + jnp.where(last, edge[:, column + TILE : column + TILE + 1], 0.0)
        middle = [x[:, LANES:-LANES]] if width > 2 * LANES else []
        return jnp.concatenate([head] + middle + [tail], axis=1)

    def arrays_of(q):
        at = q * rows
        own, core, across, both = [r[pl.ds(at, main), :] for r in sources]
        arrays = butterfly(own, core, across, both)
        arrays = arrays[:3] + (sign * arrays[3],)
        arrays = [with_edges(x, i, q) for i, x in enumerate(arrays)]
        residual_ref[q] = with_edges(own, 4, q)
        mask = None
        if spare:
            tiles = in_order(odd, *[r[pl.ds(at + main, spare), :] for r in sources])
            disp = [pltpu.roll(t, spare - 2, 0) for t in tiles]
            holes = [pltpu.roll(t, spare - 4, 0) for t in tiles]
            place = lanes_of((spare, width))
            fixed = []
            for s in range(SECTORS):
                beside = jnp.where(place == 0, pltpu.roll(disp[s - 1], 1, 1), 0.0)
                beside = beside + jnp.where(
                    place == width - 1, pltpu.roll(disp[(s + 1) % SECTORS], width - 1, 1), 0.0
                )
                value = tiles[s] + holes[s] * beside
                fixed.append(jnp.where(rows_of((spare, width)) < 2, value, 0.0))
            mask = holes[0]
            arrays = [jnp.concatenate(pair, axis=0) for pair in zip(arrays, butterfly(*fixed))]
        y0, y2, real, imag = arrays
        turned_real = (real[:, half:] - imag[:, half:]) * F32(np.sqrt(0.5))
        turned_imag = (real[:, half:] + imag[:, half:]) * F32(np.sqrt(0.5))
        plus = jnp.concatenate([real[:, :half] + turned_real, imag[:, :half] + turned_imag], axis=1)
        minus = jnp.concatenate([real[:, :half] - turned_real, imag[:, :half] - turned_imag], axis=1)
        return (y0, y2, plus, minus), mask

    beyond_solid = jnp.where(first, edge[:, 11 * TILE - 1 : 11 * TILE], edge[:, 12 * TILE - 1 : 12 * TILE])
    masks = []
    for start in range(0, comps, group):
        found = [arrays_of(q) for q in range(start, start + group)]
        masks += [mask for _, mask in found]
        at = pl.ds(start * rows, group * rows)
        for i in range(4):
            high, low = split(jnp.concatenate([arrays[i] for arrays, _ in found], axis=0))
            left_ref[at, 2 * i * width : (2 * i + 1) * width] = high
            left_ref[at, (2 * i + 1) * width : (2 * i + 2) * width] = low

    for i in range(4):
        high = left_ref[:, 2 * i * width : (2 * i + 1) * width]
        low = left_ref[:, (2 * i + 1) * width : (2 * i + 2) * width]
        part = jnp.dot(
            jnp.concatenate([high, low, high], axis=1),
            forward_ref[pl.ds(3 * i * width, 3 * width), :],
            preferred_element_type=F32,
        )
        spectrum_ref[:, :, i * width : (i + 1) * width] = part.reshape(total // TILE, TILE, width)

    around = SECTORS * width

    def scale(row, count):
        tiles = count // TILE

        def spectrum(p, lanes):
            return spectrum_ref[pl.ds((p * rows + row) // TILE, tiles), :, lanes]

        for start in range(0, comps, group):
            halo = [[None, None] for _ in range(group)]
            for k in range(4):
                for h in range(2):
                    lanes = slice(k * width + h * half, k * width + (h + 1) * half)
                    kind = h if k == 0 else k + 1
                    values = []
                    for i in range(group):
                        value = None
                        for p in range(comps):
                            weight = weight_ref[(start + i) * comps + p, :, kind * half : (kind + 1) * half]
                            term = spectrum(p, lanes) * weight
                            value = term if value is None else value + term
                        for side in range(2):
                            term = value * beyond_ref[side, :, lanes]
                            halo[i][side] = term if halo[i][side] is None else halo[i][side] + term
                        values.append(value.reshape(count, half))
                    high, low = split(values[0] if group == 1 else jnp.concatenate(values, axis=0))
                    at = pl.ds(start * rows + row, group * count)
                    scaled_ref[at, lanes] = high
                    scaled_ref[at, around + lanes.start : around + lanes.stop] = low
            for i in range(group):
                before, after = [jnp.sum(x, axis=2, keepdims=True) for x in halo[i]]
                tile = jnp.where(lanes_of((tiles, TILE, LANES)) == 0, before, after)
                halo_ref[pl.ds((start + i) * rows + row, count), :] = tile.reshape(count, LANES)

    step = rows if group > 1 else 32
    for row in range(0, rows, step):
        scale(row, min(step, rows - row))
    high = scaled_ref[:, :around]
    result = jnp.dot(
        jnp.concatenate([high, scaled_ref[:, around:], high], axis=1),
        inverse_ref[...],
        preferred_element_type=F32,
    )
    for q in range(comps):
        at = q * rows
        prec_ref[q, :main, :width] = result[at : at + main] * solid
        side = halo_ref[pl.ds(at, rows), :]
        prec_ref[q, :main, width:] = side[:main] * beyond_solid
        if spare:
            prec_ref[q, main:, :width] = result[at + main : at + rows] * masks[q]
            prec_ref[q, main:, width:] = side[main:]


def image_rows(q, fields, tile, stiff, solid, factor, before, after, inner):
    field = fields[q][inner]
    beside = beside_sum(field, tile[:, :1], tile[:, 1:2])
    beside = beside + stacked_sum(fields[q], before, after)[inner]
    stiffness = stiff * factor[:, q : q + 1]
    return field, solid * ((stiffness + 4.5) * field - beside - 0.5 * fields[q ^ 1][inner])


def add_sums(sums, residual, field, image):
    rows, width = field.shape
    pairs = ((residual, field), (field, image), (residual, residual), (residual, image), (image, image))
    return [
        total + jnp.sum((x * y).reshape(rows // TILE, TILE, width), axis=0)
        for total, (x, y) in zip(sums, pairs)
    ]


def early_kernel(
    cuts, comps, stiff_ref, hole_ref, factor_ref, p0_ref, p1_ref, r0_ref, r1_ref, image_ref, sums_ref,
):
    slab, width = hole_ref.shape
    a, b, c = cuts
    high = b - TILE
    spare = a + slab - c
    own, side = slice(0, width), slice(width, width + LANES)
    fields = [jnp.concatenate([p1_ref[q, :a, own], p0_ref[q, :, own]], axis=0) for q in range(comps)]
    solid = (1 - hole_ref[:high]).astype(F32)
    factor = factor_ref[:high]
    sums = [jnp.zeros((TILE, width), F32) for _ in range(5)]
    for q in range(comps):
        tile = jnp.concatenate([p1_ref[q, :a, side], p0_ref[q, :-TILE, side]], axis=0)
        field, image = image_rows(
            q, fields, tile, stiff_ref[q, :high], solid, factor, p1_ref[q, spare : spare + 1, own], 0.0, slice(0, high)
        )
        image_ref[q] = image
        residual = jnp.concatenate([r1_ref[q, :a], r0_ref[q, :-TILE]], axis=0)
        sums = add_sums(sums, residual, field, image)
    for i, total in enumerate(sums):
        sums_ref[pl.ds(i * TILE, TILE), :] = total


def late_kernel(
    cuts, comps, stiff_ref, hole_ref, factor_ref, p0_ref, p1_ref, p2_ref,
    r0_ref, r1_ref, r2_ref, partial_ref, image_ref, sums_ref,
):
    slab, width = hole_ref.shape
    a, b, c = cuts
    low = b - TILE
    spare = a + slab - c
    own, side = slice(0, width), slice(width, width + LANES)
    sums = [partial_ref[pl.ds(i * TILE, TILE), :] for i in range(5)]
    fields = [
        jnp.concatenate([p0_ref[q, -2 * TILE :, own], p2_ref[q, :, own], p1_ref[q, a:spare, own]], axis=0)
        for q in range(comps)
    ]
    solid = (1 - hole_ref[low:]).astype(F32)
    factor = factor_ref[low:]
    for q in range(comps):
        tile = jnp.concatenate([p0_ref[q, -TILE:, side], p2_ref[q, :, side], p1_ref[q, a:spare, side]], axis=0)
        field, image = image_rows(
            q, fields, tile, stiff_ref[q, low:], solid, factor,
            0.0, p1_ref[q, spare + 1 : spare + 2, own], slice(TILE, None),
        )
        image_ref[q] = image
        residual = jnp.concatenate([r0_ref[q, -TILE:], r2_ref[q], r1_ref[q, a:]], axis=0)
        sums = add_sums(sums, residual, field, image)
    row = jnp.zeros((1, LANES), F32)
    spot = lanes_of((1, LANES))
    for i, value in enumerate(sums):
        value = jnp.sum(jnp.sum(value, axis=0, keepdims=True), axis=1, keepdims=True)
        row = jnp.where(spot == i, value, row)
    sums_ref[...] = jnp.broadcast_to(row, sums_ref.shape)


def update_kernel(
    cuts, comps, cell_total, disp_ref, early_ref, late_ref, gathered_ref,
    p0_ref, p1_ref, p2_ref, r0_ref, r1_ref, r2_ref, disp_out, residual_out, stats_out,
):
    slab, width = disp_ref.shape[1:]
    a, b, c = cuts
    values = jnp.sum(gathered_ref[...], axis=0, keepdims=True) * F32(1.0 / cell_total)
    rz, zq, rr, ri, ii = [values[:, i : i + 1] for i in range(5)]
    alpha = rz / zq
    square = rr + alpha * (alpha * ii - 2.0 * ri)
    stats_out[...] = jnp.concatenate([rz, zq, square], axis=1)
    low = b - TILE
    pieces = (
        (slice(0, a), p1_ref, r1_ref, slice(0, a)),
        (slice(a, b), p0_ref, r0_ref, slice(0, b - a)),
        (slice(b, c), p2_ref, r2_ref, slice(0, c - b)),
        (slice(c, slab), p1_ref, r1_ref, slice(a, a + slab - c)),
    )
    for q in range(comps):
        image = jnp.concatenate([early_ref[q], late_ref[q]], axis=0)
        for here, prec, residual, there in pieces:
            disp_out[q, here] = disp_ref[q, here] + alpha * prec[q, there, :width]
            residual_out[q, here] = residual[q, there] - alpha * image[here]


VMEM = pl.BlockSpec(memory_space=pltpu.VMEM)
SMEM = pl.BlockSpec(memory_space=pltpu.SMEM)
HBM = pl.BlockSpec(memory_space=pltpu.HBM)
FULL = 62


def call(kernel, name, out_shapes, in_specs, flops, moved, scratch=(), grant=32, out_spec=None):
    return pl.pallas_call(
        kernel,
        out_shape=[jax.ShapeDtypeStruct(s, F32) for s in out_shapes],
        in_specs=in_specs,
        out_specs=[out_spec or VMEM] * len(out_shapes),
        scratch_shapes=list(scratch),
        compiler_params=pltpu.CompilerParams(vmem_limit_bytes=grant * 1024 * 1024),
        cost_estimate=pl.CostEstimate(flops=flops, bytes_accessed=moved, transcendentals=0),
        name=name,
    )


def transform_call(blocks, tables, hole, rows_at, spare, comps, width):
    around = SECTORS * width
    main = sum(size for _, size in rows_at)
    rows = main + spare
    total = comps * rows
    operands = list(blocks) + list(tables) + [hole]
    return call(
        functools.partial(transform_kernel, comps, rows_at, spare), "transform",
        [(comps, rows, width + LANES), (comps, main, width)], [VMEM] * len(operands),
        2 * total * 3 * around * 2 * width, 4 * total * width * 8,
        [pltpu.VMEM((total, 8 * width), BF16), pltpu.VMEM((total // TILE, TILE, around), F32),
         pltpu.VMEM((total, 2 * around), BF16), pltpu.VMEM((total, LANES), F32)],
    )(*operands)


def after_all(x, *others):
    return lax.optimization_barrier((x, *others))[0]


def shards(load, disp, stiff, hole, section_class, class_table, precond):
    slab, comps, width = disp.shape
    ax, sec = lax.axis_size("ax"), lax.axis_size("sec")
    around = width * sec
    cell_total = slab * ax * comps * around
    cuts = (slab // 16, slab // 16 * 11, slab - slab // 16)
    a, b, c = cuts
    ends = a + slab - c
    load, disp, stiff = [x.transpose(1, 0, 2) for x in (load, disp, stiff)]
    forward, inverse, beyond, fold = harmonic_tables(width)
    block = 4 * comps * slab * width
    classes = section_class.reshape(1, slab)

    reach = b + slab - c + 2 * TILE
    shapes = [(comps * (b - a) + TILE, width), (comps * ends + TILE, width), (slab, LANES),
              (2 * TILE, width), (2 * TILE, width)]
    first, edge, factor, up, down = call(
        functools.partial(first_kernel, cuts, comps, ax), "first",
        shapes, [HBM] * 6, 10 * comps * slab * width, 2 * block,
        [pltpu.SMEM(class_table.shape, F32), pltpu.VMEM((1, slab), jnp.int32)]
        + [pltpu.VMEM((comps, reach, width), F32)] * 3 + [pltpu.VMEM((reach, width), jnp.int32)]
        + [pltpu.VMEM(shape, F32) for shape in shapes]
        + [pltpu.SemaphoreType.DMA((4 + 6 * comps,)), pltpu.SemaphoreType.DMA((5 + comps,))],
        FULL, HBM,
    )(class_table, classes, load, disp, stiff, hole)
    (second,) = call(
        functools.partial(second_kernel, cuts, comps), "second",
        [(comps * (c - b) + TILE, width)], [VMEM] * 5, 10 * comps * (c - b) * width, 2 * block,
    )(load, disp, stiff, hole, factor)

    def across(x):
        return lax.ppermute(x, "sec", [(i, i ^ 2) for i in range(sec)])

    def both(x):
        return lax.ppermute(x, "sec", [(i, i ^ 3) for i in range(sec)])

    def beside(x):
        return lax.ppermute(x, "sec", [(i, i ^ 1) for i in range(sec)])

    far0 = across(first)
    before = lax.ppermute(up, "ax", [(i, i + 1) for i in range(ax - 1)])
    after = lax.ppermute(down, "ax", [(i + 1, i) for i in range(ax - 1)])
    (weight,) = call(
        fold_kernel, "fold", [(comps * comps, TILE, 5 * width // 2)], [VMEM] * 2,
        6 * comps * comps * around * around, 2 * around * around,
    )(precond, fold)
    (last,) = call(
        functools.partial(ends_kernel, comps), "ends",
        [(comps * (ends + TILE) + TILE, width)], [VMEM] * 5, comps * ends * width, 8 * comps * ends * width,
    )(edge, up, down, before, after)
    far1 = both(last)
    far2 = across(second)
    tables = (forward, inverse, beyond, weight)

    far0 = after_all(far0, second, last, weight)
    prec0, res0 = transform_call(
        (first, beside(first), far0, beside(far0)), tables, hole, ((a, b - a),), 0, comps, width
    )
    far1 = after_all(far1, prec0)
    prec1, res1 = transform_call(
        (last, beside(last), beside(far1), far1), tables, hole, ((0, a), (c, slab - c)), TILE, comps, width
    )
    far2 = after_all(far2, prec1)
    image, partial = call(
        functools.partial(early_kernel, cuts, comps), "early",
        [(comps, b - TILE, width), (5 * TILE, width)], [VMEM] * 7, 30 * comps * slab * width, 4 * block,
    )(stiff, hole, factor, prec0, prec1, res0, res1)
    prec2, res2 = transform_call(
        (second, beside(second), far2, beside(far2)), tables, hole, ((b, c - b),), 0, comps, width
    )
    image_late, sums = call(
        functools.partial(late_kernel, cuts, comps), "late",
        [(comps, slab - b + TILE, width), (ax * sec, LANES)], [VMEM] * 10, 8 * comps * slab * width, block,
    )(stiff, hole, factor, prec0, prec1, prec2, res0, res1, res2, partial)
    gathered = lax.all_to_all(sums, ("ax", "sec"), 0, 0, tiled=True)
    disp_new, residual_new, stats = call(
        functools.partial(update_kernel, cuts, comps, cell_total), "update",
        [(comps, slab, width), (comps, slab, width), (1, 3)], [VMEM] * 10,
        4 * comps * slab * width, 6 * block,
    )(disp, image, image_late, gathered, prec0, prec1, prec2, res0, res1, res2)
    return disp_new.transpose(1, 0, 2), residual_new.transpose(1, 0, 2), stats.reshape(3)


def solution(mesh):
    in_specs = (
        P("ax", None, "sec"),
        P("ax", None, "sec"),
        P("ax", None, "sec"),
        P("ax", "sec"),
        P("ax"),
        P(),
        P(),
    )
    out_specs = (P("ax", None, "sec"), P("ax", None, "sec"), P())
    return jax.shard_map(shards, mesh=mesh, in_specs=in_specs, out_specs=out_specs, check_vma=False)
```

time: 57.6 us -> 47.8 us (0.83)
  Pallas kernels: 22 us -> 14.2 us
  local copies, waits for them, and re-layouts: 4.89 us -> 2.88 us
    pallas_call x8, Pallas kernels: 20.6 us -> 12.8 us  [the longest x3 7.14 us: transform_call(): call(functools.partial(transform_kernel, comps, rows_at, spare), 'transfo...]
    ppermute x1, waiting for transfers between devices: 4.21 us -> 0.61 us  [shards(): after = lax.ppermute(down, 'ax', [(i + 1, i) for i in range(ax - 1)])]
    ppermute x3, waiting for transfers between devices: 0.95 us -> 3.91 us  [the longest x2 3.91 us: across(): return lax.ppermute(x, 'sec', [(i, i ^ 2) for i in range(sec)])]
    unnamed x28, local copies, waits for them, and re-layouts: 4.89 us -> 2.88 us
    ppermute x6, waiting for transfers between devices: 0.47 us -> 1.68 us  [beside(): return lax.ppermute(x, 'sec', [(i, i ^ 1) for i in range(sec)])]
  transfers between devices with their start and end apart: 11 -> 11, of which waited for: 4 -> 5; matrix products, arithmetic and copies ran while one was open for 0% -> 0% of each run, Pallas kernels for 26% -> 15%
where the time goes in v3:
time: 47.8 us; the launch traced here: 47.5 us
  Pallas kernels  14.2 us (30%)
  blocking collectives  12.9 us (27%)
  starting transfers between devices  10.5 us (22%)
  waiting for transfers between devices  6.2 us (13%)
  local copies, waits for them, and re-layouts  2.88 us (6%)
  between operations  0.85 us (2%)
    all_to_all x1, blocking collectives, shards(): gathered = lax.all_to_all(sums, ('ax', 'sec'), 0, 0, tiled=True)  12.9 us
    pallas_call x3, Pallas kernels, transform_call(): call(functools.partial(transform_kernel, comps, rows_at, spare), 'transfo...  7.14 us
    ppermute x2, waiting for transfers between devices, across(): return lax.ppermute(x, 'sec', [(i, i ^ 2) for i in range(sec)])  3.91 us
    pallas_call x1, Pallas kernels, shards(): call(functools.partial(first_kernel, cuts, comps, ax), 'first', shapes, [...  3.4 us
    ppermute x1, starting transfers between devices, shards(): before = lax.ppermute(up, 'ax', [(i, i + 1) for i in range(ax - 1)])  3.38 us
    ppermute x2, starting transfers between devices, across(): return lax.ppermute(x, 'sec', [(i, i ^ 2) for i in range(sec)])  3.32 us
    unnamed x28, local copies, waits for them, and re-layouts  2.88 us
    ppermute x1, starting transfers between devices, both(): return lax.ppermute(x, 'sec', [(i, i ^ 3) for i in range(sec)])  1.85 us
  transfers between devices with their start and end apart: 11, of which 5 were waited for; matrix products, arithmetic and copies ran while one was open for 0% of the time, Pallas kernels for 15%

profile of v3, /device:TPU:0, one launch (start us, length us, event | category | flops | bytes accessed | tf_op | source)
XLA Modules:
  0.0 47.5 jit_solution(18300888038189203494)
XLA Ops:
  0.6 0.0 copy-start.2
  0.6 0.0 copy-start.3
  0.7 0.0 copy-start.4
  0.7 0.0 copy-start.10
  0.7 3.4 %first.1 = (f32[488,256]{1,0:T(8,128)}, f32[104,256]{1,0:T(8,128)}, f32[128,128]{1,0:T(8,128)}, f32[16,256]{1,0:T(8,128)}, f32[16,256]{1,0:T(8,128)}) custom-call(f32[4,6]{1,0:T(4,128)} %table_ref.1, s32[1,128]{1,0:T(1,128)} %bitcast.22, f32[6,128,256]{2,1,0:T(8,128)} %bitcast.18, f32[6,128,256]{2,1,0:T(8,128)} %bitcast.15, f32[6,128,256]{2,1,0:T(8,128)} %bitcast.11, ...), custom_call_target="tpu_custom_call" | custom-call | flops 1966080 | bytes 1572864 | tf_op jit(solution)/shard_map/first/pallas_call | solution.py:572
  4.1 3.0 %collective-permute-start.1 = (f32[488,256]{1,0:T(8,128)}, f32[488,256]{1,0:T(8,128)S(1)}, u32[]{:S(2)}, u32[]{:S(2)}) collective-permute-start(f32[488,256]{1,0:T(8,128)} %get-tuple-element.25.own_ref), channel_id=1, source_target_pairs={{0,2},{1,3},{2,0},{3,1},{4,6},{5,7},{6,4},{7,5},{8,10},{9,11},{10,... | collective-permute-start | bytes 1499144 | tf_op jit(solution)/shard_map/ppermute | solution.py:587
  7.1 0.0 collective-permute-start
  7.1 3.4 %collective-permute-start.2 = (f32[16,256]{1,0:T(8,128)}, f32[16,256]{1,0:T(8,128)S(1)}, u32[]{:S(2)}, u32[]{:S(2)}) collective-permute-start(f32[16,256]{1,0:T(8,128)} %get-tuple-element.27.up_ref), channel_id=1, source_target_pairs={{0,4},{4,8},{8,12},{12,16},{16,20},{20,24},{24,28},{1,5},{5,9},{9,... | collective-permute-start | bytes 49160 | tf_op jit(solution)/shard_map/ppermute | solution.py:596
  10.5 1.3 %collective-permute-start.3 = (f32[16,256]{1,0:T(8,128)}, f32[16,256]{1,0:T(8,128)S(1)}, u32[]{:S(2)}, u32[]{:S(2)}) collective-permute-start(f32[16,256]{1,0:T(8,128)} %get-tuple-element.28.down_ref), channel_id=1, source_target_pairs={{4,0},{8,4},{12,8},{16,12},{20,16},{24,20},{28,24},{5,1},{9,5},{13... | collective-permute-start | bytes 49160 | tf_op jit(solution)/shard_map/ppermute | solution.py:597
  11.8 0.0 copy-done.2
  11.8 0.0 copy-done.3
  11.8 0.0 copy-done.4
  11.8 0.0 copy-start.5
  11.9 1.1 %copy-done.5 = f32[128,6,256]{2,0,1:T(8,128)S(1)} copy-done((f32[128,6,256]{2,0,1:T(8,128)S(1)}, f32[128,6,256]{2,0,1:T(8,128)}, u32[]{:S(2)}) %copy-start.5) | copy-done | bytes 786456
  13.0 0.8 %copy-done.8 = f32[128,128]{1,0:T(8,128)S(1)} copy-done((f32[128,128]{1,0:T(8,128)S(1)}, f32[128,128]{1,0:T(8,128)}, u32[]{:S(2)}) %copy-start.8) | copy-done | bytes 65560
  13.8 0.0 copy-start.1
  13.8 0.3 second.1.own_ref
  14.2 0.0 copy-done.10
  14.2 0.9 %copy-done.6 = bf16[1024,512]{1,0:T(8,128)(2,1)S(1)} copy-done((bf16[1024,512]{1,0:T(8,128)(2,1)S(1)}, bf16[1024,512]{1,0:T(8,128)(2,1)}, u32[]{:S(2)}) %copy-start.6) | copy-done | bytes 1048600
  15.0 0.7 %fold.1.weight_ref = f32[36,8,640]{2,1,0:T(8,128)S(1)} custom-call(f32[6,6,1024]{2,1,0:T(8,128)S(1)} %copy-done.10, bf16[1024,512]{1,0:T(8,128)(2,1)S(1)} %copy-done.6), custom_call_target="tpu_custom_call" | custom-call | flops 226492416 | bytes 2097152 | tf_op jit(solution)/shard_map/fold/pallas_call | solution.py:598
  15.7 0.0 collective-permute-done.2.before_ref
  15.7 0.6 %collective-permute-done.3.after_ref = f32[16,256]{1,0:T(8,128)S(1)} collective-permute-done((f32[16,256]{1,0:T(8,128)}, f32[16,256]{1,0:T(8,128)S(1)}, u32[]{:S(2)}, u32[]{:S(2)}) %collective-permute-start.3) | collective-permute-done | bytes 16416 | tf_op jit(solution)/shard_map/ppermute | solution.py:597
  16.4 0.0 copy-done.11
  16.4 0.0 copy-done.12
  16.4 0.0 copy-done.13
  16.4 2.3 %collective-permute-done.1.across_ref = f32[488,256]{1,0:T(8,128)S(1)} collective-permute-done((f32[488,256]{1,0:T(8,128)}, f32[488,256]{1,0:T(8,128)S(1)}, u32[]{:S(2)}, u32[]{:S(2)}) %collective-permute-start.1) | collective-permute-done | bytes 499744 | tf_op jit(solution)/shard_map/ppermute | solution.py:587
  18.7 0.0 collective-permute-start.4
  18.7 1.9 %collective-permute-start.6 = (f32[152,256]{1,0:T(8,128)S(1)}, f32[152,256]{1,0:T(8,128)S(1)}, u32[]{:S(2)}, u32[]{:S(2)}) collective-permute-start(f32[152,256]{1,0:T(8,128)S(1)} %ends.1.own_ref), channel_id=1, source_target_pairs={{0,3},{1,2},{2,1},{3,0},{4,7},{5,6},{6,5},{7,4},{8,11},{9,10},{10,... | collective-permute-start | bytes 466952 | tf_op jit(solution)/shard_map/ppermute | solution.py:590
  20.6 0.3 collective-permute-start.9
  20.9 0.0 collective-permute-start.5
  20.9 0.0 collective-permute-done.core_ref
  20.9 0.0 collective-permute-done.4.both_ref
  20.9 4.1 %transform.3 = (f32[6,80,384]{2,1,0:T(8,128)S(1)}, f32[6,80,256]{2,1,0:T(8,128)S(1)}) custom-call(f32[488,256]{1,0:T(8,128)S(1)} %copy-done.9, f32[488,256]{1,0:T(8,128)S(1)} %collective-permute-done.core_ref, f32[488,256]{1,0:T(8,128)S(1)} %collective-permute-done.1.across_ref, f32[488,256]{1,0:T(8,128)S(1)} %collective-permute-done.4.both_ref, ...), custom_call_target="tpu_custom_call" | custom-call | flops 1509949440 | bytes 3932160 | tf_op jit(solution)/shard_map/transform/pallas_call | solution.py:543
  25.0 0.0 collective-permute-done.6.both_ref
  25.0 0.6 %collective-permute-start.7 = (f32[152,256]{1,0:T(8,128)S(1)}, f32[152,256]{1,0:T(8,128)S(1)}, u32[]{:S(2)}, u32[]{:S(2)}) collective-permute-start(f32[152,256]{1,0:T(8,128)S(1)} %collective-permute-done.6.both_ref), channel_id=1, source_target_pairs={{0,1},{1,0},{2,3},{3,2},{4,5},{5,4},{6,7},{7,6},{8,9},{9,8},{10,11... | collective-permute-start | bytes 466952 | tf_op jit(solution)/shard_map/ppermute | solution.py:593
  25.6 0.1 collective-permute-start.8
  25.6 0.0 collective-permute-done.5.core_ref
  25.6 0.9 %collective-permute-done.7.across_ref = f32[152,256]{1,0:T(8,128)S(1)} collective-permute-done((f32[152,256]{1,0:T(8,128)S(1)}, f32[152,256]{1,0:T(8,128)S(1)}, u32[]{:S(2)}, u32[]{:S(2)}) %collective-permute-start.7) | collective-permute-done | bytes 155680 | tf_op jit(solution)/shard_map/ppermute | solution.py:593
  26.6 1.4 %transform.4 = (f32[6,24,384]{2,1,0:T(8,128)S(1)}, f32[6,16,256]{2,1,0:T(8,128)S(1)}) custom-call(f32[152,256]{1,0:T(8,128)S(1)} %ends.1.own_ref, f32[152,256]{1,0:T(8,128)S(1)} %collective-permute-done.5.core_ref, f32[152,256]{1,0:T(8,128)S(1)} %collective-permute-done.7.across_ref, f32[152,256]{1,0:T(8,128)S(1)} %collective-permute-done.6.both_ref, ...), custom_call_target="tpu_custom_call" | custom-call | flops 452984832 | bytes 1179648 | tf_op jit(solution)/shard_map/transform/pallas_call | solution.py:543
  27.9 1.6 %collective-permute-done.9.across_ref = f32[200,256]{1,0:T(8,128)S(1)} collective-permute-done((f32[200,256]{1,0:T(8,128)S(1)}, f32[200,256]{1,0:T(8,128)S(1)}, u32[]{:S(2)}, u32[]{:S(2)}) %collective-permute-start.9) | collective-permute-done | bytes 204832 | tf_op jit(solution)/shard_map/ppermute | solution.py:587
  29.5 0.0 collective-permute-start.10
  29.6 0.7 %early.1 = (f32[6,80,256]{2,1,0:T(8,128)S(1)}, f32[40,256]{1,0:T(8,128)S(1)}) custom-call(f32[6,128,256]{2,1,0:T(8,128)S(1)} %bitcast.13, s32[128,256]{1,0:T(8,128)S(1)} %copy-done.4, f32[128,128]{1,0:T(8,128)S(1)} %copy-done.8, f32[6,80,384]{2,1,0:T(8,128)S(1)} %get-tuple-element.30.p0_ref, f32[6,24,384]{2,1,0:T(8,128)S(1)} %get-tuple-element.32.p1_ref, ...), custom_call_target="tpu_custom_call" | custom-call | flops 5898240 | bytes 3145728 | tf_op jit(solution)/shard_map/early/pallas_call | solution.py:619
  30.3 0.0 collective-permute-done.8.core_ref
  30.3 0.7 %collective-permute-done.10.both_ref = f32[200,256]{1,0:T(8,128)S(1)} collective-permute-done((f32[200,256]{1,0:T(8,128)S(1)}, f32[200,256]{1,0:T(8,128)S(1)}, u32[]{:S(2)}, u32[]{:S(2)}) %collective-permute-start.10) | collective-permute-done | bytes 204832 | tf_op jit(solution)/shard_map/ppermute | solution.py:593
  31.0 1.7 %transform.5 = (f32[6,32,384]{2,1,0:T(8,128)S(1)}, f32[6,32,256]{2,1,0:T(8,128)S(1)}) custom-call(f32[200,256]{1,0:T(8,128)S(1)} %second.1.own_ref, f32[200,256]{1,0:T(8,128)S(1)} %collective-permute-done.8.core_ref, f32[200,256]{1,0:T(8,128)S(1)} %collective-permute-done.9.across_ref, f32[200,256]{1,0:T(8,128)S(1)} %collective-permute-done.10.both_ref, ...), custom_call_target="tpu_custom_call" | custom-call | flops 603979776 | bytes 1572864 | tf_op jit(solution)/shard_map/transform/pallas_call | solution.py:543
  32.7 0.5 %late.1 = (f32[6,48,256]{2,1,0:T(8,128)S(1)}, f32[32,128]{1,0:T(8,128)S(1)}) custom-call(f32[6,128,256]{2,1,0:T(8,128)S(1)} %bitcast.14, s32[128,256]{1,0:T(8,128)S(1)} %copy-done.4, f32[128,128]{1,0:T(8,128)S(1)} %copy-done.8, f32[6,80,384]{2,1,0:T(8,128)S(1)} %get-tuple-element.30.p0_ref, f32[6,24,384]{2,1,0:T(8,128)S(1)} %get-tuple-element.32.p1_ref, ...), custom_call_target="tpu_custom_call" | custom-call | flops 1572864 | bytes 786432 | tf_op jit(solution)/shard_map/late/pallas_call | solution.py:626
  33.2 12.9 %all_to_all.11 = f32[32,1,128]{2,1,0:T(1,128)S(1)} all-to-all(f32[32,1,128]{2,1,0:T(1,128)S(1)} %bitcast.21), channel_id=1, replica_groups=mesh['ax'=8,'sec'=4] {'ax','sec'}, dimensions={0} | all-to-all | bytes 32768 | tf_op jit(solution)/shard_map/all_to_all | solution.py:630
  46.2 1.3 %update.1 = (f32[6,128,256]{2,1,0:T(8,128)}, f32[6,128,256]{2,1,0:T(8,128)}, f32[1,3]{1,0:T(1,128)}) custom-call(f32[6,128,256]{2,1,0:T(8,128)S(1)} %bitcast.17, f32[6,80,256]{2,1,0:T(8,128)S(1)} %get-tuple-element.35.early_ref, f32[6,48,256]{2,1,0:T(8,128)S(1)} %get-tuple-element.40.late_ref, f32[32,128]{1,0:T(8,128)S(1)} %bitcast.20, ...), custom_call_target="tpu_custom_call" | custom-call | flops 786432 | bytes 4718592 | tf_op jit(solution)/shard_map/update/pallas_call | solution.py:631
  (13 shorter events, 0.1 us)
Async XLA Ops:
  0.6 11.2 %copy-start.2 = (f32[128,6,256]{2,0,1:T(8,128)S(1)}, f32[128,6,256]{2,0,1:T(8,128)}, u32[]{:S(2)}) copy-start(f32[128,6,256]{2,0,1:T(8,128)} %param.13) | copy-start | bytes 2359300
  0.6 11.2 %copy-start.3 = (f32[128,6,256]{2,0,1:T(8,128)S(1)}, f32[128,6,256]{2,0,1:T(8,128)}, u32[]{:S(2)}) copy-start(f32[128,6,256]{2,0,1:T(8,128)} %param.12) | copy-start | bytes 2359300
  0.7 11.2 %copy-start.4 = (s32[128,256]{1,0:T(8,128)S(1)}, s32[128,256]{1,0:T(8,128)}, u32[]{:S(2)}) copy-start(s32[128,256]{1,0:T(8,128)} %hole_ref.13) | copy-start | bytes 393220
  0.7 13.5 %copy-start.10 = (f32[6,6,1024]{2,1,0:T(8,128)S(1)}, f32[6,6,1024]{2,1,0:T(8,128)}, u32[]{:S(2)}) copy-start(f32[6,6,1024]{2,1,0:T(8,128)} %precond_ref.1) | copy-start | bytes 442372
  4.1 14.6 %collective-permute-start.1 = (f32[488,256]{1,0:T(8,128)}, f32[488,256]{1,0:T(8,128)S(1)}, u32[]{:S(2)}, u32[]{:S(2)}) collective-permute-start(f32[488,256]{1,0:T(8,128)} %get-tuple-element.25.own_ref), channel_id=1, source_target_pairs={{0,2},{1,3},{2,0},{3,1},{4,6},{5,7},{6,4},{7,5},{8,10},{9,11},{10,... | collective-permute-start | bytes 1499144 | tf_op jit(solution)/shard_map/ppermute | solution.py:587
  7.1 13.8 %collective-permute-start = (f32[488,256]{1,0:T(8,128)}, f32[488,256]{1,0:T(8,128)S(1)}, u32[]{:S(2)}, u32[]{:S(2)}) collective-permute-start(f32[488,256]{1,0:T(8,128)} %get-tuple-element.25.own_ref), channel_id=1, source_target_pairs={{0,1},{1,0},{2,3},{3,2},{4,5},{5,4},{6,7},{7,6},{8,9},{9,8},{10,11... | collective-permute-start | bytes 1499144 | tf_op jit(solution)/shard_map/ppermute | solution.py:593
  7.1 8.6 %collective-permute-start.2 = (f32[16,256]{1,0:T(8,128)}, f32[16,256]{1,0:T(8,128)S(1)}, u32[]{:S(2)}, u32[]{:S(2)}) collective-permute-start(f32[16,256]{1,0:T(8,128)} %get-tuple-element.27.up_ref), channel_id=1, source_target_pairs={{0,4},{4,8},{8,12},{12,16},{16,20},{20,24},{24,28},{1,5},{5,9},{9,... | collective-permute-start | bytes 49160 | tf_op jit(solution)/shard_map/ppermute | solution.py:596
  10.5 5.8 %collective-permute-start.3 = (f32[16,256]{1,0:T(8,128)}, f32[16,256]{1,0:T(8,128)S(1)}, u32[]{:S(2)}, u32[]{:S(2)}) collective-permute-start(f32[16,256]{1,0:T(8,128)} %get-tuple-element.28.down_ref), channel_id=1, source_target_pairs={{4,0},{8,4},{12,8},{16,12},{20,16},{24,20},{28,24},{5,1},{9,5},{13... | collective-permute-start | bytes 49160 | tf_op jit(solution)/shard_map/ppermute | solution.py:597
  11.8 1.1 %copy-start.5 = (f32[128,6,256]{2,0,1:T(8,128)S(1)}, f32[128,6,256]{2,0,1:T(8,128)}, u32[]{:S(2)}) copy-start(f32[128,6,256]{2,0,1:T(8,128)} %param.11) | copy-start | bytes 2359300
  13.0 0.8 %copy-start.8 = (f32[128,128]{1,0:T(8,128)S(1)}, f32[128,128]{1,0:T(8,128)}, u32[]{:S(2)}) copy-start(f32[128,128]{1,0:T(8,128)} %get-tuple-element.24.factor_ref) | copy-start | bytes 196612
  13.8 1.2 %copy-start.6 = (bf16[1024,512]{1,0:T(8,128)(2,1)S(1)}, bf16[1024,512]{1,0:T(8,128)(2,1)}, u32[]{:S(2)}) copy-start(bf16[1024,512]{1,0:T(8,128)(2,1)} %constant.8.clone.fold_ref) | copy-start | bytes 3145732
  13.8 2.5 %copy-start.11 = (f32[104,256]{1,0:T(8,128)S(1)}, f32[104,256]{1,0:T(8,128)}, u32[]{:S(2)}) copy-start(f32[104,256]{1,0:T(8,128)} %get-tuple-element.26.ends_ref) | copy-start | bytes 319492
  13.8 2.5 %copy-start.12 = (f32[16,256]{1,0:T(8,128)S(1)}, f32[16,256]{1,0:T(8,128)}, u32[]{:S(2)}) copy-start(f32[16,256]{1,0:T(8,128)} %get-tuple-element.27.up_ref) | copy-start | bytes 49156
  13.8 2.5 %copy-start.13 = (f32[16,256]{1,0:T(8,128)S(1)}, f32[16,256]{1,0:T(8,128)}, u32[]{:S(2)}) copy-start(f32[16,256]{1,0:T(8,128)} %get-tuple-element.28.down_ref) | copy-start | bytes 49156
  13.8 7.1 %copy-start.1 = (bf16[3072,256]{1,0:T(8,128)(2,1)S(1)}, bf16[3072,256]{1,0:T(8,128)(2,1)}, u32[]{:S(2)}) copy-start(bf16[3072,256]{1,0:T(8,128)(2,1)} %constant.9.clone.forward_ref) | copy-start | bytes 4718596
  15.0 5.8 %copy-start = (bf16[3072,256]{1,0:T(8,128)(2,1)S(1)}, bf16[3072,256]{1,0:T(8,128)(2,1)}, u32[]{:S(2)}) copy-start(bf16[3072,256]{1,0:T(8,128)(2,1)} %constant.10.clone.inverse_ref) | copy-start | bytes 4718596
  15.0 5.9 %copy-start.7 = (f32[2,8,1024]{2,1,0:T(8,128)S(1)}, f32[2,8,1024]{2,1,0:T(8,128)}, u32[]{:S(2)}) copy-start(f32[2,8,1024]{2,1,0:T(8,128)} %constant.11.clone.beyond_ref) | copy-start | bytes 196612
  15.0 5.9 %copy-start.9 = (f32[488,256]{1,0:T(8,128)S(1)}, f32[488,256]{1,0:T(8,128)}, u32[]{:S(2)}) copy-start(f32[488,256]{1,0:T(8,128)} %get-tuple-element.25.own_ref) | copy-start | bytes 1499140
  18.7 2.2 %collective-permute-start.4 = (f32[488,256]{1,0:T(8,128)S(1)}, f32[488,256]{1,0:T(8,128)S(1)}, u32[]{:S(2)}, u32[]{:S(2)}) collective-permute-start(f32[488,256]{1,0:T(8,128)S(1)} %collective-permute-done.1.across_ref), channel_id=1, source_target_pairs={{0,1},{1,0},{2,3},{3,2},{4,5},{5,4},{6,7},{7,6},{8,9},{9,8},{10,11... | collective-permute-start | bytes 1499144 | tf_op jit(solution)/shard_map/ppermute | solution.py:593
  18.7 6.3 %collective-permute-start.6 = (f32[152,256]{1,0:T(8,128)S(1)}, f32[152,256]{1,0:T(8,128)S(1)}, u32[]{:S(2)}, u32[]{:S(2)}) collective-permute-start(f32[152,256]{1,0:T(8,128)S(1)} %ends.1.own_ref), channel_id=1, source_target_pairs={{0,3},{1,2},{2,1},{3,0},{4,7},{5,6},{6,5},{7,4},{8,11},{9,10},{10,... | collective-permute-start | bytes 466952 | tf_op jit(solution)/shard_map/ppermute | solution.py:590
  20.6 9.0 %collective-permute-start.9 = (f32[200,256]{1,0:T(8,128)S(1)}, f32[200,256]{1,0:T(8,128)S(1)}, u32[]{:S(2)}, u32[]{:S(2)}) collective-permute-start(f32[200,256]{1,0:T(8,128)S(1)} %second.1.own_ref), channel_id=1, source_target_pairs={{0,2},{1,3},{2,0},{3,1},{4,6},{5,7},{6,4},{7,5},{8,10},{9,11},{10,... | collective-permute-start | bytes 614408 | tf_op jit(solution)/shard_map/ppermute | solution.py:587
  20.9 4.8 %collective-permute-start.5 = (f32[152,256]{1,0:T(8,128)S(1)}, f32[152,256]{1,0:T(8,128)S(1)}, u32[]{:S(2)}, u32[]{:S(2)}) collective-permute-start(f32[152,256]{1,0:T(8,128)S(1)} %ends.1.own_ref), channel_id=1, source_target_pairs={{0,1},{1,0},{2,3},{3,2},{4,5},{5,4},{6,7},{7,6},{8,9},{9,8},{10,11... | collective-permute-start | bytes 466952 | tf_op jit(solution)/shard_map/ppermute | solution.py:593
  25.0 1.6 %collective-permute-start.7 = (f32[152,256]{1,0:T(8,128)S(1)}, f32[152,256]{1,0:T(8,128)S(1)}, u32[]{:S(2)}, u32[]{:S(2)}) collective-permute-start(f32[152,256]{1,0:T(8,128)S(1)} %collective-permute-done.6.both_ref), channel_id=1, source_target_pairs={{0,1},{1,0},{2,3},{3,2},{4,5},{5,4},{6,7},{7,6},{8,9},{9,8},{10,11... | collective-permute-start | bytes 466952 | tf_op jit(solution)/shard_map/ppermute | solution.py:593
  25.6 4.7 %collective-permute-start.8 = (f32[200,256]{1,0:T(8,128)S(1)}, f32[200,256]{1,0:T(8,128)S(1)}, u32[]{:S(2)}, u32[]{:S(2)}) collective-permute-start(f32[200,256]{1,0:T(8,128)S(1)} %second.1.own_ref), channel_id=1, source_target_pairs={{0,1},{1,0},{2,3},{3,2},{4,5},{5,4},{6,7},{7,6},{8,9},{9,8},{10,11... | collective-permute-start | bytes 614408 | tf_op jit(solution)/shard_map/ppermute | solution.py:593
  29.5 1.5 %collective-permute-start.10 = (f32[200,256]{1,0:T(8,128)S(1)}, f32[200,256]{1,0:T(8,128)S(1)}, u32[]{:S(2)}, u32[]{:S(2)}) collective-permute-start(f32[200,256]{1,0:T(8,128)S(1)} %collective-permute-done.9.across_ref), channel_id=1, source_target_pairs={{0,1},{1,0},{2,3},{3,2},{4,5},{5,4},{6,7},{7,6},{8,9},{9,8},{10,11... | collective-permute-start | bytes 614408 | tf_op jit(solution)/shard_map/ppermute | solution.py:593

commit v4 on v3

v4 whole, which is shorter than its diff:
```python
import functools

import jax
import jax.numpy as jnp
import ml_dtypes
import numpy as np
from jax import lax
from jax.experimental import pallas as pl
from jax.experimental.pallas import tpu as pltpu
from jax.sharding import PartitionSpec as P

F32 = jnp.float32
BF16 = jnp.bfloat16
SECTORS = 4
TILE = 8
LANES = 128


def two_parts(table):
    high = table.astype(ml_dtypes.bfloat16)
    low = (table - high.astype(np.float64)).astype(ml_dtypes.bfloat16)
    return np.stack([high, low])


@functools.lru_cache(maxsize=None)
def harmonic_tables(width):
    around = SECTORS * width
    half = width // 2
    zero = [("c", 4 * q) for q in range(half + 1)] + [("s", 4 * q) for q in range(1, half)]
    two = [(f, 4 * q + 2) for f in "cs" for q in range(half)]
    one = [(f, 8 * q + 1) for f in "cs" for q in range(half)]
    five = [(f, 8 * q + 5) for f in "cs" for q in range(half)]
    columns = zero + two + one + five
    harmonic = np.array([k for _, k in columns], dtype=np.int64)
    is_sin = np.array([f == "s" for f, _ in columns])

    def wave(place, shift):
        angle = 2.0 * np.pi / around * ((place[:, None] * harmonic[None, :]) % around)
        return np.cos(angle - shift)

    place = np.arange(width)
    shift = np.where(is_sin, np.pi / 2, 0.0)[None, :]
    direct = wave(place, shift)
    turned = np.concatenate([direct[:half], wave(place[:half], shift - np.pi / 2)], axis=0)
    forward = [direct[:, :width], direct[:, width : 2 * width]]
    forward += [turned[:, 2 * width : 3 * width], turned[:, 3 * width :]]
    ends = np.array([around - 1, 2 * width, around - width - 1, width])
    beyond = np.repeat(wave(ends, shift).astype(np.float32)[:, None, :], TILE, axis=1)
    odd = np.concatenate([direct.T, wave(place + width, shift).T], axis=1)[2 * width :]
    fold = np.zeros((around, 4 * half))
    kinds = [4 * np.arange(half), 4 * np.arange(half) + 2, 8 * np.arange(half) + 1, 8 * np.arange(half) + 5]
    for column, k in enumerate(np.concatenate(kinds)):
        for place in {k, (around - k) % around}:
            fold[place, column] = 1.0 / around
    return (
        np.stack([two_parts(t) for t in forward]),
        np.stack([two_parts(t) for t in (direct.T[:width], direct.T[width : 2 * width])]),
        two_parts(odd),
        beyond,
        fold.astype(ml_dtypes.bfloat16),
    )


def split(x):
    high = x.astype(BF16)
    return high, (x - high.astype(F32)).astype(BF16)


def product(high, low, table_ref):
    left = jnp.concatenate([high, low, high], axis=1)
    table = jnp.concatenate([table_ref[0], table_ref[0], table_ref[1]], axis=0)
    return jnp.dot(left, table, preferred_element_type=F32)


def lanes_of(shape):
    return lax.broadcasted_iota(jnp.int32, shape, len(shape) - 1)


def rows_of(shape):
    return lax.broadcasted_iota(jnp.int32, shape, len(shape) - 2)


def beside_sum(x, before, after):
    lane = lanes_of(x.shape)
    size = x.shape[-1]
    left = jnp.where(lane == 0, before, pltpu.roll(x, 1, x.ndim - 1))
    right = jnp.where(lane == size - 1, after, pltpu.roll(x, size - 1, x.ndim - 1))
    return left + right


def stacked_sum(x, before=0.0, after=0.0):
    row = rows_of(x.shape)
    size = x.shape[0]
    up = jnp.where(row == 0, before, pltpu.roll(x, 1, 0))
    down = jnp.where(row == size - 1, after, pltpu.roll(x, size - 1, 0))
    return up + down


def fold_kernel(precond_ref, fold_ref, *refs):
    out_ref, beyond_ref = refs[-2:]
    comps = precond_ref.shape[0]
    value = jnp.concatenate([precond_ref[q] for q in range(comps)], axis=0)
    pairs, around = value.shape
    high = value.astype(BF16)
    rest = value - high.astype(F32)
    middle = rest.astype(BF16)
    low = (rest - middle.astype(F32)).astype(BF16)
    terms = [jnp.dot(t, fold_ref[...], preferred_element_type=F32) for t in (high, middle, low)]
    folded = terms[0] + (terms[1] + terms[2])
    half = folded.shape[1] // 4
    zero = folded[:, :half]
    top = value[:, around // 2 : around // 2 + 1] * F32(1.0 / around)
    other = jnp.where(lanes_of(zero.shape) == 0, top, zero)
    folded = jnp.concatenate([zero, other, folded[:, half:]], axis=1)
    for i in range(pairs):
        out_ref[i] = jnp.broadcast_to(folded[i : i + 1], out_ref.shape[1:])
    rest = [jnp.zeros((TILE - comps, folded.shape[1]), F32)]
    for p in range(comps):
        beyond_ref[p] = jnp.concatenate([folded[i : i + 1] for i in range(p, pairs, comps)] + rest, axis=0)


def factor_columns(table_ref, class_ref, ax_size, comps):
    classes = class_ref[...]
    slab = classes.shape[1]
    position = lax.axis_index("ax") * slab + lanes_of(classes.shape)
    taper = 1.0 + 2.0 * position.astype(F32) / F32(ax_size * slab - 1)
    rows = []
    for q in range(comps):
        value = jnp.zeros(classes.shape, F32)
        for kind in range(table_ref.shape[0]):
            value = jnp.where(classes == kind, table_ref[kind, q], value)
        rows.append(value * taper)
    rows.append(jnp.zeros((LANES - comps, slab), F32))
    return jnp.concatenate(rows, axis=0).T


def local_part(q, block, inner, solid, factor, load, stiff, other):
    field = block[inner]
    beside = stacked_sum(block)[inner] + beside_sum(field, 0.0, 0.0)
    stiffness = stiff * factor[:, q : q + 1]
    image = (stiffness + 4.5) * field - beside - 0.5 * other[inner]
    return solid * (load - image)


def edge_rows(fields, solid):
    rows, width = solid.shape
    sources = fields + [solid] * (TILE - len(fields))
    columns = [x[:, :1] for x in sources] + [x[:, width - 1 :] for x in sources]
    table = jnp.concatenate(columns + [jnp.zeros((rows, LANES - 2 * TILE), F32)], axis=1)
    if rows < LANES:
        table = jnp.concatenate([table, jnp.zeros((LANES - rows, LANES), F32)], axis=0)
    table = table.T
    return table[:TILE], table[TILE : 2 * TILE]


def first_kernel(
    end, comps, ax_size, table_ref, class_ref, load_ref, disp_ref, stiff_ref, hole_ref,
    keep_ref, other_ref, ends_ref, factor_ref, up_ref, down_ref,
    table_in, class_in, load_in, disp_in, stiff_in, hole_in, inner_out, ends_out, factor_out, up_out, down_out,
    in_sems, out_sems,
):
    slab, width = hole_ref.shape
    half = slab // 2
    inner = half - end
    core = lax.axis_index("sec") % 2

    def copy(src, dst, sems, i):
        moving = pltpu.make_async_copy(src, dst, sems.at[i])
        moving.start()
        return moving

    small = [
        copy(class_ref, class_in, in_sems, 0), copy(table_ref, table_in, in_sems, 1), copy(hole_ref, hole_in, in_sems, 2)
    ]
    moving = []
    for q in range(comps):
        pairs = ((disp_ref, disp_in), (load_ref, load_in), (stiff_ref, stiff_in))
        moving.append([copy(src.at[q], dst.at[q], in_sems, 3 + 3 * q + k) for k, (src, dst) in enumerate(pairs)])
    for one in small:
        one.wait()
    factor_out[...] = factor_columns(table_in, class_in, ax_size, comps)
    leaving = [copy(factor_out, factor_ref, out_sems, 0)]
    solid = (1 - hole_in[...]).astype(F32)
    factor = factor_out[...]
    for q in range(comps):
        if q % 2 == 0:
            for one in moving[q] + moving[q + 1]:
                one.wait()
        field = disp_in[q]
        part = local_part(q, field, slice(0, slab), solid, factor, load_in[q], stiff_in[q], disp_in[q ^ 1])
        rows = pl.ds(q * inner, inner)
        inner_out[0, rows, :] = part[end:half]
        inner_out[1, rows, :] = part[half : slab - end]
        leaving.append(copy(inner_out.at[core, rows], keep_ref.at[rows], out_sems, 1 + 2 * q))
        leaving.append(copy(inner_out.at[1 - core, rows], other_ref.at[rows], out_sems, 2 + 2 * q))
        rows = pl.ds(q * end, end)
        ends_out[0, rows, :] = part[:end]
        ends_out[1, rows, :] = part[slab - end :]
        up_out[q : q + 1, :] = part[slab - 1 :]
        down_out[q : q + 1, :] = part[:1]
        up_out[TILE + q : TILE + q + 1, :] = field[slab - 1 :]
        down_out[TILE + q : TILE + q + 1, :] = field[:1]
    spare = TILE - comps
    for ref, row in ((up_out, slab - 1), (down_out, 0)):
        ref[comps:TILE, :] = jnp.broadcast_to(solid[row : row + 1], (spare, width))
        ref[TILE + comps :, :] = jnp.zeros((spare, width), F32)
    count = 1 + 2 * comps
    leaving.append(copy(up_out, up_ref, out_sems, count))
    leaving.append(copy(down_out, down_ref, out_sems, count + 1))

    def ordered(x):
        return jnp.concatenate([x[end:half], x[:end], x[half:]], axis=0)

    edges = edge_rows([ordered(disp_in[q]) for q in range(comps)], ordered(solid))
    last = pl.ds(comps * inner, TILE)
    for h in range(2):
        inner_out[h, last, :] = jnp.concatenate([pltpu.roll(x, (LANES - half * h) % LANES, 1) for x in edges], axis=1)
        ends_out[h, pl.ds(comps * end, 2 * TILE), :] = (down_out, up_out)[h][...]
    leaving.append(copy(inner_out.at[core, last], keep_ref.at[last], out_sems, count + 2))
    leaving.append(copy(inner_out.at[1 - core, last], other_ref.at[last], out_sems, count + 3))
    leaving.append(copy(ends_out, ends_ref, out_sems, count + 4))
    for one in leaving:
        one.wait()


def ends_kernel(comps, ends_ref, before_ref, after_ref, keep_ref, other_ref, out_ref):
    rows = (ends_ref.shape[1] - 2 * TILE) // comps
    width = ends_ref.shape[2]
    row = rows_of((rows, width))
    core = lax.axis_index("sec") % 2
    for h, far_ref, at in ((0, before_ref, 0), (1, after_ref, rows - 1)):
        own_ref = ends_ref.at[h, pl.ds(comps * rows, 2 * TILE)]
        solid_own = own_ref[comps : comps + 1]
        far = far_ref[...]
        for q in range(comps):
            part = ends_ref[h, pl.ds(q * rows, rows), :]
            part = part + jnp.where(row == at, solid_own * far[TILE + q : TILE + q + 1], 0.0)
            out_ref[h, pl.ds(q * rows, rows), :] = part
        solid_far = far[comps : comps + 1]
        residual = far[:TILE] + solid_far * own_ref[TILE:]
        out_ref[h, pl.ds(comps * rows, TILE), :] = jnp.where(rows_of(residual.shape) < comps, residual, solid_far)
        out_ref[h, pl.ds(comps * rows + TILE, TILE), :] = far[TILE:]
    keep_ref[...] = out_ref[core]
    other_ref[...] = out_ref[1 - core]


def in_order(odd, own, core, across, both):
    return own, jnp.where(odd, both, core), across, jnp.where(odd, core, both)


def butterfly(x0, x1, x2, x3):
    even, other = x0 + x2, x1 + x3
    return even + other, even - other, x0 - x2, x1 - x3


def edge_table(odd, blocks):
    tiles = in_order(odd, *blocks)
    left = [t[:, :LANES] for t in tiles]
    right = [t[:, LANES:] for t in tiles]
    solid = TILE - 1
    at_left = [left[s][solid:] * right[s - 1] for s in range(SECTORS)]
    at_right = [right[s][solid:] * left[(s + 1) % SECTORS] for s in range(SECTORS)]
    stack = []
    for one, other in zip(butterfly(*at_left), butterfly(*at_right)):
        stack += [one, other]
    stack += [at_left[0], at_right[0]]
    stack += [jnp.where(odd, at_left[3], at_left[1]), jnp.where(odd, at_right[3], at_right[1])]
    stack += [right[3], left[1], jnp.where(odd, right[2], right[0]), jnp.where(odd, left[0], left[2])]
    return jnp.concatenate(stack, axis=0).T


def transform_kernel(
    comps, main, at_end, edge_at, hole_at, own_ref, core_ref, across_ref, both_ref,
    forward_ref, even_ref, odd_ref, beyond_ref, weight_ref, beyond_weight_ref, hole_ref, edge_ref,
    prec_ref, residual_ref, back_ref, left_ref, spectrum_ref, scaled_ref, halo_ref,
):
    width = own_ref.shape[1]
    half = width // 2
    core = lax.axis_index("sec") % 2
    odd = core == 1
    sign = jnp.where(odd, -1.0, 1.0)
    rows = main
    total = comps * rows
    group = 1 if rows % 16 == 0 else 2
    sources = (own_ref, core_ref, across_ref, both_ref)
    start, stride = hole_at
    solid = (1 - hole_ref[pl.ds(pl.multiple_of(start + stride * core, TILE), main)]).astype(F32)
    if not at_end:
        edge_ref[...] = edge_table(odd, [r[total : total + TILE] for r in sources])
    edge = edge_ref[pl.ds(edge_at, main), :]
    lane = lanes_of((main, LANES))
    first = lane == 0
    last = lane == LANES - 1

    def edge_column(tile, q):
        column = tile * TILE + q
        return edge[:, column : column + 1]

    def with_edges(x, array, q):
        head = x[:, :LANES] + jnp.where(first, edge_column(2 * array, q), 0.0)
        tail = x[:, -LANES:] + jnp.where(last, edge_column(2 * array + 1, q), 0.0)
        middle = [x[:, LANES:-LANES]] if width > 2 * LANES else []
        return jnp.concatenate([head] + middle + [tail], axis=1)

    def arrays_of(q):
        at = q * rows
        own, core, across, both = [r[pl.ds(at, main), :] for r in sources]
        arrays = butterfly(own, core, across, both)
        arrays = arrays[:3] + (sign * arrays[3],)
        arrays = [with_edges(x, i, q) for i, x in enumerate(arrays)]
        residual_ref[q] = with_edges(own, 4, q)
        return turned(*arrays)

    def turned(y0, y2, real, imag):
        turned_real = (real[:, half:] - imag[:, half:]) * F32(np.sqrt(0.5))
        turned_imag = (real[:, half:] + imag[:, half:]) * F32(np.sqrt(0.5))
        plus = jnp.concatenate([real[:, :half] + turned_real, imag[:, :half] + turned_imag], axis=1)
        minus = jnp.concatenate([real[:, :half] - turned_real, imag[:, :half] - turned_imag], axis=1)
        return y0, y2, plus, minus

    def arrays_beyond():
        tiles = in_order(odd, *[r[pl.ds(total, TILE), :] for r in sources])
        disp = in_order(odd, *[r[pl.ds(total + TILE, TILE), :] for r in sources])
        place = lanes_of((TILE, width))
        fixed = []
        for s in range(SECTORS):
            beside = jnp.where(place == 0, pltpu.roll(disp[s - 1], 1, 1), 0.0)
            beside = beside + jnp.where(
                place == width - 1, pltpu.roll(disp[(s + 1) % SECTORS], width - 1, 1), 0.0
            )
            value = tiles[s] + tiles[s][comps : comps + 1] * beside
            fixed.append(jnp.where(rows_of((TILE, width)) < comps, value, 0.0))
        return turned(*butterfly(*fixed))

    def put(at, arrays):
        for i, x in enumerate(arrays):
            high, low = split(x)
            left_ref[at, 2 * i * width : (2 * i + 1) * width] = high
            left_ref[at, (2 * i + 1) * width : (2 * i + 2) * width] = low

    for begin in range(0, comps, group):
        found = [arrays_of(q) for q in range(begin, begin + group)]
        put(pl.ds(begin * rows, group * rows), [jnp.concatenate([x[i] for x in found], axis=0) for i in range(4)])
    if at_end:
        put(pl.ds(total, 2 * TILE), [jnp.concatenate([x, jnp.zeros_like(x)], axis=0) for x in arrays_beyond()])
    height = left_ref.shape[0]

    for i in range(4):
        high = left_ref[:, 2 * i * width : (2 * i + 1) * width]
        low = left_ref[:, (2 * i + 1) * width : (2 * i + 2) * width]
        part = product(high, low, forward_ref.at[i])
        spectrum_ref[:, :, i * width : (i + 1) * width] = part.reshape(height // TILE, TILE, width)

    around = SECTORS * width

    def scale(row, count):
        tiles = count // TILE

        def spectrum(p, lanes):
            return spectrum_ref[pl.ds((p * rows + row) // TILE, tiles), :, lanes]

        for begin in range(0, comps, group):
            halo = [[None, None] for _ in range(group)]
            for k in range(4):
                for h in range(2):
                    lanes = slice(k * width + h * half, k * width + (h + 1) * half)
                    kind = h if k == 0 else k + 1
                    values = []
                    for i in range(group):
                        value = None
                        for p in range(comps):
                            weight = weight_ref[(begin + i) * comps + p, :, kind * half : (kind + 1) * half]
                            term = spectrum(p, lanes) * weight
                            value = term if value is None else value + term
                        for side in range(2):
                            term = value * beyond_ref[2 * core + side, :, lanes]
                            halo[i][side] = term if halo[i][side] is None else halo[i][side] + term
                        values.append(value.reshape(count, half))
                    high, low = split(values[0] if group == 1 else jnp.concatenate(values, axis=0))
                    at = pl.ds(begin * rows + row, group * count)
                    scaled_ref[at, lanes] = high
                    scaled_ref[at, around + lanes.start : around + lanes.stop] = low
            for i in range(group):
                before, after = [jnp.sum(x, axis=2, keepdims=True) for x in halo[i]]
                tile = jnp.where(lanes_of((tiles, TILE, LANES)) == 0, before, after)
                halo_ref[pl.ds((begin + i) * rows + row, count), :] = tile.reshape(count, LANES)

    def scale_beyond():
        at = pl.ds(total, 2 * TILE)
        for k in range(4):
            for h in range(2):
                lanes = slice(k * width + h * half, k * width + (h + 1) * half)
                kind = h if k == 0 else k + 1
                parts = spectrum_ref[total // TILE, :, lanes]
                value = None
                for p in range(comps):
                    term = parts[p : p + 1] * beyond_weight_ref[p, :, kind * half : (kind + 1) * half]
                    value = term if value is None else value + term
                high, low = split(jnp.concatenate([value, jnp.zeros_like(value)], axis=0))
                scaled_ref[at, lanes] = high
                scaled_ref[at, around + lanes.start : around + lanes.stop] = low

    if at_end:
        scale_beyond()
    step = rows if group > 1 else 32
    for row in range(0, rows, step):
        scale(row, min(step, rows - row))

    def inverse(columns, table_ref):
        low = scaled_ref[:, around + columns.start : around + columns.stop]
        return product(scaled_ref[:, columns], low, table_ref)

    zero = inverse(slice(0, width), even_ref.at[0])
    two = inverse(slice(width, 2 * width), even_ref.at[1])
    odds = inverse(slice(2 * width, around), odd_ref)
    own_all = zero + two + odds[:, :width]
    other_all = zero - two + sign * odds[:, width:]
    for q in range(comps):
        at = q * rows
        own, other = own_all[at : at + rows], other_all[at : at + rows]
        side = halo_ref[pl.ds(at, rows), :]
        far_before, far_after = side[:, :1], side[:, 1:2]
        own_before = jnp.where(odd, other[:, width - 1 :], far_before)
        own_after = jnp.where(odd, far_after, other[:, :1])
        other_before = jnp.where(odd, far_before, own[:, width - 1 :])
        other_after = jnp.where(odd, own[:, :1], far_after)
        solids = [edge_column(tile, TILE - 1) for tile in (12, 13, 14, 15)]
        at = pl.ds(at, rows)
        prec_ref[at, :width] = own * solid
        prec_ref[at, width:] = jnp.where(first, own_before * solids[0], own_after * solids[1])
        tile = jnp.where(first, other_before * solids[2], other_after * solids[3])
        tile = jnp.where(lane == 2, edge_column(10, q), jnp.where(lane == 3, edge_column(11, q), tile))
        back_ref[at, :width] = other
        back_ref[at, width:] = tile
    if at_end:
        at = pl.ds(total, TILE)
        for ref, result, source in ((prec_ref, own_all, own_ref), (back_ref, other_all, core_ref)):
            ref[at, :width] = result[total : total + TILE] * source[pl.ds(total + comps, 1), :]
            ref[at, width:] = jnp.zeros((TILE, LANES), F32)


def image_rows(q, fields, tile, stiff, solid, factor, before, after, inner):
    field = fields[q][inner]
    beside = beside_sum(field, tile[:, :1], tile[:, 1:2])
    beside = beside + stacked_sum(fields[q], before, after)[inner]
    stiffness = stiff * factor[:, q : q + 1]
    return field, solid * ((stiffness + 4.5) * field - beside - 0.5 * fields[q ^ 1][inner])


def add_sums(sums, residual, field, image):
    rows, width = field.shape
    pairs = ((residual, field), (field, image), (residual, residual), (residual, image), (image, image))
    return [
        total + jnp.sum((x * y).reshape(rows // TILE, TILE, width), axis=0)
        for total, (x, y) in zip(sums, pairs)
    ]


def returned(back, sent, solid, q, rows):
    width = sent.shape[1]
    side = back[pl.ds(q * rows, rows), width:]
    residual = sent[pl.ds(q * rows, rows), :]
    lane = lanes_of(residual.shape)
    residual = residual + jnp.where(lane == 0, side[:, 2:3], 0.0) + jnp.where(lane == width - 1, side[:, 3:4], 0.0)
    return back[pl.ds(q * rows, rows), :width] * solid, side, residual


def early_kernel(
    end, comps, stiff_ref, hole_ref, factor_ref, own_ref, back_ref, residual_ref, sent_ref,
    prec_out, residual_out, image_ref, sums_ref,
):
    slab, width = hole_ref.shape
    inner = slab // 2 - end
    core = lax.axis_index("sec") % 2
    here = pl.ds(pl.multiple_of(inner * core, TILE), inner)
    there = pl.ds(pl.multiple_of(inner * (1 - core), TILE), inner)
    solid_there = (1 - hole_ref[pl.ds(pl.multiple_of(end + inner * (1 - core), TILE), inner)]).astype(F32)
    for q in range(comps):
        prec, side, residual = returned(back_ref, sent_ref, solid_there, q, inner)
        prec_out[q, here] = own_ref[pl.ds(q * inner, inner), :]
        prec_out[q, there, :width] = prec
        prec_out[q, there, width:] = side
        residual_out[q, here] = residual_ref[q]
        residual_out[q, there] = residual
    low, high = end + TILE, slab - end - TILE
    core_rows = slice(TILE, 2 * inner - TILE)
    solid = (1 - hole_ref[low:high]).astype(F32)
    factor = factor_ref[low:high]
    sums = [jnp.zeros((TILE, width), F32) for _ in range(5)]
    for q in range(comps):
        fields = {k: prec_out[k, :, :width] for k in (q, q ^ 1)}
        field, image = image_rows(
            q, fields, prec_out[q, core_rows, width:], stiff_ref[q, low:high], solid, factor, 0.0, 0.0, core_rows
        )
        image_ref[q] = image
        sums = add_sums(sums, residual_out[q, core_rows], field, image)
    for i, total in enumerate(sums):
        sums_ref[pl.ds(i * TILE, TILE), :] = total


def late_kernel(
    end, comps, stiff_ref, hole_ref, factor_ref, inner_ref, inner_residual_ref,
    own_ref, back_ref, residual_ref, sent_ref, partial_ref,
    prec_out, residual_out, image_ref, sums_ref,
):
    slab, width = hole_ref.shape
    reach = end + TILE
    core = lax.axis_index("sec") % 2
    odd = core == 1
    solid = (1 - hole_ref[...]).astype(F32)
    factor = factor_ref[...]
    sums = [partial_ref[pl.ds(i * TILE, TILE), :] for i in range(5)]
    fields, tiles, beyond, residuals = [[], []], [[], []], [[], []], [[], []]
    for q in range(comps):
        solid_there = jnp.where(odd, solid[:end], solid[slab - end :])
        there, side, residual = returned(back_ref, sent_ref, solid_there, q, end)
        rows, far = pl.ds(q * end, end), pl.ds(comps * end + q, 1)
        here, own_side = own_ref[rows, :width], own_ref[rows, width:]
        far_here, far_there = own_ref[far, :width], back_ref[far, :width]
        for h, swap in ((0, odd), (1, core == 0)):
            prec = jnp.where(swap, there, here)
            tile = jnp.where(swap, side, own_side)
            rest = jnp.where(swap, residual, residual_ref[q])
            beyond[h].append(jnp.where(swap, far_there, far_here))
            rows = pl.ds(end * h, end)
            prec_out[q, rows] = prec
            residual_out[q, rows] = rest
            near = slice(0, 2 * TILE) if h == 0 else slice(-2 * TILE, None)
            close = slice(0, TILE) if h == 0 else slice(-TILE, None)
            parts = [prec, inner_ref[q, near, :width]]
            sides = [tile, inner_ref[q, close, width:]]
            rests = [rest, inner_residual_ref[q, close]]
            order = slice(None) if h == 0 else slice(None, None, -1)
            fields[h].append(jnp.concatenate(parts[order], axis=0))
            tiles[h].append(jnp.concatenate(sides[order], axis=0))
            residuals[h].append(jnp.concatenate(rests[order], axis=0))
    for h in range(2):
        rows = slice(0, reach) if h == 0 else slice(slab - reach, slab)
        inner = slice(0, reach) if h == 0 else slice(TILE, None)
        for q in range(comps):
            before, after = (beyond[0][q], 0.0) if h == 0 else (0.0, beyond[1][q])
            field, image = image_rows(
                q, fields[h], tiles[h][q], stiff_ref[q, rows], solid[rows], factor[rows], before, after, inner
            )
            image_ref[q, pl.ds(reach * h, reach)] = image
            sums = add_sums(sums, residuals[h][q], field, image)
    row = jnp.zeros((1, LANES), F32)
    spot = lanes_of((1, LANES))
    for i, value in enumerate(sums):
        value = jnp.sum(jnp.sum(value, axis=0, keepdims=True), axis=1, keepdims=True)
        row = jnp.where(spot == i, value, row)
    sums_ref[...] = jnp.broadcast_to(row, sums_ref.shape)


def update_kernel(
    end, comps, cell_total, disp_ref, gathered_ref, inner_ref, inner_residual_ref, inner_image_ref,
    ends_ref, ends_residual_ref, ends_image_ref, disp_out, residual_out, stats_out,
):
    slab, width = disp_ref.shape[1:]
    values = jnp.sum(gathered_ref[...], axis=0, keepdims=True) * F32(1.0 / cell_total)
    rz, zq, rr, ri, ii = [values[:, i : i + 1] for i in range(5)]
    alpha = rz / zq
    square = rr + alpha * (alpha * ii - 2.0 * ri)
    stats_out[...] = jnp.concatenate([rz, zq, square], axis=1)
    reach = end + TILE
    inner = slice(end, slab - end)
    for q in range(comps):
        disp_out[q, :end] = disp_ref[q, :end] + alpha * ends_ref[q, :end]
        disp_out[q, inner] = disp_ref[q, inner] + alpha * inner_ref[q, :, :width]
        disp_out[q, slab - end :] = disp_ref[q, slab - end :] + alpha * ends_ref[q, end:]
        image = jnp.concatenate([ends_image_ref[q, :reach], inner_image_ref[q], ends_image_ref[q, reach:]], axis=0)
        residual_out[q, :end] = ends_residual_ref[q, :end] - alpha * image[:end]
        residual_out[q, inner] = inner_residual_ref[q] - alpha * image[inner]
        residual_out[q, slab - end :] = ends_residual_ref[q, end:] - alpha * image[slab - end :]


VMEM = pl.BlockSpec(memory_space=pltpu.VMEM)
SMEM = pl.BlockSpec(memory_space=pltpu.SMEM)
HBM = pl.BlockSpec(memory_space=pltpu.HBM)
FULL = 62


def call(kernel, name, out_shapes, in_specs, flops, moved, scratch=(), grant=32, out_spec=None):
    return pl.pallas_call(
        kernel,
        out_shape=[jax.ShapeDtypeStruct(s, F32) for s in out_shapes],
        in_specs=in_specs,
        out_specs=[out_spec or VMEM] * len(out_shapes),
        scratch_shapes=list(scratch),
        compiler_params=pltpu.CompilerParams(vmem_limit_bytes=grant * 1024 * 1024),
        cost_estimate=pl.CostEstimate(flops=flops, bytes_accessed=moved, transcendentals=0),
        name=name,
    )


def transform_call(blocks, tables, hole, edge, main, edge_at, hole_at, comps, width, slab, weight):
    around = SECTORS * width
    at_end = edge is not None
    total = comps * main
    out_rows = total + (TILE if at_end else 0)
    rows = total + (2 * TILE if at_end else 0)
    operands = list(blocks) + list(tables) + [hole] + ([edge] if at_end else [])
    shapes = [(out_rows, width + LANES), (comps, main, width), (out_rows, width + LANES)]
    return call(
        functools.partial(transform_kernel, comps, main, at_end, edge_at, hole_at), "transform",
        ([] if at_end else [(slab, LANES)]) + shapes, [VMEM] * len(operands),
        weight * 2 * total * 3 * around * 3 * width, weight * 4 * total * width * 8,
        [pltpu.VMEM((rows, 8 * width), BF16), pltpu.VMEM((rows // TILE, TILE, around), F32),
         pltpu.VMEM((rows, 2 * around), BF16), pltpu.VMEM((total, LANES), F32)],
    )(*operands)


def after_all(x, *others):
    return lax.optimization_barrier((x, *others))[0]


def shards(load, disp, stiff, hole, section_class, class_table, precond):
    slab, comps, width = disp.shape
    ax, sec = lax.axis_size("ax"), lax.axis_size("sec")
    around = width * sec
    cell_total = slab * ax * comps * around
    end = slab // 16 * 2
    inner = slab // 2 - end
    load, disp, stiff = [x.transpose(1, 0, 2) for x in (load, disp, stiff)]
    forward, even, odd, beyond, fold = harmonic_tables(width)
    block = 4 * comps * slab * width
    classes = section_class.reshape(1, slab)

    sent = (comps * inner + TILE, width)
    ends_shape = (2, comps * end + 2 * TILE, width)
    shapes = [sent, sent, ends_shape, (slab, LANES), (2 * TILE, width), (2 * TILE, width)]
    keep, other, edge, factor, up, down = call(
        functools.partial(first_kernel, end, comps, ax), "first",
        shapes, [HBM] * 6, 10 * comps * slab * width, 2 * block,
        [pltpu.SMEM(class_table.shape, F32), pltpu.VMEM((1, slab), jnp.int32)]
        + [pltpu.VMEM((comps, slab, width), F32)] * 3 + [pltpu.VMEM((slab, width), jnp.int32)]
        + [pltpu.VMEM((2,) + sent, F32)] + [pltpu.VMEM(shape, F32) for shape in shapes[2:]]
        + [pltpu.SemaphoreType.DMA((3 + 3 * comps,)), pltpu.SemaphoreType.DMA((6 + 2 * comps,))],
        FULL, HBM,
    )(class_table, classes, load, disp, stiff, hole)

    def to(x, mask):
        return lax.ppermute(x, "sec", [(i, i ^ mask) for i in range(sec)])

    def gather(keep, other):
        return keep, to(other, 1), to(keep, 2), to(other, 3)

    blocks = gather(keep, other)
    before = lax.ppermute(up, "ax", [(i, i + 1) for i in range(ax - 1)])
    after = lax.ppermute(down, "ax", [(i + 1, i) for i in range(ax - 1)])
    weight, beyond_weight = call(
        fold_kernel, "fold", [(comps * comps, TILE, 5 * width // 2), (comps, TILE, 5 * width // 2)], [VMEM] * 6,
        1, 1,
    )(precond, fold, forward, even, odd, beyond)
    rows = (comps * end + 2 * TILE, width)
    keep_ends, other_ends = call(
        functools.partial(ends_kernel, comps), "ends",
        [rows, rows], [VMEM] * 3, 2 * comps * end * width, 16 * comps * end * width, [pltpu.VMEM((2,) + rows, F32)],
    )(after_all(edge, weight), before, after)
    end_blocks = gather(keep_ends, other_ends)
    tables = (forward, even, odd, beyond, weight, beyond_weight)

    across = after_all(blocks[2], keep_ends, weight)
    edge, own, residual, back = transform_call(
        (keep, blocks[1], across, blocks[3]), tables, hole, None, inner, 0, (end, inner), comps, width, slab, 0
    )
    back = to(back, 1)
    across = after_all(end_blocks[2], own)
    own_ends, residual_ends, back_ends = transform_call(
        (keep_ends, end_blocks[1], across, end_blocks[3]), tables, hole, edge, end, inner, (0, slab - end),
        comps, width, slab, 100,
    )
    back_ends = to(back_ends, 1)
    prec, residual, image, partial = call(
        functools.partial(early_kernel, end, comps), "early",
        [(comps, 2 * inner, width + LANES), (comps, 2 * inner, width), (comps, 2 * (inner - TILE), width), (5 * TILE, width)],
        [VMEM] * 7, 30 * comps * slab * width, 4 * block,
    )(stiff, hole, after_all(factor, own_ends), own, back, residual, other)
    prec_ends, residual_ends, image_ends, sums = call(
        functools.partial(late_kernel, end, comps), "late",
        [(comps, 2 * end, width), (comps, 2 * end, width), (comps, 2 * (end + TILE), width), (ax * sec, LANES)],
        [VMEM] * 10, 8 * comps * slab * width, block,
    )(stiff, hole, factor, prec, residual, own_ends, back_ends, residual_ends, other_ends, partial)
    gathered = lax.all_to_all(sums, ("ax", "sec"), 0, 0, tiled=True)
    disp_new, residual_new, stats = call(
        functools.partial(update_kernel, end, comps, cell_total), "update",
        [(comps, slab, width), (comps, slab, width), (1, 3)], [VMEM] * 8,
        4 * comps * slab * width, 6 * block,
    )(disp, gathered, prec, residual, image, prec_ends, residual_ends, image_ends)
    return disp_new.transpose(1, 0, 2), residual_new.transpose(1, 0, 2), stats.reshape(3)


def solution(mesh):
    in_specs = (
        P("ax", None, "sec"),
        P("ax", None, "sec"),
        P("ax", None, "sec"),
        P("ax", "sec"),
        P("ax"),
        P(),
        P(),
    )
    out_specs = (P("ax", None, "sec"), P("ax", None, "sec"), P())
    return jax.shard_map(shards, mesh=mesh, in_specs=in_specs, out_specs=out_specs, check_vma=False)
```

time: 47.8 us -> 43.5 us (0.910)
  Pallas kernels: 14.2 us -> 11.2 us
  waiting for transfers between devices: 6.2 us -> 4.26 us
  starting transfers between devices: 10.5 us -> 11.4 us
    pallas_call x10 -> x8, Pallas kernels: 14.2 us -> 11.2 us  [the longest x2 4.09 us: transform_call(): call(functools.partial(transform_kernel, comps, main, at_end, edge_at, ho...]
    ppermute x9 -> x8, waiting for transfers between devices: 5.59 us -> 2.96 us  [to(): return lax.ppermute(x, 'sec', [(i, i ^ mask) for i in range(sec)])]
    ppermute x1, waiting for transfers between devices: 0.61 us -> 1.3 us  [shards(): after = lax.ppermute(down, 'ax', [(i + 1, i) for i in range(ax - 1)])]
    ppermute x9 -> x8, starting transfers between devices: 5.82 us -> 6.28 us  [to(): return lax.ppermute(x, 'sec', [(i, i ^ mask) for i in range(sec)])]
  transfers between devices with their start and end apart: 11 -> 10, of which waited for: 5 -> 4; matrix products, arithmetic and copies ran while one was open for 0% -> 0% of each run, Pallas kernels for 15% -> 13%
where the time goes in v4:
time: 43.5 us; the launch traced here: 43.2 us
  blocking collectives  13 us (30%)
  starting transfers between devices  11.4 us (26%)
  Pallas kernels  11.2 us (26%)
  waiting for transfers between devices  4.26 us (10%)
  local copies, waits for them, and re-layouts  2.5 us (6%)
  between operations  0.81 us (2%)
    all_to_all x1, blocking collectives, shards(): gathered = lax.all_to_all(sums, ('ax', 'sec'), 0, 0, tiled=True)  13 us
    ppermute x8, starting transfers between devices, to(): return lax.ppermute(x, 'sec', [(i, i ^ mask) for i in range(sec)])  6.28 us
    pallas_call x2, Pallas kernels, transform_call(): call(functools.partial(transform_kernel, comps, main, at_end, edge_at, ho...  4.09 us
    ppermute x1, starting transfers between devices, shards(): before = lax.ppermute(up, 'ax', [(i, i + 1) for i in range(ax - 1)])  3.8 us
    pallas_call x1, Pallas kernels, shards(): call(functools.partial(first_kernel, end, comps, ax), 'first', shapes, [H...  3.58 us
    ppermute x8, waiting for transfers between devices, to(): return lax.ppermute(x, 'sec', [(i, i ^ mask) for i in range(sec)])  2.96 us
    unnamed x28, local copies, waits for them, and re-layouts  2.5 us
    pallas_call x1, Pallas kernels, shards(): call(functools.partial(update_kernel, end, comps, cell_total), 'update',...  1.34 us
  transfers between devices with their start and end apart: 10, of which 4 were waited for; matrix products, arithmetic and copies ran while one was open for 0% of the time, Pallas kernels for 13%

profile of v4, /device:TPU:0, one launch (start us, length us, event | category | flops | bytes accessed | tf_op | source)
XLA Modules:
  0.0 43.2 jit_solution(14146905485564345915)
XLA Ops:
  0.6 0.0 copy-start.1
  0.6 0.0 copy-start.5
  0.7 0.0 copy-start.8
  0.7 0.0 copy-start.13
  0.7 3.6 %first.1 = (f32[296,256]{1,0:T(8,128)}, f32[296,256]{1,0:T(8,128)}, f32[2,112,256]{2,1,0:T(8,128)}, f32[128,128]{1,0:T(8,128)}, f32[16,256]{1,0:T(8,128)}, /*index=5*/f32[16,256]{1,0:T(8,128)}) custom-call(f32[4,6]{1,0:T(4,128)} %table_ref.1, s32[1,128]{1,0:T(1,128)} %bitcast.19, f32[6,128,256]{2,1,0:T(8,128)} %bitcast.18, f32[6,128,256]{2,1,0:T(8,128)} %bitcast.14, ...), custom_call_target="tpu_custom_call" | custom-call | flops 1966080 | bytes 1572864 | tf_op jit(solution)/shard_map/first/pallas_call | solution.py:632
  4.3 3.0 %collective-permute-start.5 = (f32[296,256]{1,0:T(8,128)}, f32[296,256]{1,0:T(8,128)S(1)}, u32[]{:S(2)}, u32[]{:S(2)}) collective-permute-start(f32[296,256]{1,0:T(8,128)} %get-tuple-element.43.own_ref), channel_id=1, source_target_pairs={{0,2},{1,3},{2,0},{3,1},{4,6},{5,7},{6,4},{7,5},{8,10},{9,11},{10,... | collective-permute-start | bytes 909320 | tf_op jit(solution)/shard_map/ppermute | solution.py:643
  7.3 0.0 collective-permute-start.4
  7.3 0.2 collective-permute-start.6
  7.5 3.8 %collective-permute-start = (f32[16,256]{1,0:T(8,128)}, f32[16,256]{1,0:T(8,128)S(1)}, u32[]{:S(2)}, u32[]{:S(2)}) collective-permute-start(f32[16,256]{1,0:T(8,128)} %get-tuple-element.39), channel_id=1, source_target_pairs={{0,4},{4,8},{8,12},{12,16},{16,20},{20,24},{24,28},{1,5},{5,9},{9,... | collective-permute-start | bytes 49160 | tf_op jit(solution)/shard_map/ppermute | solution.py:649
  11.3 1.3 %collective-permute-start.1 = (f32[16,256]{1,0:T(8,128)}, f32[16,256]{1,0:T(8,128)S(1)}, u32[]{:S(2)}, u32[]{:S(2)}) collective-permute-start(f32[16,256]{1,0:T(8,128)} %get-tuple-element.40), channel_id=1, source_target_pairs={{4,0},{8,4},{12,8},{16,12},{20,16},{24,20},{28,24},{5,1},{9,5},{13... | collective-permute-start | bytes 49160 | tf_op jit(solution)/shard_map/ppermute | solution.py:650
  12.6 0.0 copy-done.1
  12.6 0.0 copy-done.5
  12.6 0.0 copy-done.8
  12.6 0.0 copy-done.13
  12.7 0.0 copy-start.2
  12.7 1.2 %copy-done.2 = bf16[2,512,512]{2,1,0:T(8,128)(2,1)S(1)} copy-done((bf16[2,512,512]{2,1,0:T(8,128)(2,1)S(1)}, bf16[2,512,512]{2,1,0:T(8,128)(2,1)}, u32[]{:S(2)}) %copy-start.2) | copy-done | bytes 1048600
  13.9 1.2 %copy-done.7 = bf16[1024,512]{1,0:T(8,128)(2,1)S(1)} copy-done((bf16[1024,512]{1,0:T(8,128)(2,1)S(1)}, bf16[1024,512]{1,0:T(8,128)(2,1)}, u32[]{:S(2)}) %copy-start.7) | copy-done | bytes 1048600
  15.1 0.7 %fold.1 = (f32[36,8,640]{2,1,0:T(8,128)S(1)}, f32[6,8,640]{2,1,0:T(8,128)S(1)}) custom-call(f32[6,6,1024]{2,1,0:T(8,128)S(1)} %copy-done.13, bf16[1024,512]{1,0:T(8,128)(2,1)S(1)} %copy-done.7, bf16[4,2,256,256]{3,2,1,0:T(8,128)(2,1)S(1)} %copy-done.1, bf16[2,2,256,256]{3,2,1,0:T(8,128)(2,1)S(1)} %copy-done.5, bf16[2,512,512]{2,1,0:T(8,128)(2,1)S(1)} %copy-done.2, ...), custom_call_target="tpu_custom_call" | custom-call | flops 1 | bytes 1 | tf_op jit(solution)/shard_map/fold/pallas_call | solution.py:651
  15.8 0.0 copy-start.6
  15.8 0.0 collective-permute-done.before_ref
  15.9 1.3 %collective-permute-done.1.after_ref = f32[16,256]{1,0:T(8,128)S(1)} collective-permute-done((f32[16,256]{1,0:T(8,128)}, f32[16,256]{1,0:T(8,128)S(1)}, u32[]{:S(2)}, u32[]{:S(2)}) %collective-permute-start.1) | collective-permute-done | bytes 16416 | tf_op jit(solution)/shard_map/ppermute | solution.py:650
  17.2 0.0 copy-done.12
  17.2 1.6 %collective-permute-start.3 = (f32[112,256]{1,0:T(8,128)S(1)}, f32[112,256]{1,0:T(8,128)S(1)}, u32[]{:S(2)}, u32[]{:S(2)}) collective-permute-start(f32[112,256]{1,0:T(8,128)S(1)} %get-tuple-element.41.own_ref), channel_id=1, source_target_pairs={{0,2},{1,3},{2,0},{3,1},{4,6},{5,7},{6,4},{7,5},{8,10},{9,11},{10,... | collective-permute-start | bytes 344072 | tf_op jit(solution)/shard_map/ppermute | solution.py:643
  18.8 0.0 collective-permute-start.2
  18.8 0.0 collective-permute-done.5.across_ref
  18.8 0.6 %collective-permute-start.7 = (f32[112,256]{1,0:T(8,128)S(1)}, f32[112,256]{1,0:T(8,128)S(1)}, u32[]{:S(2)}, u32[]{:S(2)}) collective-permute-start(f32[112,256]{1,0:T(8,128)S(1)} %get-tuple-element.42.sent_ref), channel_id=1, source_target_pairs={{0,3},{1,2},{2,1},{3,0},{4,7},{5,6},{6,5},{7,4},{8,11},{9,10},{10,... | collective-permute-start | bytes 344072 | tf_op jit(solution)/shard_map/ppermute | solution.py:643
  19.4 0.0 collective-permute-done.4.core_ref
  19.4 2.3 %collective-permute-done.6.both_ref = f32[296,256]{1,0:T(8,128)S(1)} collective-permute-done((f32[296,256]{1,0:T(8,128)}, f32[296,256]{1,0:T(8,128)S(1)}, u32[]{:S(2)}, u32[]{:S(2)}) %collective-permute-start.6) | collective-permute-done | bytes 303136 | tf_op jit(solution)/shard_map/ppermute | solution.py:643
  21.7 0.0 copy-done.3
  21.7 0.0 copy-done.9
  21.7 0.0 copy-done.6
  21.7 2.9 %transform.2 = (f32[128,128]{1,0:T(8,128)S(1)}, f32[288,384]{1,0:T(8,128)S(1)}, f32[6,48,256]{2,1,0:T(8,128)S(1)}, f32[288,384]{1,0:T(8,128)S(1)}) custom-call(f32[296,256]{1,0:T(8,128)S(1)} %copy-done.9, f32[296,256]{1,0:T(8,128)S(1)} %collective-permute-done.4.core_ref, f32[296,256]{1,0:T(8,128)S(1)} %collective-permute-done.5.across_ref, ...), custom_call_target="tpu_custom_call" | custom-call | tf_op jit(solution)/shard_map/transform/pallas_call | solution.py:604
  24.6 0.0 collective-permute-done.3.across_ref
  24.6 0.2 collective-permute-start.8
  24.8 0.0 collective-permute-done.2.core_ref
  24.8 0.6 %collective-permute-done.7.both_ref = f32[112,256]{1,0:T(8,128)S(1)} collective-permute-done((f32[112,256]{1,0:T(8,128)S(1)}, f32[112,256]{1,0:T(8,128)S(1)}, u32[]{:S(2)}, u32[]{:S(2)}) %collective-permute-start.7) | collective-permute-done | bytes 114720 | tf_op jit(solution)/shard_map/ppermute | solution.py:643
  25.4 1.2 %transform.3 = (f32[104,384]{1,0:T(8,128)S(1)}, f32[6,16,256]{2,1,0:T(8,128)S(1)}, f32[104,384]{1,0:T(8,128)S(1)}) custom-call(f32[112,256]{1,0:T(8,128)S(1)} %get-tuple-element.41.own_ref, f32[112,256]{1,0:T(8,128)S(1)} %collective-permute-done.2.core_ref, f32[112,256]{1,0:T(8,128)S(1)} %collective-permute-done.3.across_ref, ...), custom_call_target="tpu_custom_call" | custom-call | flops 45298483200 | bytes 78643200 | tf_op jit(solution)/shard_map/transform/pallas_call | solution.py:604
  26.6 0.6 %collective-permute-start.9 = (f32[104,384]{1,0:T(8,128)S(1)}, f32[104,384]{1,0:T(8,128)S(1)}, u32[]{:S(2)}, u32[]{:S(2)}) collective-permute-start(f32[104,384]{1,0:T(8,128)S(1)} %get-tuple-element.56), channel_id=1, source_target_pairs={{0,1},{1,0},{2,3},{3,2},{4,5},{5,4},{6,7},{7,6},{8,9},{9,8},{10,11... | collective-permute-start | bytes 479240 | tf_op jit(solution)/shard_map/ppermute | solution.py:643
  27.2 0.0 collective-permute-done.8.back_ref
  27.2 0.0 copy-done
  27.2 0.0 copy-done.10
  27.2 0.0 copy-done.11
  27.2 0.9 %early.1 = (f32[6,96,384]{2,1,0:T(8,128)S(1)}, f32[6,96,256]{2,1,0:T(8,128)S(1)}, f32[6,80,256]{2,1,0:T(8,128)S(1)}, f32[40,256]{1,0:T(8,128)S(1)}) custom-call(f32[6,128,256]{2,1,0:T(8,128)S(1)} %bitcast.12, s32[128,256]{1,0:T(8,128)S(1)} %copy-done.6, f32[128,128]{1,0:T(8,128)S(1)} %copy-done.11, f32[288,384]{1,0:T(8,128)S(1)} %get-tuple-element.47.own_ref, ...), custom_call_target="tpu_custom_call" | custom-call | flops 5898240 | bytes 3145728 | tf_op jit(solution)/shard_map/early/pallas_call | solution.py:674
  28.1 0.1 collective-permute-done.9.back_ref
  28.3 0.6 %late.1 = (f32[6,32,256]{2,1,0:T(8,128)S(1)}, f32[6,32,256]{2,1,0:T(8,128)S(1)}, f32[6,48,256]{2,1,0:T(8,128)S(1)}, f32[32,128]{1,0:T(8,128)S(1)}) custom-call(f32[6,128,256]{2,1,0:T(8,128)S(1)} %bitcast.13, s32[128,256]{1,0:T(8,128)S(1)} %copy-done.6, f32[128,128]{1,0:T(8,128)S(1)} %copy-done.11, f32[6,96,384]{2,1,0:T(8,128)S(1)} %get-tuple-element.54.inner_ref, ...), custom_call_target="tpu_custom_call" | custom-call | flops 1572864 | bytes 786432 | tf_op jit(solution)/shard_map/late/pallas_call | solution.py:679
  28.8 13.0 %all_to_all.11 = f32[32,1,128]{2,1,0:T(1,128)S(1)} all-to-all(f32[32,1,128]{2,1,0:T(1,128)S(1)} %bitcast.17), channel_id=1, replica_groups=mesh['ax'=8,'sec'=4] {'ax','sec'}, dimensions={0} | all-to-all | bytes 32768 | tf_op jit(solution)/shard_map/all_to_all | solution.py:684
  41.9 0.0 copy-done.4
  41.9 1.3 %update.1 = (f32[6,128,256]{2,1,0:T(8,128)}, f32[6,128,256]{2,1,0:T(8,128)}, f32[1,3]{1,0:T(1,128)}) custom-call(f32[6,128,256]{2,1,0:T(8,128)S(1)} %bitcast.15, f32[32,128]{1,0:T(8,128)S(1)} %bitcast.16, f32[6,96,384]{2,1,0:T(8,128)S(1)} %get-tuple-element.54.inner_ref, f32[6,96,256]{2,1,0:T(8,128)S(1)} %get-tuple-element.55.inner_residual_ref, ...), custom_call_target="tpu_custom_call" | custom-call | flops 786432 | bytes 4718592 | tf_op jit(solution)/shard_map/update/pallas_call | solution.py:685
  (9 shorter events, 0.1 us)
Async XLA Ops:
  0.6 12.0 %copy-start.1 = (bf16[4,2,256,256]{3,2,1,0:T(8,128)(2,1)S(1)}, bf16[4,2,256,256]{3,2,1,0:T(8,128)(2,1)}, u32[]{:S(2)}) copy-start(bf16[4,2,256,256]{3,2,1,0:T(8,128)(2,1)} %constant.11.clone.refs_0_.forward_ref) | copy-start | bytes 3145732
  0.6 12.0 %copy-start.5 = (bf16[2,2,256,256]{3,2,1,0:T(8,128)(2,1)S(1)}, bf16[2,2,256,256]{3,2,1,0:T(8,128)(2,1)}, u32[]{:S(2)}) copy-start(bf16[2,2,256,256]{3,2,1,0:T(8,128)(2,1)} %constant.12.clone.refs_1_.even_ref) | copy-start | bytes 1572868
  0.7 12.0 %copy-start.8 = (f32[4,8,1024]{2,1,0:T(8,128)S(1)}, f32[4,8,1024]{2,1,0:T(8,128)}, u32[]{:S(2)}) copy-start(f32[4,8,1024]{2,1,0:T(8,128)} %constant.14.clone.refs_3_.beyond_ref) | copy-start | bytes 393220
  0.7 12.0 %copy-start.13 = (f32[6,6,1024]{2,1,0:T(8,128)S(1)}, f32[6,6,1024]{2,1,0:T(8,128)}, u32[]{:S(2)}) copy-start(f32[6,6,1024]{2,1,0:T(8,128)} %precond_ref.1) | copy-start | bytes 442372
  4.3 14.5 %collective-permute-start.5 = (f32[296,256]{1,0:T(8,128)}, f32[296,256]{1,0:T(8,128)S(1)}, u32[]{:S(2)}, u32[]{:S(2)}) collective-permute-start(f32[296,256]{1,0:T(8,128)} %get-tuple-element.43.own_ref), channel_id=1, source_target_pairs={{0,2},{1,3},{2,0},{3,1},{4,6},{5,7},{6,4},{7,5},{8,10},{9,11},{10,... | collective-permute-start | bytes 909320 | tf_op jit(solution)/shard_map/ppermute | solution.py:643
  7.3 12.1 %collective-permute-start.4 = (f32[296,256]{1,0:T(8,128)}, f32[296,256]{1,0:T(8,128)S(1)}, u32[]{:S(2)}, u32[]{:S(2)}) collective-permute-start(f32[296,256]{1,0:T(8,128)} %get-tuple-element.44.sent_ref), channel_id=1, source_target_pairs={{0,1},{1,0},{2,3},{3,2},{4,5},{5,4},{6,7},{7,6},{8,9},{9,8},{10,11... | collective-permute-start | bytes 909320 | tf_op jit(solution)/shard_map/ppermute | solution.py:643
  7.3 14.4 %collective-permute-start.6 = (f32[296,256]{1,0:T(8,128)}, f32[296,256]{1,0:T(8,128)S(1)}, u32[]{:S(2)}, u32[]{:S(2)}) collective-permute-start(f32[296,256]{1,0:T(8,128)} %get-tuple-element.44.sent_ref), channel_id=1, source_target_pairs={{0,3},{1,2},{2,1},{3,0},{4,7},{5,6},{6,5},{7,4},{8,11},{9,10},{10,... | collective-permute-start | bytes 909320 | tf_op jit(solution)/shard_map/ppermute | solution.py:643
  7.5 8.3 %collective-permute-start = (f32[16,256]{1,0:T(8,128)}, f32[16,256]{1,0:T(8,128)S(1)}, u32[]{:S(2)}, u32[]{:S(2)}) collective-permute-start(f32[16,256]{1,0:T(8,128)} %get-tuple-element.39), channel_id=1, source_target_pairs={{0,4},{4,8},{8,12},{12,16},{16,20},{20,24},{24,28},{1,5},{5,9},{9,... | collective-permute-start | bytes 49160 | tf_op jit(solution)/shard_map/ppermute | solution.py:649
  11.3 5.8 %collective-permute-start.1 = (f32[16,256]{1,0:T(8,128)}, f32[16,256]{1,0:T(8,128)S(1)}, u32[]{:S(2)}, u32[]{:S(2)}) collective-permute-start(f32[16,256]{1,0:T(8,128)} %get-tuple-element.40), channel_id=1, source_target_pairs={{4,0},{8,4},{12,8},{16,12},{20,16},{24,20},{28,24},{5,1},{9,5},{13... | collective-permute-start | bytes 49160 | tf_op jit(solution)/shard_map/ppermute | solution.py:650
  12.7 1.2 %copy-start.2 = (bf16[2,512,512]{2,1,0:T(8,128)(2,1)S(1)}, bf16[2,512,512]{2,1,0:T(8,128)(2,1)}, u32[]{:S(2)}) copy-start(bf16[2,512,512]{2,1,0:T(8,128)(2,1)} %constant.13.clone.refs_2_.odd_ref) | copy-start | bytes 3145732
  13.9 1.2 %copy-start.7 = (bf16[1024,512]{1,0:T(8,128)(2,1)S(1)}, bf16[1024,512]{1,0:T(8,128)(2,1)}, u32[]{:S(2)}) copy-start(bf16[1024,512]{1,0:T(8,128)(2,1)} %constant.10.clone.fold_ref) | copy-start | bytes 3145732
  15.1 2.1 %copy-start.12 = (f32[2,112,256]{2,1,0:T(8,128)S(1)}, f32[2,112,256]{2,1,0:T(8,128)}, u32[]{:S(2)}) copy-start(f32[2,112,256]{2,1,0:T(8,128)} %get-tuple-element.38.ends_ref) | copy-start | bytes 688132
  15.1 6.6 %copy-start.3 = (bf16[2,512,512]{2,1,0:T(8,128)(2,1)S(1)}, bf16[2,512,512]{2,1,0:T(8,128)(2,1)}, u32[]{:S(2)}) copy-start(bf16[2,512,512]{2,1,0:T(8,128)(2,1)} %constant.13.clone.refs_2_.odd_ref) | copy-start | bytes 3145732
  15.1 6.6 %copy-start.9 = (f32[296,256]{1,0:T(8,128)S(1)}, f32[296,256]{1,0:T(8,128)}, u32[]{:S(2)}) copy-start(f32[296,256]{1,0:T(8,128)} %get-tuple-element.43.own_ref) | copy-start | bytes 909316
  15.8 5.9 %copy-start.6 = (s32[128,256]{1,0:T(8,128)S(1)}, s32[128,256]{1,0:T(8,128)}, u32[]{:S(2)}) copy-start(s32[128,256]{1,0:T(8,128)} %hole_ref.9) | copy-start | bytes 393220
  17.2 7.4 %collective-permute-start.3 = (f32[112,256]{1,0:T(8,128)S(1)}, f32[112,256]{1,0:T(8,128)S(1)}, u32[]{:S(2)}, u32[]{:S(2)}) collective-permute-start(f32[112,256]{1,0:T(8,128)S(1)} %get-tuple-element.41.own_ref), channel_id=1, source_target_pairs={{0,2},{1,3},{2,0},{3,1},{4,6},{5,7},{6,4},{7,5},{8,10},{9,11},{10,... | collective-permute-start | bytes 344072 | tf_op jit(solution)/shard_map/ppermute | solution.py:643
  18.8 6.0 %collective-permute-start.2 = (f32[112,256]{1,0:T(8,128)S(1)}, f32[112,256]{1,0:T(8,128)S(1)}, u32[]{:S(2)}, u32[]{:S(2)}) collective-permute-start(f32[112,256]{1,0:T(8,128)S(1)} %get-tuple-element.42.sent_ref), channel_id=1, source_target_pairs={{0,1},{1,0},{2,3},{3,2},{4,5},{5,4},{6,7},{7,6},{8,9},{9,8},{10,11... | collective-permute-start | bytes 344072 | tf_op jit(solution)/shard_map/ppermute | solution.py:643
  18.8 6.6 %collective-permute-start.7 = (f32[112,256]{1,0:T(8,128)S(1)}, f32[112,256]{1,0:T(8,128)S(1)}, u32[]{:S(2)}, u32[]{:S(2)}) collective-permute-start(f32[112,256]{1,0:T(8,128)S(1)} %get-tuple-element.42.sent_ref), channel_id=1, source_target_pairs={{0,3},{1,2},{2,1},{3,0},{4,7},{5,6},{6,5},{7,4},{8,11},{9,10},{10,... | collective-permute-start | bytes 344072 | tf_op jit(solution)/shard_map/ppermute | solution.py:643
  24.6 2.7 %collective-permute-start.8 = (f32[288,384]{1,0:T(8,128)S(1)}, f32[288,384]{1,0:T(8,128)S(1)}, u32[]{:S(2)}, u32[]{:S(2)}) collective-permute-start(f32[288,384]{1,0:T(8,128)S(1)} %get-tuple-element.52), channel_id=1, source_target_pairs={{0,1},{1,0},{2,3},{3,2},{4,5},{5,4},{6,7},{7,6},{8,9},{9,8},{10,11... | collective-permute-start | bytes 1327112 | tf_op jit(solution)/shard_map/ppermute | solution.py:643
  25.4 1.9 %copy-start = (f32[128,6,256]{2,0,1:T(8,128)S(1)}, f32[128,6,256]{2,0,1:T(8,128)}, u32[]{:S(2)}) copy-start(f32[128,6,256]{2,0,1:T(8,128)} %param.14) | copy-start | bytes 2359300
  25.4 1.9 %copy-start.10 = (f32[296,256]{1,0:T(8,128)S(1)}, f32[296,256]{1,0:T(8,128)}, u32[]{:S(2)}) copy-start(f32[296,256]{1,0:T(8,128)} %get-tuple-element.44.sent_ref) | copy-start | bytes 909316
  25.4 1.9 %copy-start.11 = (f32[128,128]{1,0:T(8,128)S(1)}, f32[128,128]{1,0:T(8,128)}, u32[]{:S(2)}) copy-start(f32[128,128]{1,0:T(8,128)} %get-tuple-element.51.factor_ref) | copy-start | bytes 196612
  26.6 1.6 %collective-permute-start.9 = (f32[104,384]{1,0:T(8,128)S(1)}, f32[104,384]{1,0:T(8,128)S(1)}, u32[]{:S(2)}, u32[]{:S(2)}) collective-permute-start(f32[104,384]{1,0:T(8,128)S(1)} %get-tuple-element.56), channel_id=1, source_target_pairs={{0,1},{1,0},{2,3},{3,2},{4,5},{5,4},{6,7},{7,6},{8,9},{9,8},{10,11... | collective-permute-start | bytes 479240 | tf_op jit(solution)/shard_map/ppermute | solution.py:643
  28.3 13.6 %copy-start.4 = (f32[128,6,256]{2,0,1:T(8,128)S(1)}, f32[128,6,256]{2,0,1:T(8,128)}, u32[]{:S(2)}) copy-start(f32[128,6,256]{2,0,1:T(8,128)} %param.13) | copy-start | bytes 2359300

commit v5 on v4

--- a/solution.py
+++ b/solution.py
@@ -47,17 +47,11 @@
     ends = np.array([around - 1, 2 * width, around - width - 1, width])
     beyond = np.repeat(wave(ends, shift).astype(np.float32)[:, None, :], TILE, axis=1)
     odd = np.concatenate([direct.T, wave(place + width, shift).T], axis=1)[2 * width :]
-    fold = np.zeros((around, 4 * half))
-    kinds = [4 * np.arange(half), 4 * np.arange(half) + 2, 8 * np.arange(half) + 1, 8 * np.arange(half) + 5]
-    for column, k in enumerate(np.concatenate(kinds)):
-        for place in {k, (around - k) % around}:
-            fold[place, column] = 1.0 / around
     return (
         np.stack([two_parts(t) for t in forward]),
         np.stack([two_parts(t) for t in (direct.T[:width], direct.T[width : 2 * width])]),
         two_parts(odd),
         beyond,
-        fold.astype(ml_dtypes.bfloat16),
     )
 
 
@@ -96,7 +90,7 @@
     return up + down
 
 
-def fold_kernel(precond_ref, fold_ref, *refs):
+def fold_kernel(precond_ref, *refs):
     out_ref, beyond_ref = refs[-2:]
     comps = precond_ref.shape[0]
     value = jnp.concatenate([precond_ref[q] for q in range(comps)], axis=0)
@@ -105,9 +99,14 @@
     rest = value - high.astype(F32)
     middle = rest.astype(BF16)
     low = (rest - middle.astype(F32)).astype(BF16)
-    terms = [jnp.dot(t, fold_ref[...], preferred_element_type=F32) for t in (high, middle, low)]
+    half = around // 8
+    row, step = rows_of((around, half)), lanes_of((around, half))
+    kinds = []
+    for k in (4 * step, 4 * step + 2, 8 * step + 1, 8 * step + 5):
+        kinds.append(jnp.where((row == k) | (row == around - k), F32(1.0 / around), 0.0).astype(BF16))
+    fold = jnp.concatenate(kinds, axis=1)
+    terms = [jnp.dot(t, fold, preferred_element_type=F32) for t in (high, middle, low)]
     folded = terms[0] + (terms[1] + terms[2])
-    half = folded.shape[1] // 4
     zero = folded[:, :half]
     top = value[:, around // 2 : around // 2 + 1] * F32(1.0 / around)
     other = jnp.where(lanes_of(zero.shape) == 0, top, zero)
@@ -153,10 +152,72 @@
     return table[:TILE], table[TILE : 2 * TILE]
 
 
+def copy(src, dst, sem):
+    moving = pltpu.make_async_copy(src, dst, sem)
+    moving.start()
+    return moving
+
+
 def first_kernel(
+    end, comps, ax_size, table_ref, class_ref, load_ref, disp_ref, stiff_ref, hole_ref, keep_ref,
+    table_in, class_in, load_in, disp_in, stiff_in, hole_in, keep_out, factor_in, in_sems, out_sems,
+):
+    slab, width = hole_ref.shape
+    half = slab // 2
+    inner, reach = half - end, half + TILE
+    core = lax.axis_index("sec") % 2
+    base = pl.multiple_of((half - TILE) * core, TILE)
+    start = pl.multiple_of(end + inner * core, TILE)
+    here = pl.ds(pl.multiple_of(end - (end - TILE) * core, TILE), inner)
+    around = pl.ds(pl.multiple_of(end - TILE - (end - TILE) * core, TILE), inner + 2 * TILE)
+    tail = pl.ds(pl.multiple_of((reach - end) * core, TILE), end)
+    small = [
+        copy(class_ref, class_in, in_sems.at[0]),
+        copy(table_ref, table_in, in_sems.at[1]),
+        copy(hole_ref.at[pl.ds(base, reach)], hole_in, in_sems.at[2]),
+    ]
+    pairs = comps // 2
+    moving = []
+    for g in range(pairs):
+        both = pl.ds(2 * g, 2)
+        arrays = (
+            (disp_ref.at[both, pl.ds(base, reach)], disp_in), (load_ref.at[both, pl.ds(start, inner)], load_in),
+            (stiff_ref.at[both, pl.ds(start, inner)], stiff_in),
+        )
+        moving.append([copy(src, dst.at[both], in_sems.at[3 + 3 * g + k]) for k, (src, dst) in enumerate(arrays)])
+    for one in small:
+        one.wait()
+    factor_in[...] = factor_columns(table_in, class_in, ax_size, comps)
+    factor = factor_in[pl.ds(start, inner), :]
+    solid = (1 - hole_in[here, :]).astype(F32)
+    solid_tail = (1 - hole_in[tail, :]).astype(F32)
+    inside = slice(TILE, TILE + inner)
+    leaving = []
+    for g in range(pairs):
+        moving[g][0].wait()
+        if g == pairs - 1:
+            fields = [jnp.concatenate([disp_in[q, here], disp_in[q, tail]], axis=0) for q in range(comps)]
+            last = pl.ds(comps * inner, TILE)
+            keep_out[last, :] = jnp.concatenate(
+                edge_rows(fields, jnp.concatenate([solid, solid_tail], axis=0)), axis=1
+            )
+            leaving.append(copy(keep_out.at[last], keep_ref.at[last], out_sems.at[pairs]))
+        moving[g][1].wait()
+        moving[g][2].wait()
+        for q in (2 * g, 2 * g + 1):
+            keep_out[pl.ds(q * inner, inner), :] = local_part(
+                q, disp_in[q, around], inside, solid, factor, load_in[q], stiff_in[q], disp_in[q ^ 1, around]
+            )
+        rows = pl.ds(2 * g * inner, 2 * inner)
+        leaving.append(copy(keep_out.at[rows], keep_ref.at[rows], out_sems.at[g]))
+    for one in leaving:
+        one.wait()
+
+
+def second_kernel(
     end, comps, ax_size, table_ref, class_ref, load_ref, disp_ref, stiff_ref, hole_ref,
-    keep_ref, other_ref, ends_ref, factor_ref, up_ref, down_ref,
-    table_in, class_in, load_in, disp_in, stiff_in, hole_in, inner_out, ends_out, factor_out, up_out, down_out,
+    other_ref, ends_ref, factor_ref, near_ref, next_ref,
+    table_in, class_in, load_in, disp_in, stiff_in, hole_in, inner_out, ends_out, factor_out, message_out,
     in_sems, out_sems,
 ):
     slab, width = hole_ref.shape
@@ -164,82 +225,88 @@
     inner = half - end
     core = lax.axis_index("sec") % 2
 
-    def copy(src, dst, sems, i):
-        moving = pltpu.make_async_copy(src, dst, sems.at[i])
-        moving.start()
-        return moving
-
     small = [
-        copy(class_ref, class_in, in_sems, 0), copy(table_ref, table_in, in_sems, 1), copy(hole_ref, hole_in, in_sems, 2)
+        copy(class_ref, class_in, in_sems.at[0]), copy(table_ref, table_in, in_sems.at[1]), copy(hole_ref, hole_in, in_sems.at[2])
     ]
+    pairs = comps // 2
     moving = []
-    for q in range(comps):
-        pairs = ((disp_ref, disp_in), (load_ref, load_in), (stiff_ref, stiff_in))
-        moving.append([copy(src.at[q], dst.at[q], in_sems, 3 + 3 * q + k) for k, (src, dst) in enumerate(pairs)])
+    for g in range(pairs):
+        both = pl.ds(2 * g, 2)
+        arrays = ((disp_ref, disp_in), (load_ref, load_in), (stiff_ref, stiff_in))
+        moving.append([copy(src.at[both], dst.at[both], in_sems.at[3 + 3 * g + k]) for k, (src, dst) in enumerate(arrays)])
     for one in small:
         one.wait()
     factor_out[...] = factor_columns(table_in, class_in, ax_size, comps)
-    leaving = [copy(factor_out, factor_ref, out_sems, 0)]
+    leaving = [copy(factor_out, factor_ref, out_sems.at[0])]
     solid = (1 - hole_in[...]).astype(F32)
+    spare = TILE - comps
+    for h, row in ((0, 0), (1, slab - 1)):
+        message_out[h, comps:TILE, :] = jnp.broadcast_to(solid[row : row + 1], (spare, width))
+        message_out[h, TILE + comps :, :] = jnp.zeros((spare, width), F32)
     factor = factor_out[...]
-    for q in range(comps):
-        if q % 2 == 0:
-            for one in moving[q] + moving[q + 1]:
-                one.wait()
-        field = disp_in[q]
-        part = local_part(q, field, slice(0, slab), solid, factor, load_in[q], stiff_in[q], disp_in[q ^ 1])
-        rows = pl.ds(q * inner, inner)
-        inner_out[0, rows, :] = part[end:half]
-        inner_out[1, rows, :] = part[half : slab - end]
-        leaving.append(copy(inner_out.at[core, rows], keep_ref.at[rows], out_sems, 1 + 2 * q))
-        leaving.append(copy(inner_out.at[1 - core, rows], other_ref.at[rows], out_sems, 2 + 2 * q))
-        rows = pl.ds(q * end, end)
-        ends_out[0, rows, :] = part[:end]
-        ends_out[1, rows, :] = part[slab - end :]
-        up_out[q : q + 1, :] = part[slab - 1 :]
-        down_out[q : q + 1, :] = part[:1]
-        up_out[TILE + q : TILE + q + 1, :] = field[slab - 1 :]
-        down_out[TILE + q : TILE + q + 1, :] = field[:1]
-    spare = TILE - comps
-    for ref, row in ((up_out, slab - 1), (down_out, 0)):
-        ref[comps:TILE, :] = jnp.broadcast_to(solid[row : row + 1], (spare, width))
-        ref[TILE + comps :, :] = jnp.zeros((spare, width), F32)
-    count = 1 + 2 * comps
-    leaving.append(copy(up_out, up_ref, out_sems, count))
-    leaving.append(copy(down_out, down_ref, out_sems, count + 1))
 
     def ordered(x):
         return jnp.concatenate([x[end:half], x[:end], x[half:]], axis=0)
 
-    edges = edge_rows([ordered(disp_in[q]) for q in range(comps)], ordered(solid))
-    last = pl.ds(comps * inner, TILE)
+    for g in range(pairs):
+        moving[g][0].wait()
+        if g == pairs - 1:
+            edges = edge_rows([ordered(disp_in[q]) for q in range(comps)], ordered(solid))
+            last = pl.ds(comps * inner, TILE)
+            for h in range(2):
+                inner_out[h, last, :] = jnp.concatenate(
+                    [pltpu.roll(x, (LANES - half * h) % LANES, 1) for x in edges], axis=1
+                )
+            leaving.append(copy(inner_out.at[1 - core, last], other_ref.at[last], out_sems.at[2]))
+        moving[g][1].wait()
+        moving[g][2].wait()
+        for q in (2 * g, 2 * g + 1):
+            field = disp_in[q]
+            part = local_part(q, field, slice(0, slab), solid, factor, load_in[q], stiff_in[q], disp_in[q ^ 1])
+            rows = pl.ds(q * inner, inner)
+            inner_out[0, rows, :] = part[end:half]
+            inner_out[1, rows, :] = part[half : slab - end]
+            rows = pl.ds(q * end, end)
+            ends_out[0, rows, :] = part[:end]
+            ends_out[1, rows, :] = part[slab - end :]
+            for h, row in ((0, slice(0, 1)), (1, slice(slab - 1, slab))):
+                message_out[h, q : q + 1, :] = part[row]
+                message_out[h, TILE + q : TILE + q + 1, :] = field[row]
+        rows = pl.ds(2 * g * inner, 2 * inner)
+        leaving.append(copy(inner_out.at[1 - core, rows], other_ref.at[rows], out_sems.at[4 + 2 * g]))
+    count = 3 + 2 * pairs
+    side = lax.axis_index("ax") % 2
+    leaving.append(copy(message_out.at[1 - side], near_ref, out_sems.at[count]))
+    leaving.append(copy(message_out.at[side], next_ref, out_sems.at[count + 1]))
     for h in range(2):
-        inner_out[h, last, :] = jnp.concatenate([pltpu.roll(x, (LANES - half * h) % LANES, 1) for x in edges], axis=1)
-        ends_out[h, pl.ds(comps * end, 2 * TILE), :] = (down_out, up_out)[h][...]
-    leaving.append(copy(inner_out.at[core, last], keep_ref.at[last], out_sems, count + 2))
-    leaving.append(copy(inner_out.at[1 - core, last], other_ref.at[last], out_sems, count + 3))
-    leaving.append(copy(ends_out, ends_ref, out_sems, count + 4))
+        ends_out[h, pl.ds(comps * end, 2 * TILE), :] = message_out[h]
+    leaving.append(copy(ends_out, ends_ref, out_sems.at[count + 2]))
     for one in leaving:
         one.wait()
 
 
-def ends_kernel(comps, ends_ref, before_ref, after_ref, keep_ref, other_ref, out_ref):
+def ends_kernel(comps, ends_ref, near_ref, next_ref, keep_ref, other_ref, out_ref):
     rows = (ends_ref.shape[1] - 2 * TILE) // comps
     width = ends_ref.shape[2]
     row = rows_of((rows, width))
+    spot, place = rows_of((TILE, width)), lanes_of((TILE, width))
     core = lax.axis_index("sec") % 2
-    for h, far_ref, at in ((0, before_ref, 0), (1, after_ref, rows - 1)):
+    odd = lax.axis_index("ax") % 2 == 1
+    near, other = near_ref[...], next_ref[...]
+    for h, far, at in ((0, jnp.where(odd, near, other), 0), (1, jnp.where(odd, other, near), rows - 1)):
         own_ref = ends_ref.at[h, pl.ds(comps * rows, 2 * TILE)]
         solid_own = own_ref[comps : comps + 1]
-        far = far_ref[...]
         for q in range(comps):
             part = ends_ref[h, pl.ds(q * rows, rows), :]
             part = part + jnp.where(row == at, solid_own * far[TILE + q : TILE + q + 1], 0.0)
             out_ref[h, pl.ds(q * rows, rows), :] = part
-        solid_far = far[comps : comps + 1]
-        residual = far[:TILE] + solid_far * own_ref[TILE:]
-        out_ref[h, pl.ds(comps * rows, TILE), :] = jnp.where(rows_of(residual.shape) < comps, residual, solid_far)
-        out_ref[h, pl.ds(comps * rows + TILE, TILE), :] = far[TILE:]
+        solid_far, disp_far = far[comps : comps + 1], far[TILE:]
+        edges = jnp.where(place == spot, disp_far[:, :1], 0.0)
+        edges = edges + jnp.where(place == spot + TILE, disp_far[:, width - 1 :], 0.0)
+        edges = jnp.sum(edges, axis=0, keepdims=True)
+        beyond = far[:TILE] + solid_far * own_ref[TILE:]
+        beyond = jnp.where(spot < comps, beyond, jnp.where(spot == TILE - 1, edges, solid_far))
+        out_ref[h, pl.ds(comps * rows, TILE), :] = beyond
     keep_ref[...] = out_ref[core]
     other_ref[...] = out_ref[1 - core]
 
@@ -320,16 +387,17 @@
 
     def arrays_beyond():
         tiles = in_order(odd, *[r[pl.ds(total, TILE), :] for r in sources])
-        disp = in_order(odd, *[r[pl.ds(total + TILE, TILE), :] for r in sources])
-        place = lanes_of((TILE, width))
+        spot, place = rows_of((TILE, width)), lanes_of((TILE, width))
+
+        def column(tile, at):
+            return jnp.sum(jnp.where(place == spot + at, tile[TILE - 1 :], 0.0), axis=1, keepdims=True)
+
         fixed = []
         for s in range(SECTORS):
-            beside = jnp.where(place == 0, pltpu.roll(disp[s - 1], 1, 1), 0.0)
-            beside = beside + jnp.where(
-                place == width - 1, pltpu.roll(disp[(s + 1) % SECTORS], width - 1, 1), 0.0
-            )
+            beside = jnp.where(place == 0, column(tiles[s - 1], TILE), 0.0)
+            beside = beside + jnp.where(place == width - 1, column(tiles[(s + 1) % SECTORS], 0), 0.0)
             value = tiles[s] + tiles[s][comps : comps + 1] * beside
-            fixed.append(jnp.where(rows_of((TILE, width)) < comps, value, 0.0))
+            fixed.append(jnp.where(spot < comps, value, 0.0))
         return turned(*butterfly(*fixed))
 
     def put(at, arrays):
@@ -580,12 +648,12 @@
 FULL = 62
 
 
-def call(kernel, name, out_shapes, in_specs, flops, moved, scratch=(), grant=32, out_spec=None):
+def call(kernel, name, out_shapes, in_specs, flops, moved, scratch=(), grant=32, out_specs=None):
     return pl.pallas_call(
         kernel,
         out_shape=[jax.ShapeDtypeStruct(s, F32) for s in out_shapes],
         in_specs=in_specs,
-        out_specs=[out_spec or VMEM] * len(out_shapes),
+        out_specs=out_specs or [VMEM] * len(out_shapes),
         scratch_shapes=list(scratch),
         compiler_params=pltpu.CompilerParams(vmem_limit_bytes=grant * 1024 * 1024),
         cost_estimate=pl.CostEstimate(flops=flops, bytes_accessed=moved, transcendentals=0),
@@ -622,22 +690,32 @@
     end = slab // 16 * 2
     inner = slab // 2 - end
     load, disp, stiff = [x.transpose(1, 0, 2) for x in (load, disp, stiff)]
-    forward, even, odd, beyond, fold = harmonic_tables(width)
+    forward, even, odd, beyond = harmonic_tables(width)
     block = 4 * comps * slab * width
     classes = section_class.reshape(1, slab)
 
     sent = (comps * inner + TILE, width)
     ends_shape = (2, comps * end + 2 * TILE, width)
-    shapes = [sent, sent, ends_shape, (slab, LANES), (2 * TILE, width), (2 * TILE, width)]
-    keep, other, edge, factor, up, down = call(
+    shapes = [sent, ends_shape, (slab, LANES), (2 * TILE, width), (2 * TILE, width)]
+    small = [pltpu.SMEM(class_table.shape, F32), pltpu.VMEM((1, slab), jnp.int32)]
+    arguments = (class_table, classes, load, disp, stiff, hole)
+    reach = slab // 2 + TILE
+    (keep,) = call(
         functools.partial(first_kernel, end, comps, ax), "first",
+        [sent], [HBM] * 6, 10 * comps * inner * width, block,
+        small + [pltpu.VMEM((comps, rows, width), F32) for rows in (inner, reach, inner)]
+        + [pltpu.VMEM((reach, width), jnp.int32), pltpu.VMEM(sent, F32), pltpu.VMEM((slab, LANES), F32)]
+        + [pltpu.SemaphoreType.DMA((3 + 3 * comps // 2,)), pltpu.SemaphoreType.DMA((1 + comps // 2,))],
+        FULL, [HBM],
+    )(*arguments)
+    other, edge, factor, near, other_side = call(
+        functools.partial(second_kernel, end, comps, ax), "second",
         shapes, [HBM] * 6, 10 * comps * slab * width, 2 * block,
-        [pltpu.SMEM(class_table.shape, F32), pltpu.VMEM((1, slab), jnp.int32)]
-        + [pltpu.VMEM((comps, slab, width), F32)] * 3 + [pltpu.VMEM((slab, width), jnp.int32)]
-        + [pltpu.VMEM((2,) + sent, F32)] + [pltpu.VMEM(shape, F32) for shape in shapes[2:]]
-        + [pltpu.SemaphoreType.DMA((3 + 3 * comps,)), pltpu.SemaphoreType.DMA((6 + 2 * comps,))],
-        FULL, HBM,
-    )(class_table, classes, load, disp, stiff, hole)
+        small + [pltpu.VMEM((comps, slab, width), F32)] * 3 + [pltpu.VMEM((slab, width), jnp.int32)]
+        + [pltpu.VMEM((2,) + sent, F32)] + [pltpu.VMEM(shape, F32) for shape in shapes[1:3] + [(2, 2 * TILE, width)]]
+        + [pltpu.SemaphoreType.DMA((3 + 3 * comps // 2,)), pltpu.SemaphoreType.DMA((6 + comps,))],
+        FULL, [HBM] * len(shapes),
+    )(*arguments)
 
     def to(x, mask):
         return lax.ppermute(x, "sec", [(i, i ^ mask) for i in range(sec)])
@@ -646,17 +724,17 @@
         return keep, to(other, 1), to(keep, 2), to(other, 3)
 
     blocks = gather(keep, other)
-    before = lax.ppermute(up, "ax", [(i, i + 1) for i in range(ax - 1)])
-    after = lax.ppermute(down, "ax", [(i + 1, i) for i in range(ax - 1)])
+    near = lax.ppermute(near, "ax", [(i, i ^ 1) for i in range(ax)])
+    other_side = lax.ppermute(other_side, "ax", [(i, ((i + 1) ^ 1) - 1) for i in range(1, ax - 1)])
     weight, beyond_weight = call(
-        fold_kernel, "fold", [(comps * comps, TILE, 5 * width // 2), (comps, TILE, 5 * width // 2)], [VMEM] * 6,
+        fold_kernel, "fold", [(comps * comps, TILE, 5 * width // 2), (comps, TILE, 5 * width // 2)], [VMEM] * 5,
         1, 1,
-    )(precond, fold, forward, even, odd, beyond)
-    rows = (comps * end + 2 * TILE, width)
+    )(precond, forward, even, odd, beyond)
+    rows = (comps * end + TILE, width)
     keep_ends, other_ends = call(
         functools.partial(ends_kernel, comps), "ends",
         [rows, rows], [VMEM] * 3, 2 * comps * end * width, 16 * comps * end * width, [pltpu.VMEM((2,) + rows, F32)],
-    )(after_all(edge, weight), before, after)
+    )(after_all(edge, weight), near, other_side)
     end_blocks = gather(keep_ends, other_ends)
     tables = (forward, even, odd, beyond, weight, beyond_weight)
 

time: 43.5 us -> 42.2 us (0.970)
  starting transfers between devices: 11.4 us -> 8.67 us
  Pallas kernels: 11.2 us -> 13.9 us
  waiting for transfers between devices: 4.26 us -> 3.22 us
    ppermute x2, starting transfers between devices: 5.09 us -> 2.53 us  [the longest x1 1.88 us: shards(): near = lax.ppermute(near, 'ax', [(i, i ^ 1) for i in range(ax)])]
    pallas_call x1 -> x2, Pallas kernels: 3.58 us -> 5.95 us  [the longest x1 3.4 us: shards(): call(functools.partial(second_kernel, end, comps, ax), 'second', shapes,...]
    ppermute x2, waiting for transfers between devices: 1.3 us -> 0.01 us  [the longest x1 0.01 us: shards(): near = lax.ppermute(near, 'ax', [(i, i ^ 1) for i in range(ax)])]
    unnamed x28 -> x26, local copies, waits for them, and re-layouts: 2.5 us -> 2.2 us
  transfers between devices with their start and end apart: 10 -> 10, of which waited for: 4 -> 3; matrix products, arithmetic and copies ran while one was open for 0% -> 0% of each run, Pallas kernels for 13% -> 22%
where the time goes in v5:
time: 42.2 us; the launch traced here: 42 us
  Pallas kernels  13.9 us (33%)
  blocking collectives  13.2 us (31%)
  starting transfers between devices  8.67 us (21%)
  waiting for transfers between devices  3.22 us (8%)
  local copies, waits for them, and re-layouts  2.2 us (5%)
  between operations  0.82 us (2%)
    all_to_all x1, blocking collectives, shards(): gathered = lax.all_to_all(sums, ('ax', 'sec'), 0, 0, tiled=True)  13.2 us
    ppermute x8, starting transfers between devices, to(): return lax.ppermute(x, 'sec', [(i, i ^ mask) for i in range(sec)])  6.14 us
    pallas_call x2, Pallas kernels, transform_call(): call(functools.partial(transform_kernel, comps, main, at_end, edge_at, ho...  4.04 us
    pallas_call x1, Pallas kernels, shards(): call(functools.partial(second_kernel, end, comps, ax), 'second', shapes,...  3.4 us
    ppermute x8, waiting for transfers between devices, to(): return lax.ppermute(x, 'sec', [(i, i ^ mask) for i in range(sec)])  3.21 us
    pallas_call x1, Pallas kernels, shards(): call(functools.partial(first_kernel, end, comps, ax), 'first', [sent], [H...  2.55 us
    unnamed x26, local copies, waits for them, and re-layouts  2.2 us
    ppermute x1, starting transfers between devices, shards(): near = lax.ppermute(near, 'ax', [(i, i ^ 1) for i in range(ax)])  1.88 us
  transfers between devices with their start and end apart: 10, of which 3 were waited for; matrix products, arithmetic and copies ran while one was open for 0% of the time, Pallas kernels for 22%

profile of v5, /device:TPU:0, one launch (start us, length us, event | category | flops | bytes accessed | tf_op | source)
XLA Modules:
  0.0 42.0 jit_solution(15454067181549170745)
XLA Ops:
  0.6 2.5 %first.1.own_ref = f32[296,256]{1,0:T(8,128)} custom-call(f32[4,6]{1,0:T(4,128)} %table_ref.3, s32[1,128]{1,0:T(1,128)} %bitcast.22, f32[6,128,256]{2,1,0:T(8,128)} %bitcast.20, f32[6,128,256]{2,1,0:T(8,128)} %bitcast.15, f32[6,128,256]{2,1,0:T(8,128)} %bitcast.11, s32[128,256]{1,0:T(8,128)} %hole_ref.11), custom_call_target="tpu_custom_call" | custom-call | flops 737280 | bytes 786432 | tf_op jit(solution)/shard_map/first/pallas_call | solution.py:703
  3.2 0.0 copy-start.2
  3.2 0.0 copy-start.6
  3.2 0.0 copy-start.8
  3.2 3.0 %collective-permute-start.5 = (f32[296,256]{1,0:T(8,128)}, f32[296,256]{1,0:T(8,128)S(1)}, u32[]{:S(2)}, u32[]{:S(2)}) collective-permute-start(f32[296,256]{1,0:T(8,128)} %first.1.own_ref), channel_id=1, source_target_pairs={{0,2},{1,3},{2,0},{3,1},{4,6},{5,7},{6,4},{7,5},{8,10},{9,11},{10,... | collective-permute-start | bytes 909320 | tf_op jit(solution)/shard_map/ppermute | solution.py:721
  6.3 3.4 %second.1 = (f32[296,256]{1,0:T(8,128)}, f32[2,112,256]{2,1,0:T(8,128)}, f32[128,128]{1,0:T(8,128)}, f32[16,256]{1,0:T(8,128)}, f32[16,256]{1,0:T(8,128)}) custom-call(f32[4,6]{1,0:T(4,128)} %table_ref.3, s32[1,128]{1,0:T(1,128)} %bitcast.23, f32[6,128,256]{2,1,0:T(8,128)} %bitcast.21, f32[6,128,256]{2,1,0:T(8,128)} %bitcast.16, f32[6,128,256]{2,1,0:T(8,128)} %bitcast.12, ...), custom_call_target="tpu_custom_call" | custom-call | flops 1966080 | bytes 1572864 | tf_op jit(solution)/shard_map/second/pallas_call | solution.py:711
  9.7 0.1 collective-permute-start.6
  9.7 0.2 collective-permute-start.4
  10.0 1.9 %collective-permute-start = (f32[16,256]{1,0:T(8,128)}, f32[16,256]{1,0:T(8,128)S(1)}, u32[]{:S(2)}, u32[]{:S(2)}) collective-permute-start(f32[16,256]{1,0:T(8,128)} %get-tuple-element.38), channel_id=1, source_target_pairs={{0,4},{4,0},{8,12},{12,8},{16,20},{20,16},{24,28},{28,24},{1,5},{5... | collective-permute-start | bytes 49160 | tf_op jit(solution)/shard_map/ppermute | solution.py:727
  11.8 0.7 %collective-permute-start.1 = (f32[16,256]{1,0:T(8,128)}, f32[16,256]{1,0:T(8,128)S(1)}, u32[]{:S(2)}, u32[]{:S(2)}) collective-permute-start(f32[16,256]{1,0:T(8,128)} %get-tuple-element.39), channel_id=1, source_target_pairs={{4,8},{8,4},{12,16},{16,12},{20,24},{24,20},{5,9},{9,5},{13,17},{1... | collective-permute-start | bytes 49160 | tf_op jit(solution)/shard_map/ppermute | solution.py:728
  12.5 0.0 copy-done.2
  12.5 0.0 copy-done.6
  12.5 0.0 copy-done.8
  12.5 0.0 copy-start.3
  12.5 1.2 %copy-done.3 = bf16[4,2,256,256]{3,2,1,0:T(8,128)(2,1)S(1)} copy-done((bf16[4,2,256,256]{3,2,1,0:T(8,128)(2,1)S(1)}, bf16[4,2,256,256]{3,2,1,0:T(8,128)(2,1)}, u32[]{:S(2)}) %copy-start.3) | copy-done | bytes 1048600
  13.8 0.9 %copy-done.12 = f32[6,6,1024]{2,1,0:T(8,128)S(1)} copy-done((f32[6,6,1024]{2,1,0:T(8,128)S(1)}, f32[6,6,1024]{2,1,0:T(8,128)}, u32[]{:S(2)}) %copy-start.12) | copy-done | bytes 147480
  14.7 1.0 %fold.1 = (f32[36,8,640]{2,1,0:T(8,128)S(1)}, f32[6,8,640]{2,1,0:T(8,128)S(1)}) custom-call(f32[6,6,1024]{2,1,0:T(8,128)S(1)} %copy-done.12, bf16[4,2,256,256]{3,2,1,0:T(8,128)(2,1)S(1)} %copy-done.3, bf16[2,2,256,256]{3,2,1,0:T(8,128)(2,1)S(1)} %copy-done.6, bf16[2,512,512]{2,1,0:T(8,128)(2,1)S(1)} %copy-done.2, f32[4,8,1024]{2,1,0:T(8,128)S(1)} %copy-done.8), custom_call_target="tpu_custom_call" | custom-call | flops 1 | bytes 1 | tf_op jit(solution)/shard_map/fold/pallas_call | solution.py:729
  15.7 0.0 copy-start.5
  15.7 0.0 collective-permute-done.near_ref
  15.7 0.0 collective-permute-done.1.next_ref
  15.7 0.0 copy-done.11
  15.7 0.1 ends.1
  15.8 1.6 %collective-permute-start.3 = (f32[104,256]{1,0:T(8,128)S(1)}, f32[104,256]{1,0:T(8,128)S(1)}, u32[]{:S(2)}, u32[]{:S(2)}) collective-permute-start(f32[104,256]{1,0:T(8,128)S(1)} %get-tuple-element.40.own_ref), channel_id=1, source_target_pairs={{0,2},{1,3},{2,0},{3,1},{4,6},{5,7},{6,4},{7,5},{8,10},{9,11},{10,... | collective-permute-start | bytes 319496 | tf_op jit(solution)/shard_map/ppermute | solution.py:721
  17.4 0.0 collective-permute-start.7
  17.4 0.0 collective-permute-done.5.across_ref
  17.4 0.6 %collective-permute-start.2 = (f32[104,256]{1,0:T(8,128)S(1)}, f32[104,256]{1,0:T(8,128)S(1)}, u32[]{:S(2)}, u32[]{:S(2)}) collective-permute-start(f32[104,256]{1,0:T(8,128)S(1)} %get-tuple-element.41.sent_ref), channel_id=1, source_target_pairs={{0,1},{1,0},{2,3},{3,2},{4,5},{5,4},{6,7},{7,6},{8,9},{9,8},{10,11... | collective-permute-start | bytes 319496 | tf_op jit(solution)/shard_map/ppermute | solution.py:721
  18.0 2.6 %collective-permute-done.6.both_ref = f32[296,256]{1,0:T(8,128)S(1)} collective-permute-done((f32[296,256]{1,0:T(8,128)}, f32[296,256]{1,0:T(8,128)S(1)}, u32[]{:S(2)}, u32[]{:S(2)}) %collective-permute-start.6) | collective-permute-done | bytes 303136 | tf_op jit(solution)/shard_map/ppermute | solution.py:721
  20.7 0.0 collective-permute-done.4.core_ref
  20.7 0.0 copy-done.4
  20.7 0.0 copy-done.7
  20.7 0.0 copy-done.5
  20.7 2.8 %transform.2 = (f32[128,128]{1,0:T(8,128)S(1)}, f32[288,384]{1,0:T(8,128)S(1)}, f32[6,48,256]{2,1,0:T(8,128)S(1)}, f32[288,384]{1,0:T(8,128)S(1)}) custom-call(f32[296,256]{1,0:T(8,128)S(1)} %copy-done.7, f32[296,256]{1,0:T(8,128)S(1)} %collective-permute-done.4.core_ref, f32[296,256]{1,0:T(8,128)S(1)} %collective-permute-done.5.across_ref, ...), custom_call_target="tpu_custom_call" | custom-call | tf_op jit(solution)/shard_map/transform/pallas_call | solution.py:672
  23.5 0.0 collective-permute-done.3.across_ref
  23.5 0.1 collective-permute-start.8
  23.6 0.5 %collective-permute-done.7.both_ref = f32[104,256]{1,0:T(8,128)S(1)} collective-permute-done((f32[104,256]{1,0:T(8,128)S(1)}, f32[104,256]{1,0:T(8,128)S(1)}, u32[]{:S(2)}, u32[]{:S(2)}) %collective-permute-start.7) | collective-permute-done | bytes 106528 | tf_op jit(solution)/shard_map/ppermute | solution.py:721
  24.1 0.0 collective-permute-done.2.core_ref
  24.1 1.2 %transform.3 = (f32[104,384]{1,0:T(8,128)S(1)}, f32[6,16,256]{2,1,0:T(8,128)S(1)}, f32[104,384]{1,0:T(8,128)S(1)}) custom-call(f32[104,256]{1,0:T(8,128)S(1)} %get-tuple-element.40.own_ref, f32[104,256]{1,0:T(8,128)S(1)} %collective-permute-done.2.core_ref, f32[104,256]{1,0:T(8,128)S(1)} %collective-permute-done.3.across_ref, ...), custom_call_target="tpu_custom_call" | custom-call | flops 45298483200 | bytes 78643200 | tf_op jit(solution)/shard_map/transform/pallas_call | solution.py:672
  25.3 0.5 %collective-permute-start.9 = (f32[104,384]{1,0:T(8,128)S(1)}, f32[104,384]{1,0:T(8,128)S(1)}, u32[]{:S(2)}, u32[]{:S(2)}) collective-permute-start(f32[104,384]{1,0:T(8,128)S(1)} %get-tuple-element.54), channel_id=1, source_target_pairs={{0,1},{1,0},{2,3},{3,2},{4,5},{5,4},{6,7},{7,6},{8,9},{9,8},{10,11... | collective-permute-start | bytes 479240 | tf_op jit(solution)/shard_map/ppermute | solution.py:721
  25.8 0.0 collective-permute-done.8.back_ref
  25.8 0.0 copy-done
  25.9 0.0 copy-done.9
  25.9 0.0 copy-done.10
  25.9 0.9 %early.1 = (f32[6,96,384]{2,1,0:T(8,128)S(1)}, f32[6,96,256]{2,1,0:T(8,128)S(1)}, f32[6,80,256]{2,1,0:T(8,128)S(1)}, f32[40,256]{1,0:T(8,128)S(1)}) custom-call(f32[6,128,256]{2,1,0:T(8,128)S(1)} %bitcast.13, s32[128,256]{1,0:T(8,128)S(1)} %copy-done.5, f32[128,128]{1,0:T(8,128)S(1)} %copy-done.10, f32[288,384]{1,0:T(8,128)S(1)} %get-tuple-element.45.own_ref, ...), custom_call_target="tpu_custom_call" | custom-call | flops 5898240 | bytes 3145728 | tf_op jit(solution)/shard_map/early/pallas_call | solution.py:752
  26.8 0.1 collective-permute-done.9.back_ref
  26.9 0.6 %late.1 = (f32[6,32,256]{2,1,0:T(8,128)S(1)}, f32[6,32,256]{2,1,0:T(8,128)S(1)}, f32[6,48,256]{2,1,0:T(8,128)S(1)}, f32[32,128]{1,0:T(8,128)S(1)}) custom-call(f32[6,128,256]{2,1,0:T(8,128)S(1)} %bitcast.14, s32[128,256]{1,0:T(8,128)S(1)} %copy-done.5, f32[128,128]{1,0:T(8,128)S(1)} %copy-done.10, f32[6,96,384]{2,1,0:T(8,128)S(1)} %get-tuple-element.52.inner_ref, ...), custom_call_target="tpu_custom_call" | custom-call | flops 1572864 | bytes 786432 | tf_op jit(solution)/shard_map/late/pallas_call | solution.py:757
  27.4 13.2 %all_to_all.11 = f32[32,1,128]{2,1,0:T(1,128)S(1)} all-to-all(f32[32,1,128]{2,1,0:T(1,128)S(1)} %bitcast.19), channel_id=1, replica_groups=mesh['ax'=8,'sec'=4] {'ax','sec'}, dimensions={0} | all-to-all | bytes 32768 | tf_op jit(solution)/shard_map/all_to_all | solution.py:762
  40.6 0.0 copy-done.1
  40.6 1.3 %update.1 = (f32[6,128,256]{2,1,0:T(8,128)}, f32[6,128,256]{2,1,0:T(8,128)}, f32[1,3]{1,0:T(1,128)}) custom-call(f32[6,128,256]{2,1,0:T(8,128)S(1)} %bitcast.17, f32[32,128]{1,0:T(8,128)S(1)} %bitcast.18, f32[6,96,384]{2,1,0:T(8,128)S(1)} %get-tuple-element.52.inner_ref, f32[6,96,256]{2,1,0:T(8,128)S(1)} %get-tuple-element.53.inner_residual_ref, ...), custom_call_target="tpu_custom_call" | custom-call | flops 786432 | bytes 4718592 | tf_op jit(solution)/shard_map/update/pallas_call | solution.py:763
  (8 shorter events, 0.0 us)
Async XLA Ops:
  3.2 9.3 %copy-start.2 = (bf16[2,512,512]{2,1,0:T(8,128)(2,1)S(1)}, bf16[2,512,512]{2,1,0:T(8,128)(2,1)}, u32[]{:S(2)}) copy-start(bf16[2,512,512]{2,1,0:T(8,128)(2,1)} %constant.10.clone.refs_2_.odd_ref) | copy-start | bytes 3145732
  3.2 9.3 %copy-start.6 = (bf16[2,2,256,256]{3,2,1,0:T(8,128)(2,1)S(1)}, bf16[2,2,256,256]{3,2,1,0:T(8,128)(2,1)}, u32[]{:S(2)}) copy-start(bf16[2,2,256,256]{3,2,1,0:T(8,128)(2,1)} %constant.9.clone.refs_1_.even_ref) | copy-start | bytes 1572868
  3.2 9.3 %copy-start.8 = (f32[4,8,1024]{2,1,0:T(8,128)S(1)}, f32[4,8,1024]{2,1,0:T(8,128)}, u32[]{:S(2)}) copy-start(f32[4,8,1024]{2,1,0:T(8,128)} %constant.11.clone.refs_3_.beyond_ref) | copy-start | bytes 393220
  3.2 14.2 %collective-permute-start.5 = (f32[296,256]{1,0:T(8,128)}, f32[296,256]{1,0:T(8,128)S(1)}, u32[]{:S(2)}, u32[]{:S(2)}) collective-permute-start(f32[296,256]{1,0:T(8,128)} %first.1.own_ref), channel_id=1, source_target_pairs={{0,2},{1,3},{2,0},{3,1},{4,6},{5,7},{6,4},{7,5},{8,10},{9,11},{10,... | collective-permute-start | bytes 909320 | tf_op jit(solution)/shard_map/ppermute | solution.py:721
  9.7 11.0 %collective-permute-start.6 = (f32[296,256]{1,0:T(8,128)}, f32[296,256]{1,0:T(8,128)S(1)}, u32[]{:S(2)}, u32[]{:S(2)}) collective-permute-start(f32[296,256]{1,0:T(8,128)} %get-tuple-element.42.sent_ref), channel_id=1, source_target_pairs={{0,3},{1,2},{2,1},{3,0},{4,7},{5,6},{6,5},{7,4},{8,11},{9,10},{10,... | collective-permute-start | bytes 909320 | tf_op jit(solution)/shard_map/ppermute | solution.py:721
  9.7 10.9 %collective-permute-start.4 = (f32[296,256]{1,0:T(8,128)}, f32[296,256]{1,0:T(8,128)S(1)}, u32[]{:S(2)}, u32[]{:S(2)}) collective-permute-start(f32[296,256]{1,0:T(8,128)} %get-tuple-element.42.sent_ref), channel_id=1, source_target_pairs={{0,1},{1,0},{2,3},{3,2},{4,5},{5,4},{6,7},{7,6},{8,9},{9,8},{10,11... | collective-permute-start | bytes 909320 | tf_op jit(solution)/shard_map/ppermute | solution.py:721
  10.0 5.7 %collective-permute-start = (f32[16,256]{1,0:T(8,128)}, f32[16,256]{1,0:T(8,128)S(1)}, u32[]{:S(2)}, u32[]{:S(2)}) collective-permute-start(f32[16,256]{1,0:T(8,128)} %get-tuple-element.38), channel_id=1, source_target_pairs={{0,4},{4,0},{8,12},{12,8},{16,20},{20,16},{24,28},{28,24},{1,5},{5... | collective-permute-start | bytes 49160 | tf_op jit(solution)/shard_map/ppermute | solution.py:727
  11.8 3.9 %collective-permute-start.1 = (f32[16,256]{1,0:T(8,128)}, f32[16,256]{1,0:T(8,128)S(1)}, u32[]{:S(2)}, u32[]{:S(2)}) collective-permute-start(f32[16,256]{1,0:T(8,128)} %get-tuple-element.39), channel_id=1, source_target_pairs={{4,8},{8,4},{12,16},{16,12},{20,24},{24,20},{5,9},{9,5},{13,17},{1... | collective-permute-start | bytes 49160 | tf_op jit(solution)/shard_map/ppermute | solution.py:728
  12.5 1.2 %copy-start.3 = (bf16[4,2,256,256]{3,2,1,0:T(8,128)(2,1)S(1)}, bf16[4,2,256,256]{3,2,1,0:T(8,128)(2,1)}, u32[]{:S(2)}) copy-start(bf16[4,2,256,256]{3,2,1,0:T(8,128)(2,1)} %constant.8.clone.refs_0_.forward_ref) | copy-start | bytes 3145732
  13.8 0.9 %copy-start.12 = (f32[6,6,1024]{2,1,0:T(8,128)S(1)}, f32[6,6,1024]{2,1,0:T(8,128)}, u32[]{:S(2)}) copy-start(f32[6,6,1024]{2,1,0:T(8,128)} %precond_ref.1) | copy-start | bytes 442372
  14.7 1.0 %copy-start.11 = (f32[2,112,256]{2,1,0:T(8,128)S(1)}, f32[2,112,256]{2,1,0:T(8,128)}, u32[]{:S(2)}) copy-start(f32[2,112,256]{2,1,0:T(8,128)} %get-tuple-element.37.ends_ref) | copy-start | bytes 688132
  14.7 6.0 %copy-start.4 = (bf16[4,2,256,256]{3,2,1,0:T(8,128)(2,1)S(1)}, bf16[4,2,256,256]{3,2,1,0:T(8,128)(2,1)}, u32[]{:S(2)}) copy-start(bf16[4,2,256,256]{3,2,1,0:T(8,128)(2,1)} %constant.8.clone.refs_0_.forward_ref) | copy-start | bytes 3145732
  14.7 6.0 %copy-start.7 = (f32[296,256]{1,0:T(8,128)S(1)}, f32[296,256]{1,0:T(8,128)}, u32[]{:S(2)}) copy-start(f32[296,256]{1,0:T(8,128)} %first.1.own_ref) | copy-start | bytes 909316
  15.7 5.0 %copy-start.5 = (s32[128,256]{1,0:T(8,128)S(1)}, s32[128,256]{1,0:T(8,128)}, u32[]{:S(2)}) copy-start(s32[128,256]{1,0:T(8,128)} %hole_ref.11) | copy-start | bytes 393220
  15.8 7.7 %collective-permute-start.3 = (f32[104,256]{1,0:T(8,128)S(1)}, f32[104,256]{1,0:T(8,128)S(1)}, u32[]{:S(2)}, u32[]{:S(2)}) collective-permute-start(f32[104,256]{1,0:T(8,128)S(1)} %get-tuple-element.40.own_ref), channel_id=1, source_target_pairs={{0,2},{1,3},{2,0},{3,1},{4,6},{5,7},{6,4},{7,5},{8,10},{9,11},{10,... | collective-permute-start | bytes 319496 | tf_op jit(solution)/shard_map/ppermute | solution.py:721
  17.4 6.6 %collective-permute-start.7 = (f32[104,256]{1,0:T(8,128)S(1)}, f32[104,256]{1,0:T(8,128)S(1)}, u32[]{:S(2)}, u32[]{:S(2)}) collective-permute-start(f32[104,256]{1,0:T(8,128)S(1)} %get-tuple-element.41.sent_ref), channel_id=1, source_target_pairs={{0,3},{1,2},{2,1},{3,0},{4,7},{5,6},{6,5},{7,4},{8,11},{9,10},{10,... | collective-permute-start | bytes 319496 | tf_op jit(solution)/shard_map/ppermute | solution.py:721
  17.4 6.6 %collective-permute-start.2 = (f32[104,256]{1,0:T(8,128)S(1)}, f32[104,256]{1,0:T(8,128)S(1)}, u32[]{:S(2)}, u32[]{:S(2)}) collective-permute-start(f32[104,256]{1,0:T(8,128)S(1)} %get-tuple-element.41.sent_ref), channel_id=1, source_target_pairs={{0,1},{1,0},{2,3},{3,2},{4,5},{5,4},{6,7},{7,6},{8,9},{9,8},{10,11... | collective-permute-start | bytes 319496 | tf_op jit(solution)/shard_map/ppermute | solution.py:721
  23.5 2.4 %collective-permute-start.8 = (f32[288,384]{1,0:T(8,128)S(1)}, f32[288,384]{1,0:T(8,128)S(1)}, u32[]{:S(2)}, u32[]{:S(2)}) collective-permute-start(f32[288,384]{1,0:T(8,128)S(1)} %get-tuple-element.50), channel_id=1, source_target_pairs={{0,1},{1,0},{2,3},{3,2},{4,5},{5,4},{6,7},{7,6},{8,9},{9,8},{10,11... | collective-permute-start | bytes 1327112 | tf_op jit(solution)/shard_map/ppermute | solution.py:721
  24.1 1.8 %copy-start = (f32[128,6,256]{2,0,1:T(8,128)S(1)}, f32[128,6,256]{2,0,1:T(8,128)}, u32[]{:S(2)}) copy-start(f32[128,6,256]{2,0,1:T(8,128)} %param.13) | copy-start | bytes 2359300
  24.1 1.8 %copy-start.9 = (f32[296,256]{1,0:T(8,128)S(1)}, f32[296,256]{1,0:T(8,128)}, u32[]{:S(2)}) copy-start(f32[296,256]{1,0:T(8,128)} %get-tuple-element.42.sent_ref) | copy-start | bytes 909316
  24.1 1.8 %copy-start.10 = (f32[128,128]{1,0:T(8,128)S(1)}, f32[128,128]{1,0:T(8,128)}, u32[]{:S(2)}) copy-start(f32[128,128]{1,0:T(8,128)} %get-tuple-element.49.factor_ref) | copy-start | bytes 196612
  25.3 1.6 %collective-permute-start.9 = (f32[104,384]{1,0:T(8,128)S(1)}, f32[104,384]{1,0:T(8,128)S(1)}, u32[]{:S(2)}, u32[]{:S(2)}) collective-permute-start(f32[104,384]{1,0:T(8,128)S(1)} %get-tuple-element.54), channel_id=1, source_target_pairs={{0,1},{1,0},{2,3},{3,2},{4,5},{5,4},{6,7},{7,6},{8,9},{9,8},{10,11... | collective-permute-start | bytes 479240 | tf_op jit(solution)/shard_map/ppermute | solution.py:721
  26.9 13.8 %copy-start.1 = (f32[128,6,256]{2,0,1:T(8,128)S(1)}, f32[128,6,256]{2,0,1:T(8,128)}, u32[]{:S(2)}) copy-start(f32[128,6,256]{2,0,1:T(8,128)} %param.12) | copy-start | bytes 2359300

commit v6 on v5

--- a/solution.py
+++ b/solution.py
@@ -144,8 +144,11 @@
 def edge_rows(fields, solid):
     rows, width = solid.shape
     sources = fields + [solid] * (TILE - len(fields))
-    columns = [x[:, :1] for x in sources] + [x[:, width - 1 :] for x in sources]
-    table = jnp.concatenate(columns + [jnp.zeros((rows, LANES - 2 * TILE), F32)], axis=1)
+    lane = lanes_of((rows, LANES))
+    table = jnp.zeros((rows, LANES), F32)
+    for i, x in enumerate(sources):
+        table = jnp.where(lane == i, pltpu.roll(x[:, :LANES], i, 1) if i else x[:, :LANES], table)
+        table = jnp.where(lane == TILE + i, pltpu.roll(x[:, width - LANES :], TILE + i + 1, 1), table)
     if rows < LANES:
         table = jnp.concatenate([table, jnp.zeros((LANES - rows, LANES), F32)], axis=0)
     table = table.T
@@ -201,15 +204,15 @@
             keep_out[last, :] = jnp.concatenate(
                 edge_rows(fields, jnp.concatenate([solid, solid_tail], axis=0)), axis=1
             )
-            leaving.append(copy(keep_out.at[last], keep_ref.at[last], out_sems.at[pairs]))
+            leaving.append(copy(keep_out.at[last], keep_ref.at[last], out_sems.at[comps]))
         moving[g][1].wait()
         moving[g][2].wait()
         for q in (2 * g, 2 * g + 1):
-            keep_out[pl.ds(q * inner, inner), :] = local_part(
+            rows = pl.ds(q * inner, inner)
+            keep_out[rows, :] = local_part(
                 q, disp_in[q, around], inside, solid, factor, load_in[q], stiff_in[q], disp_in[q ^ 1, around]
             )
-        rows = pl.ds(2 * g * inner, 2 * inner)
-        leaving.append(copy(keep_out.at[rows], keep_ref.at[rows], out_sems.at[g]))
+            leaving.append(copy(keep_out.at[rows], keep_ref.at[rows], out_sems.at[q]))
     for one in leaving:
         one.wait()
 
@@ -533,9 +536,37 @@
     return back[pl.ds(q * rows, rows), :width] * solid, side, residual
 
 
+def end_image(h, end, comps, found, inner_ref, inner_residual_ref, stiff_ref, hole_ref, factor_ref, sums):
+    slab, width = hole_ref.shape
+    near = 2 * TILE
+    lower = h == 1
+    there = pl.ds(pl.multiple_of((inner_ref.shape[1] - near) * h, TILE), near)
+    here = pl.ds(pl.multiple_of((slab - end - near) * h, TILE), end + near)
+
+    def joined(ends, inner):
+        return jnp.where(lower, jnp.concatenate([inner, ends], axis=0), jnp.concatenate([ends, inner], axis=0))
+
+    solid = (1 - hole_ref[here, :]).astype(F32)
+    factor = factor_ref[here, :]
+    fields = [joined(found[q][0], inner_ref[q, there, :width]) for q in range(comps)]
+    row = rows_of((end + near, width))
+    valid = (row >= jnp.where(lower, TILE, 0)) & (row < jnp.where(lower, end + near, end + TILE))
+    images = []
+    for q in range(comps):
+        beyond = found[q][2]
+        field, image = image_rows(
+            q, fields, joined(found[q][1], inner_ref[q, there, width:]), stiff_ref[q, here], solid, factor,
+            jnp.where(lower, 0.0, beyond), jnp.where(lower, beyond, 0.0), slice(0, end + near),
+        )
+        images.append(jnp.where(lower, image[TILE:], image[: end + TILE]))
+        residual = joined(found[q][3], inner_residual_ref[q, there])
+        sums = add_sums(sums, *[jnp.where(valid, x, 0.0) for x in (residual, field, image)])
+    return images, sums
+
+
 def early_kernel(
     end, comps, stiff_ref, hole_ref, factor_ref, own_ref, back_ref, residual_ref, sent_ref,
-    prec_out, residual_out, image_ref, sums_ref,
+    own_ends_ref, residual_ends_ref, prec_out, residual_out, image_ref, sums_ref, image_ends_ref,
 ):
     slab, width = hole_ref.shape
     inner = slab // 2 - end
@@ -562,56 +593,46 @@
         )
         image_ref[q] = image
         sums = add_sums(sums, residual_out[q, core_rows], field, image)
+    found = []
+    for q in range(comps):
+        rows = pl.ds(q * end, end)
+        far = own_ends_ref[pl.ds(comps * end + q, 1), :width]
+        found.append((own_ends_ref[rows, :width], own_ends_ref[rows, width:], far, residual_ends_ref[q]))
+    images, sums = end_image(
+        core, end, comps, found, prec_out, residual_out, stiff_ref, hole_ref, factor_ref, sums
+    )
+    for q in range(comps):
+        image_ends_ref[q] = images[q]
     for i, total in enumerate(sums):
         sums_ref[pl.ds(i * TILE, TILE), :] = total
 
 
 def late_kernel(
     end, comps, stiff_ref, hole_ref, factor_ref, inner_ref, inner_residual_ref,
-    own_ref, back_ref, residual_ref, sent_ref, partial_ref,
+    own_ref, back_ref, residual_ref, sent_ref, partial_ref, image_own_ref,
     prec_out, residual_out, image_ref, sums_ref,
 ):
     slab, width = hole_ref.shape
     reach = end + TILE
     core = lax.axis_index("sec") % 2
-    odd = core == 1
-    solid = (1 - hole_ref[...]).astype(F32)
-    factor = factor_ref[...]
+    other = 1 - core
+    solid = (1 - hole_ref[pl.ds(pl.multiple_of((slab - end) * other, TILE), end), :]).astype(F32)
     sums = [partial_ref[pl.ds(i * TILE, TILE), :] for i in range(5)]
-    fields, tiles, beyond, residuals = [[], []], [[], []], [[], []], [[], []]
-    for q in range(comps):
-        solid_there = jnp.where(odd, solid[:end], solid[slab - end :])
-        there, side, residual = returned(back_ref, sent_ref, solid_there, q, end)
-        rows, far = pl.ds(q * end, end), pl.ds(comps * end + q, 1)
-        here, own_side = own_ref[rows, :width], own_ref[rows, width:]
-        far_here, far_there = own_ref[far, :width], back_ref[far, :width]
-        for h, swap in ((0, odd), (1, core == 0)):
-            prec = jnp.where(swap, there, here)
-            tile = jnp.where(swap, side, own_side)
-            rest = jnp.where(swap, residual, residual_ref[q])
-            beyond[h].append(jnp.where(swap, far_there, far_here))
-            rows = pl.ds(end * h, end)
-            prec_out[q, rows] = prec
-            residual_out[q, rows] = rest
-            near = slice(0, 2 * TILE) if h == 0 else slice(-2 * TILE, None)
-            close = slice(0, TILE) if h == 0 else slice(-TILE, None)
-            parts = [prec, inner_ref[q, near, :width]]
-            sides = [tile, inner_ref[q, close, width:]]
-            rests = [rest, inner_residual_ref[q, close]]
-            order = slice(None) if h == 0 else slice(None, None, -1)
-            fields[h].append(jnp.concatenate(parts[order], axis=0))
-            tiles[h].append(jnp.concatenate(sides[order], axis=0))
-            residuals[h].append(jnp.concatenate(rests[order], axis=0))
-    for h in range(2):
-        rows = slice(0, reach) if h == 0 else slice(slab - reach, slab)
-        inner = slice(0, reach) if h == 0 else slice(TILE, None)
-        for q in range(comps):
-            before, after = (beyond[0][q], 0.0) if h == 0 else (0.0, beyond[1][q])
-            field, image = image_rows(
-                q, fields[h], tiles[h][q], stiff_ref[q, rows], solid[rows], factor[rows], before, after, inner
-            )
-            image_ref[q, pl.ds(reach * h, reach)] = image
-            sums = add_sums(sums, residuals[h][q], field, image)
+    here, there = [pl.ds(pl.multiple_of(end * h, TILE), end) for h in (core, other)]
+    found = []
+    for q in range(comps):
+        prec, side, residual = returned(back_ref, sent_ref, solid, q, end)
+        found.append((prec, side, back_ref[pl.ds(comps * end + q, 1), :width], residual))
+        prec_out[q, there] = prec
+        residual_out[q, there] = residual
+        prec_out[q, here] = own_ref[pl.ds(q * end, end), :width]
+        residual_out[q, here] = residual_ref[q]
+        image_ref[q, pl.ds(pl.multiple_of(reach * core, TILE), reach)] = image_own_ref[q]
+    images, sums = end_image(
+        other, end, comps, found, inner_ref, inner_residual_ref, stiff_ref, hole_ref, factor_ref, sums
+    )
+    for q in range(comps):
+        image_ref[q, pl.ds(pl.multiple_of(reach * other, TILE), reach)] = images[q]
     row = jnp.zeros((1, LANES), F32)
     spot = lanes_of((1, LANES))
     for i, value in enumerate(sums):
@@ -645,7 +666,7 @@
 VMEM = pl.BlockSpec(memory_space=pltpu.VMEM)
 SMEM = pl.BlockSpec(memory_space=pltpu.SMEM)
 HBM = pl.BlockSpec(memory_space=pltpu.HBM)
-FULL = 62
+FULL = 60
 
 
 def call(kernel, name, out_shapes, in_specs, flops, moved, scratch=(), grant=32, out_specs=None):
@@ -705,7 +726,7 @@
         [sent], [HBM] * 6, 10 * comps * inner * width, block,
         small + [pltpu.VMEM((comps, rows, width), F32) for rows in (inner, reach, inner)]
         + [pltpu.VMEM((reach, width), jnp.int32), pltpu.VMEM(sent, F32), pltpu.VMEM((slab, LANES), F32)]
-        + [pltpu.SemaphoreType.DMA((3 + 3 * comps // 2,)), pltpu.SemaphoreType.DMA((1 + comps // 2,))],
+        + [pltpu.SemaphoreType.DMA((3 + 3 * comps // 2,)), pltpu.SemaphoreType.DMA((1 + comps,))],
         FULL, [HBM],
     )(*arguments)
     other, edge, factor, near, other_side = call(
@@ -749,16 +770,17 @@
         comps, width, slab, 100,
     )
     back_ends = to(back_ends, 1)
-    prec, residual, image, partial = call(
+    prec, residual, image, partial, image_own = call(
         functools.partial(early_kernel, end, comps), "early",
-        [(comps, 2 * inner, width + LANES), (comps, 2 * inner, width), (comps, 2 * (inner - TILE), width), (5 * TILE, width)],
-        [VMEM] * 7, 30 * comps * slab * width, 4 * block,
-    )(stiff, hole, after_all(factor, own_ends), own, back, residual, other)
+        [(comps, 2 * inner, width + LANES), (comps, 2 * inner, width), (comps, 2 * (inner - TILE), width),
+         (5 * TILE, width), (comps, end + TILE, width)],
+        [VMEM] * 9, 30 * comps * slab * width, 4 * block,
+    )(stiff, hole, factor, own, back, residual, other, own_ends, residual_ends)
     prec_ends, residual_ends, image_ends, sums = call(
         functools.partial(late_kernel, end, comps), "late",
         [(comps, 2 * end, width), (comps, 2 * end, width), (comps, 2 * (end + TILE), width), (ax * sec, LANES)],
-        [VMEM] * 10, 8 * comps * slab * width, block,
-    )(stiff, hole, factor, prec, residual, own_ends, back_ends, residual_ends, other_ends, partial)
+        [VMEM] * 11, 8 * comps * slab * width, block,
+    )(stiff, hole, factor, prec, residual, own_ends, back_ends, residual_ends, other_ends, partial, image_own)
     gathered = lax.all_to_all(sums, ("ax", "sec"), 0, 0, tiled=True)
     disp_new, residual_new, stats = call(
         functools.partial(update_kernel, end, comps, cell_total), "update",

time: 42.2 us -> 42.3 us (level)
  local copies, waits for them, and re-layouts: 2.2 us -> 0.07 us
  waiting for transfers between devices: 3.22 us -> 4.99 us
    unnamed x26 -> x24, local copies, waits for them, and re-layouts: 2.2 us -> 0.07 us
    ppermute x8, waiting for transfers between devices: 3.21 us -> 4.83 us  [to(): return lax.ppermute(x, 'sec', [(i, i ^ mask) for i in range(sec)])]
  transfers between devices with their start and end apart: 10 -> 10, of which waited for: 3 -> 3; matrix products, arithmetic and copies ran while one was open for 0% -> 0% of each run, Pallas kernels for 22% -> 23%
where the time goes in v6:
time: 42.3 us; the launch traced here: 42.1 us
  Pallas kernels  14.2 us (34%)
  blocking collectives  13 us (31%)
  starting transfers between devices  8.91 us (21%)
  waiting for transfers between devices  4.99 us (12%)
  between operations  0.84 us (2%)
    all_to_all x1, blocking collectives, shards(): gathered = lax.all_to_all(sums, ('ax', 'sec'), 0, 0, tiled=True)  13 us
    ppermute x8, starting transfers between devices, to(): return lax.ppermute(x, 'sec', [(i, i ^ mask) for i in range(sec)])  6.18 us
    ppermute x8, waiting for transfers between devices, to(): return lax.ppermute(x, 'sec', [(i, i ^ mask) for i in range(sec)])  4.83 us
    pallas_call x2, Pallas kernels, transform_call(): call(functools.partial(transform_kernel, comps, main, at_end, edge_at, ho...  4.11 us
    pallas_call x1, Pallas kernels, shards(): call(functools.partial(second_kernel, end, comps, ax), 'second', shapes,...  3.39 us
    pallas_call x1, Pallas kernels, shards(): call(functools.partial(first_kernel, end, comps, ax), 'first', [sent], [H...  2.61 us
    ppermute x1, starting transfers between devices, shards(): near = lax.ppermute(near, 'ax', [(i, i ^ 1) for i in range(ax)])  1.94 us
    pallas_call x1, Pallas kernels, shards(): call(functools.partial(update_kernel, end, comps, cell_total), 'update',...  1.35 us
  transfers between devices with their start and end apart: 10, of which 3 were waited for; matrix products, arithmetic and copies ran while one was open for 0% of the time, Pallas kernels for 23%

profile of v6, /device:TPU:0, one launch (start us, length us, event | category | flops | bytes accessed | tf_op | source)
XLA Modules:
  0.0 42.1 jit_solution(3592472591907606042)
XLA Ops:
  0.6 0.0 copy-start.5
  0.6 2.6 %first.1.own_ref = f32[296,256]{1,0:T(8,128)} custom-call(f32[4,6]{1,0:T(4,128)} %table_ref.3, s32[1,128]{1,0:T(1,128)} %bitcast.22, f32[6,128,256]{2,1,0:T(8,128)} %bitcast.20, f32[6,128,256]{2,1,0:T(8,128)} %bitcast.15, f32[6,128,256]{2,1,0:T(8,128)} %bitcast.11, s32[128,256]{1,0:T(8,128)} %hole_ref.11), custom_call_target="tpu_custom_call" | custom-call | flops 737280 | bytes 786432 | tf_op jit(solution)/shard_map/first/pallas_call | solution.py:724
  3.3 0.0 copy-start.2
  3.3 0.0 copy-start.3
  3.3 0.0 copy-start.7
  3.3 0.0 copy-start.11
  3.3 3.0 %collective-permute-start.1 = (f32[296,256]{1,0:T(8,128)}, f32[296,256]{1,0:T(8,128)S(1)}, u32[]{:S(2)}, u32[]{:S(2)}) collective-permute-start(f32[296,256]{1,0:T(8,128)} %first.1.own_ref), channel_id=1, source_target_pairs={{0,2},{1,3},{2,0},{3,1},{4,6},{5,7},{6,4},{7,5},{8,10},{9,11},{10,... | collective-permute-start | bytes 909320 | tf_op jit(solution)/shard_map/ppermute | solution.py:742
  6.3 3.4 %second.1 = (f32[296,256]{1,0:T(8,128)}, f32[2,112,256]{2,1,0:T(8,128)}, f32[128,128]{1,0:T(8,128)}, f32[16,256]{1,0:T(8,128)}, f32[16,256]{1,0:T(8,128)}) custom-call(f32[4,6]{1,0:T(4,128)} %table_ref.3, s32[1,128]{1,0:T(1,128)} %bitcast.23, f32[6,128,256]{2,1,0:T(8,128)} %bitcast.21, f32[6,128,256]{2,1,0:T(8,128)} %bitcast.16, f32[6,128,256]{2,1,0:T(8,128)} %bitcast.12, ...), custom_call_target="tpu_custom_call" | custom-call | flops 1966080 | bytes 1572864 | tf_op jit(solution)/shard_map/second/pallas_call | solution.py:732
  9.7 0.1 collective-permute-start.4
  9.8 0.3 collective-permute-start
  10.1 1.9 %collective-permute-start.2 = (f32[16,256]{1,0:T(8,128)}, f32[16,256]{1,0:T(8,128)S(1)}, u32[]{:S(2)}, u32[]{:S(2)}) collective-permute-start(f32[16,256]{1,0:T(8,128)} %get-tuple-element.39), channel_id=1, source_target_pairs={{0,4},{4,0},{8,12},{12,8},{16,20},{20,16},{24,28},{28,24},{1,5},{5... | collective-permute-start | bytes 49160 | tf_op jit(solution)/shard_map/ppermute | solution.py:748
  12.0 0.8 %collective-permute-start.3 = (f32[16,256]{1,0:T(8,128)}, f32[16,256]{1,0:T(8,128)S(1)}, u32[]{:S(2)}, u32[]{:S(2)}) collective-permute-start(f32[16,256]{1,0:T(8,128)} %get-tuple-element.40), channel_id=1, source_target_pairs={{4,8},{8,4},{12,16},{16,12},{20,24},{24,20},{5,9},{9,5},{13,17},{1... | collective-permute-start | bytes 49160 | tf_op jit(solution)/shard_map/ppermute | solution.py:749
  12.8 0.0 copy-done.5
  12.8 0.0 copy-done.2
  12.8 0.0 copy-done.3
  12.9 0.0 copy-done.7
  12.9 0.0 copy-done.11
  12.9 0.0 copy-start.6
  12.9 1.0 %fold.1 = (f32[36,8,640]{2,1,0:T(8,128)S(1)}, f32[6,8,640]{2,1,0:T(8,128)S(1)}) custom-call(f32[6,6,1024]{2,1,0:T(8,128)S(1)} %copy-done.11, bf16[4,2,256,256]{3,2,1,0:T(8,128)(2,1)S(1)} %copy-done.3, bf16[2,2,256,256]{3,2,1,0:T(8,128)(2,1)S(1)} %copy-done.5, bf16[2,512,512]{2,1,0:T(8,128)(2,1)S(1)} %copy-done.2, f32[4,8,1024]{2,1,0:T(8,128)S(1)} %copy-done.7), custom_call_target="tpu_custom_call" | custom-call | flops 1 | bytes 1 | tf_op jit(solution)/shard_map/fold/pallas_call | solution.py:750
  13.9 0.0 copy-start.4
  13.9 0.2 collective-permute-done.2.near_ref
  14.0 0.0 collective-permute-done.3.next_ref
  14.0 0.0 copy-done.10
  14.0 0.1 ends.1
  14.1 1.9 %collective-permute-start.7 = (f32[104,256]{1,0:T(8,128)S(1)}, f32[104,256]{1,0:T(8,128)S(1)}, u32[]{:S(2)}, u32[]{:S(2)}) collective-permute-start(f32[104,256]{1,0:T(8,128)S(1)} %get-tuple-element.41.own_ref), channel_id=1, source_target_pairs={{0,2},{1,3},{2,0},{3,1},{4,6},{5,7},{6,4},{7,5},{8,10},{9,11},{10,... | collective-permute-start | bytes 319496 | tf_op jit(solution)/shard_map/ppermute | solution.py:742
  16.1 0.0 collective-permute-start.8
  16.1 0.0 collective-permute-done.1.across_ref
  16.1 0.3 collective-permute-start.6
  16.4 4.4 %collective-permute-done.4.both_ref = f32[296,256]{1,0:T(8,128)S(1)} collective-permute-done((f32[296,256]{1,0:T(8,128)}, f32[296,256]{1,0:T(8,128)S(1)}, u32[]{:S(2)}, u32[]{:S(2)}) %collective-permute-start.4) | collective-permute-done | bytes 303136 | tf_op jit(solution)/shard_map/ppermute | solution.py:742
  20.7 0.0 collective-permute-done.core_ref
  20.7 0.0 copy-done.6
  20.7 0.0 copy-done.4
  20.8 2.9 %transform.2 = (f32[128,128]{1,0:T(8,128)S(1)}, f32[288,384]{1,0:T(8,128)S(1)}, f32[6,48,256]{2,1,0:T(8,128)S(1)}, f32[288,384]{1,0:T(8,128)S(1)}) custom-call(f32[296,256]{1,0:T(8,128)S(1)} %copy-done.6, f32[296,256]{1,0:T(8,128)S(1)} %collective-permute-done.core_ref, f32[296,256]{1,0:T(8,128)S(1)} %collective-permute-done.1.across_ref, ...), custom_call_target="tpu_custom_call" | custom-call | tf_op jit(solution)/shard_map/transform/pallas_call | solution.py:693
  23.6 0.0 collective-permute-done.7.across_ref
  23.6 0.1 collective-permute-start.5
  23.7 0.4 %collective-permute-done.8.both_ref = f32[104,256]{1,0:T(8,128)S(1)} collective-permute-done((f32[104,256]{1,0:T(8,128)S(1)}, f32[104,256]{1,0:T(8,128)S(1)}, u32[]{:S(2)}, u32[]{:S(2)}) %collective-permute-start.8) | collective-permute-done | bytes 106528 | tf_op jit(solution)/shard_map/ppermute | solution.py:742
  24.1 0.0 collective-permute-done.6.core_ref
  24.1 1.2 %transform.3 = (f32[104,384]{1,0:T(8,128)S(1)}, f32[6,16,256]{2,1,0:T(8,128)S(1)}, f32[104,384]{1,0:T(8,128)S(1)}) custom-call(f32[104,256]{1,0:T(8,128)S(1)} %get-tuple-element.41.own_ref, f32[104,256]{1,0:T(8,128)S(1)} %collective-permute-done.6.core_ref, f32[104,256]{1,0:T(8,128)S(1)} %collective-permute-done.7.across_ref, ...), custom_call_target="tpu_custom_call" | custom-call | flops 45298483200 | bytes 78643200 | tf_op jit(solution)/shard_map/transform/pallas_call | solution.py:693
  25.4 0.5 %collective-permute-start.9 = (f32[104,384]{1,0:T(8,128)S(1)}, f32[104,384]{1,0:T(8,128)S(1)}, u32[]{:S(2)}, u32[]{:S(2)}) collective-permute-start(f32[104,384]{1,0:T(8,128)S(1)} %get-tuple-element.54), channel_id=1, source_target_pairs={{0,1},{1,0},{2,3},{3,2},{4,5},{5,4},{6,7},{7,6},{8,9},{9,8},{10,11... | collective-permute-start | bytes 479240 | tf_op jit(solution)/shard_map/ppermute | solution.py:742
  25.9 0.0 collective-permute-done.5.back_ref
  25.9 0.0 copy-done
  25.9 0.0 copy-done.9
  26.0 1.2 %early.1 = (f32[6,96,384]{2,1,0:T(8,128)S(1)}, f32[6,96,256]{2,1,0:T(8,128)S(1)}, f32[6,80,256]{2,1,0:T(8,128)S(1)}, f32[40,256]{1,0:T(8,128)S(1)}, f32[6,24,256]{2,1,0:T(8,128)S(1)}) custom-call(f32[6,128,256]{2,1,0:T(8,128)S(1)} %bitcast.13, s32[128,256]{1,0:T(8,128)S(1)} %copy-done.4, f32[128,128]{1,0:T(8,128)S(1)} %copy-done.9, ...), custom_call_target="tpu_custom_call" | custom-call | flops 5898240 | bytes 3145728 | tf_op jit(solution)/shard_map/early/pallas_call | solution.py:773
  27.2 0.0 collective-permute-done.9.back_ref
  27.2 0.0 copy-start.1
  27.2 0.5 %late.1 = (f32[6,32,256]{2,1,0:T(8,128)S(1)}, f32[6,32,256]{2,1,0:T(8,128)S(1)}, f32[6,48,256]{2,1,0:T(8,128)S(1)}, f32[32,128]{1,0:T(8,128)S(1)}) custom-call(f32[6,128,256]{2,1,0:T(8,128)S(1)} %bitcast.14, s32[128,256]{1,0:T(8,128)S(1)} %copy-done.4, f32[128,128]{1,0:T(8,128)S(1)} %copy-done.9, f32[6,96,384]{2,1,0:T(8,128)S(1)} %get-tuple-element.52.inner_ref, ...), custom_call_target="tpu_custom_call" | custom-call | flops 1572864 | bytes 786432 | tf_op jit(solution)/shard_map/late/pallas_call | solution.py:779
  27.7 13.0 %all_to_all.11 = f32[32,1,128]{2,1,0:T(1,128)S(1)} all-to-all(f32[32,1,128]{2,1,0:T(1,128)S(1)} %bitcast.19), channel_id=1, replica_groups=mesh['ax'=8,'sec'=4] {'ax','sec'}, dimensions={0} | all-to-all | bytes 32768 | tf_op jit(solution)/shard_map/all_to_all | solution.py:784
  40.7 1.3 %update.1 = (f32[6,128,256]{2,1,0:T(8,128)}, f32[6,128,256]{2,1,0:T(8,128)}, f32[1,3]{1,0:T(1,128)}) custom-call(f32[6,128,256]{2,1,0:T(8,128)S(1)} %bitcast.17, f32[32,128]{1,0:T(8,128)S(1)} %bitcast.18, f32[6,96,384]{2,1,0:T(8,128)S(1)} %get-tuple-element.52.inner_ref, f32[6,96,256]{2,1,0:T(8,128)S(1)} %get-tuple-element.53.inner_residual_ref, ...), custom_call_target="tpu_custom_call" | custom-call | flops 786432 | bytes 4718592 | tf_op jit(solution)/shard_map/update/pallas_call | solution.py:785
  (6 shorter events, 0.0 us)
Async XLA Ops:
  0.6 12.2 %copy-start.5 = (bf16[2,2,256,256]{3,2,1,0:T(8,128)(2,1)S(1)}, bf16[2,2,256,256]{3,2,1,0:T(8,128)(2,1)}, u32[]{:S(2)}) copy-start(bf16[2,2,256,256]{3,2,1,0:T(8,128)(2,1)} %constant.9.clone.refs_1_.even_ref) | copy-start | bytes 1572868
  3.3 9.6 %copy-start.2 = (bf16[2,512,512]{2,1,0:T(8,128)(2,1)S(1)}, bf16[2,512,512]{2,1,0:T(8,128)(2,1)}, u32[]{:S(2)}) copy-start(bf16[2,512,512]{2,1,0:T(8,128)(2,1)} %constant.10.clone.refs_2_.odd_ref) | copy-start | bytes 3145732
  3.3 9.6 %copy-start.3 = (bf16[4,2,256,256]{3,2,1,0:T(8,128)(2,1)S(1)}, bf16[4,2,256,256]{3,2,1,0:T(8,128)(2,1)}, u32[]{:S(2)}) copy-start(bf16[4,2,256,256]{3,2,1,0:T(8,128)(2,1)} %constant.8.clone.refs_0_.forward_ref) | copy-start | bytes 3145732
  3.3 9.6 %copy-start.7 = (f32[4,8,1024]{2,1,0:T(8,128)S(1)}, f32[4,8,1024]{2,1,0:T(8,128)}, u32[]{:S(2)}) copy-start(f32[4,8,1024]{2,1,0:T(8,128)} %constant.11.clone.refs_3_.beyond_ref) | copy-start | bytes 393220
  3.3 9.6 %copy-start.11 = (f32[6,6,1024]{2,1,0:T(8,128)S(1)}, f32[6,6,1024]{2,1,0:T(8,128)}, u32[]{:S(2)}) copy-start(f32[6,6,1024]{2,1,0:T(8,128)} %precond_ref.1) | copy-start | bytes 442372
  3.3 12.8 %collective-permute-start.1 = (f32[296,256]{1,0:T(8,128)}, f32[296,256]{1,0:T(8,128)S(1)}, u32[]{:S(2)}, u32[]{:S(2)}) collective-permute-start(f32[296,256]{1,0:T(8,128)} %first.1.own_ref), channel_id=1, source_target_pairs={{0,2},{1,3},{2,0},{3,1},{4,6},{5,7},{6,4},{7,5},{8,10},{9,11},{10,... | collective-permute-start | bytes 909320 | tf_op jit(solution)/shard_map/ppermute | solution.py:742
  9.7 11.0 %collective-permute-start.4 = (f32[296,256]{1,0:T(8,128)}, f32[296,256]{1,0:T(8,128)S(1)}, u32[]{:S(2)}, u32[]{:S(2)}) collective-permute-start(f32[296,256]{1,0:T(8,128)} %get-tuple-element.35.sent_ref), channel_id=1, source_target_pairs={{0,3},{1,2},{2,1},{3,0},{4,7},{5,6},{6,5},{7,4},{8,11},{9,10},{10,... | collective-permute-start | bytes 909320 | tf_op jit(solution)/shard_map/ppermute | solution.py:742
  9.8 10.9 %collective-permute-start = (f32[296,256]{1,0:T(8,128)}, f32[296,256]{1,0:T(8,128)S(1)}, u32[]{:S(2)}, u32[]{:S(2)}) collective-permute-start(f32[296,256]{1,0:T(8,128)} %get-tuple-element.35.sent_ref), channel_id=1, source_target_pairs={{0,1},{1,0},{2,3},{3,2},{4,5},{5,4},{6,7},{7,6},{8,9},{9,8},{10,11... | collective-permute-start | bytes 909320 | tf_op jit(solution)/shard_map/ppermute | solution.py:742
  10.1 3.9 %collective-permute-start.2 = (f32[16,256]{1,0:T(8,128)}, f32[16,256]{1,0:T(8,128)S(1)}, u32[]{:S(2)}, u32[]{:S(2)}) collective-permute-start(f32[16,256]{1,0:T(8,128)} %get-tuple-element.39), channel_id=1, source_target_pairs={{0,4},{4,0},{8,12},{12,8},{16,20},{20,16},{24,28},{28,24},{1,5},{5... | collective-permute-start | bytes 49160 | tf_op jit(solution)/shard_map/ppermute | solution.py:748
  12.0 2.0 %copy-start.10 = (f32[2,112,256]{2,1,0:T(8,128)S(1)}, f32[2,112,256]{2,1,0:T(8,128)}, u32[]{:S(2)}) copy-start(f32[2,112,256]{2,1,0:T(8,128)} %get-tuple-element.38.ends_ref) | copy-start | bytes 688132
  12.0 2.0 %collective-permute-start.3 = (f32[16,256]{1,0:T(8,128)}, f32[16,256]{1,0:T(8,128)S(1)}, u32[]{:S(2)}, u32[]{:S(2)}) collective-permute-start(f32[16,256]{1,0:T(8,128)} %get-tuple-element.40), channel_id=1, source_target_pairs={{4,8},{8,4},{12,16},{16,12},{20,24},{24,20},{5,9},{9,5},{13,17},{1... | collective-permute-start | bytes 49160 | tf_op jit(solution)/shard_map/ppermute | solution.py:749
  12.9 7.9 %copy-start.6 = (f32[296,256]{1,0:T(8,128)S(1)}, f32[296,256]{1,0:T(8,128)}, u32[]{:S(2)}) copy-start(f32[296,256]{1,0:T(8,128)} %first.1.own_ref) | copy-start | bytes 909316
  13.9 6.9 %copy-start.4 = (s32[128,256]{1,0:T(8,128)S(1)}, s32[128,256]{1,0:T(8,128)}, u32[]{:S(2)}) copy-start(s32[128,256]{1,0:T(8,128)} %hole_ref.11) | copy-start | bytes 393220
  14.1 9.5 %collective-permute-start.7 = (f32[104,256]{1,0:T(8,128)S(1)}, f32[104,256]{1,0:T(8,128)S(1)}, u32[]{:S(2)}, u32[]{:S(2)}) collective-permute-start(f32[104,256]{1,0:T(8,128)S(1)} %get-tuple-element.41.own_ref), channel_id=1, source_target_pairs={{0,2},{1,3},{2,0},{3,1},{4,6},{5,7},{6,4},{7,5},{8,10},{9,11},{10,... | collective-permute-start | bytes 319496 | tf_op jit(solution)/shard_map/ppermute | solution.py:742
  16.1 8.1 %collective-permute-start.8 = (f32[104,256]{1,0:T(8,128)S(1)}, f32[104,256]{1,0:T(8,128)S(1)}, u32[]{:S(2)}, u32[]{:S(2)}) collective-permute-start(f32[104,256]{1,0:T(8,128)S(1)} %get-tuple-element.47.sent_ref), channel_id=1, source_target_pairs={{0,3},{1,2},{2,1},{3,0},{4,7},{5,6},{6,5},{7,4},{8,11},{9,10},{10,... | collective-permute-start | bytes 319496 | tf_op jit(solution)/shard_map/ppermute | solution.py:742
  16.1 8.1 %collective-permute-start.6 = (f32[104,256]{1,0:T(8,128)S(1)}, f32[104,256]{1,0:T(8,128)S(1)}, u32[]{:S(2)}, u32[]{:S(2)}) collective-permute-start(f32[104,256]{1,0:T(8,128)S(1)} %get-tuple-element.47.sent_ref), channel_id=1, source_target_pairs={{0,1},{1,0},{2,3},{3,2},{4,5},{5,4},{6,7},{7,6},{8,9},{9,8},{10,11... | collective-permute-start | bytes 319496 | tf_op jit(solution)/shard_map/ppermute | solution.py:742
  23.6 2.3 %collective-permute-start.5 = (f32[288,384]{1,0:T(8,128)S(1)}, f32[288,384]{1,0:T(8,128)S(1)}, u32[]{:S(2)}, u32[]{:S(2)}) collective-permute-start(f32[288,384]{1,0:T(8,128)S(1)} %get-tuple-element.45), channel_id=1, source_target_pairs={{0,1},{1,0},{2,3},{3,2},{4,5},{5,4},{6,7},{7,6},{8,9},{9,8},{10,11... | collective-permute-start | bytes 1327112 | tf_op jit(solution)/shard_map/ppermute | solution.py:742
  24.1 1.8 %copy-start = (f32[128,6,256]{2,0,1:T(8,128)S(1)}, f32[128,6,256]{2,0,1:T(8,128)}, u32[]{:S(2)}) copy-start(f32[128,6,256]{2,0,1:T(8,128)} %param.13) | copy-start | bytes 2359300
  24.1 1.8 %copy-start.8 = (f32[296,256]{1,0:T(8,128)S(1)}, f32[296,256]{1,0:T(8,128)}, u32[]{:S(2)}) copy-start(f32[296,256]{1,0:T(8,128)} %get-tuple-element.35.sent_ref) | copy-start | bytes 909316
  24.1 1.8 %copy-start.9 = (f32[128,128]{1,0:T(8,128)S(1)}, f32[128,128]{1,0:T(8,128)}, u32[]{:S(2)}) copy-start(f32[128,128]{1,0:T(8,128)} %get-tuple-element.34.factor_ref) | copy-start | bytes 196612
  25.4 1.8 %collective-permute-start.9 = (f32[104,384]{1,0:T(8,128)S(1)}, f32[104,384]{1,0:T(8,128)S(1)}, u32[]{:S(2)}, u32[]{:S(2)}) collective-permute-start(f32[104,384]{1,0:T(8,128)S(1)} %get-tuple-element.54), channel_id=1, source_target_pairs={{0,1},{1,0},{2,3},{3,2},{4,5},{5,4},{6,7},{7,6},{8,9},{9,8},{10,11... | collective-permute-start | bytes 479240 | tf_op jit(solution)/shard_map/ppermute | solution.py:742
  27.2 13.5 %copy-start.1 = (f32[128,6,256]{2,0,1:T(8,128)S(1)}, f32[128,6,256]{2,0,1:T(8,128)}, u32[]{:S(2)}) copy-start(f32[128,6,256]{2,0,1:T(8,128)} %param.12) | copy-start | bytes 2359300

commit v7 on v5

--- a/solution.py
+++ b/solution.py
@@ -144,8 +144,11 @@
 def edge_rows(fields, solid):
     rows, width = solid.shape
     sources = fields + [solid] * (TILE - len(fields))
-    columns = [x[:, :1] for x in sources] + [x[:, width - 1 :] for x in sources]
-    table = jnp.concatenate(columns + [jnp.zeros((rows, LANES - 2 * TILE), F32)], axis=1)
+    lane = lanes_of((rows, LANES))
+    table = jnp.zeros((rows, LANES), F32)
+    for i, x in enumerate(sources):
+        table = jnp.where(lane == i, pltpu.roll(x[:, :LANES], i, 1) if i else x[:, :LANES], table)
+        table = jnp.where(lane == TILE + i, pltpu.roll(x[:, width - LANES :], TILE + i + 1, 1), table)
     if rows < LANES:
         table = jnp.concatenate([table, jnp.zeros((LANES - rows, LANES), F32)], axis=0)
     table = table.T
@@ -201,15 +204,15 @@
             keep_out[last, :] = jnp.concatenate(
                 edge_rows(fields, jnp.concatenate([solid, solid_tail], axis=0)), axis=1
             )
-            leaving.append(copy(keep_out.at[last], keep_ref.at[last], out_sems.at[pairs]))
+            leaving.append(copy(keep_out.at[last], keep_ref.at[last], out_sems.at[comps]))
         moving[g][1].wait()
         moving[g][2].wait()
         for q in (2 * g, 2 * g + 1):
-            keep_out[pl.ds(q * inner, inner), :] = local_part(
+            rows = pl.ds(q * inner, inner)
+            keep_out[rows, :] = local_part(
                 q, disp_in[q, around], inside, solid, factor, load_in[q], stiff_in[q], disp_in[q ^ 1, around]
             )
-        rows = pl.ds(2 * g * inner, 2 * inner)
-        leaving.append(copy(keep_out.at[rows], keep_ref.at[rows], out_sems.at[g]))
+            leaving.append(copy(keep_out.at[rows], keep_ref.at[rows], out_sems.at[q]))
     for one in leaving:
         one.wait()
 
@@ -705,7 +708,7 @@
         [sent], [HBM] * 6, 10 * comps * inner * width, block,
         small + [pltpu.VMEM((comps, rows, width), F32) for rows in (inner, reach, inner)]
         + [pltpu.VMEM((reach, width), jnp.int32), pltpu.VMEM(sent, F32), pltpu.VMEM((slab, LANES), F32)]
-        + [pltpu.SemaphoreType.DMA((3 + 3 * comps // 2,)), pltpu.SemaphoreType.DMA((1 + comps // 2,))],
+        + [pltpu.SemaphoreType.DMA((3 + 3 * comps // 2,)), pltpu.SemaphoreType.DMA((1 + comps,))],
         FULL, [HBM],
     )(*arguments)
     other, edge, factor, near, other_side = call(

time: 42.2 us -> 42.2 us (level)
  no operation moved by 1% of the time
where the time goes in v7:
time: 42.2 us; the launch traced here: 42 us
  Pallas kernels  13.9 us (33%)
  blocking collectives  13.2 us (31%)
  starting transfers between devices  8.67 us (21%)
  waiting for transfers between devices  3.22 us (8%)
  local copies, waits for them, and re-layouts  2.2 us (5%)
  between operations  0.82 us (2%)
    all_to_all x1, blocking collectives, shards(): gathered = lax.all_to_all(sums, ('ax', 'sec'), 0, 0, tiled=True)  13.2 us
    ppermute x8, starting transfers between devices, to(): return lax.ppermute(x, 'sec', [(i, i ^ mask) for i in range(sec)])  6.15 us
    pallas_call x2, Pallas kernels, transform_call(): call(functools.partial(transform_kernel, comps, main, at_end, edge_at, ho...  4.04 us
    pallas_call x1, Pallas kernels, shards(): call(functools.partial(second_kernel, end, comps, ax), 'second', shapes,...  3.4 us
    ppermute x8, waiting for transfers between devices, to(): return lax.ppermute(x, 'sec', [(i, i ^ mask) for i in range(sec)])  3.21 us
    pallas_call x1, Pallas kernels, shards(): call(functools.partial(first_kernel, end, comps, ax), 'first', [sent], [H...  2.55 us
    unnamed x26, local copies, waits for them, and re-layouts  2.2 us
    ppermute x1, starting transfers between devices, shards(): near = lax.ppermute(near, 'ax', [(i, i ^ 1) for i in range(ax)])  1.88 us
  transfers between devices with their start and end apart: 10, of which 3 were waited for; matrix products, arithmetic and copies ran while one was open for 0% of the time, Pallas kernels for 22%

profile of v7, /device:TPU:0, one launch (start us, length us, event | category | flops | bytes accessed | tf_op | source)
XLA Modules:
  0.0 42.0 jit_solution(3128153249342809858)
XLA Ops:
  0.6 2.6 %first.1.own_ref = f32[296,256]{1,0:T(8,128)} custom-call(f32[4,6]{1,0:T(4,128)} %table_ref.3, s32[1,128]{1,0:T(1,128)} %bitcast.22, f32[6,128,256]{2,1,0:T(8,128)} %bitcast.20, f32[6,128,256]{2,1,0:T(8,128)} %bitcast.15, f32[6,128,256]{2,1,0:T(8,128)} %bitcast.11, s32[128,256]{1,0:T(8,128)} %hole_ref.11), custom_call_target="tpu_custom_call" | custom-call | flops 737280 | bytes 786432 | tf_op jit(solution)/shard_map/first/pallas_call | solution.py:706
  3.2 0.0 copy-start.2
  3.2 0.0 copy-start.6
  3.2 0.0 copy-start.8
  3.2 3.0 %collective-permute-start.5 = (f32[296,256]{1,0:T(8,128)}, f32[296,256]{1,0:T(8,128)S(1)}, u32[]{:S(2)}, u32[]{:S(2)}) collective-permute-start(f32[296,256]{1,0:T(8,128)} %first.1.own_ref), channel_id=1, source_target_pairs={{0,2},{1,3},{2,0},{3,1},{4,6},{5,7},{6,4},{7,5},{8,10},{9,11},{10,... | collective-permute-start | bytes 909320 | tf_op jit(solution)/shard_map/ppermute | solution.py:724
  6.3 3.4 %second.1 = (f32[296,256]{1,0:T(8,128)}, f32[2,112,256]{2,1,0:T(8,128)}, f32[128,128]{1,0:T(8,128)}, f32[16,256]{1,0:T(8,128)}, f32[16,256]{1,0:T(8,128)}) custom-call(f32[4,6]{1,0:T(4,128)} %table_ref.3, s32[1,128]{1,0:T(1,128)} %bitcast.23, f32[6,128,256]{2,1,0:T(8,128)} %bitcast.21, f32[6,128,256]{2,1,0:T(8,128)} %bitcast.16, f32[6,128,256]{2,1,0:T(8,128)} %bitcast.12, ...), custom_call_target="tpu_custom_call" | custom-call | flops 1966080 | bytes 1572864 | tf_op jit(solution)/shard_map/second/pallas_call | solution.py:714
  9.7 0.1 collective-permute-start.6
  9.7 0.2 collective-permute-start.4
  10.0 1.9 %collective-permute-start = (f32[16,256]{1,0:T(8,128)}, f32[16,256]{1,0:T(8,128)S(1)}, u32[]{:S(2)}, u32[]{:S(2)}) collective-permute-start(f32[16,256]{1,0:T(8,128)} %get-tuple-element.38), channel_id=1, source_target_pairs={{0,4},{4,0},{8,12},{12,8},{16,20},{20,16},{24,28},{28,24},{1,5},{5... | collective-permute-start | bytes 49160 | tf_op jit(solution)/shard_map/ppermute | solution.py:730
  11.8 0.7 %collective-permute-start.1 = (f32[16,256]{1,0:T(8,128)}, f32[16,256]{1,0:T(8,128)S(1)}, u32[]{:S(2)}, u32[]{:S(2)}) collective-permute-start(f32[16,256]{1,0:T(8,128)} %get-tuple-element.39), channel_id=1, source_target_pairs={{4,8},{8,4},{12,16},{16,12},{20,24},{24,20},{5,9},{9,5},{13,17},{1... | collective-permute-start | bytes 49160 | tf_op jit(solution)/shard_map/ppermute | solution.py:731
  12.5 0.0 copy-done.2
  12.5 0.0 copy-done.6
  12.5 0.0 copy-done.8
  12.5 0.0 copy-start.3
  12.5 1.2 %copy-done.3 = bf16[4,2,256,256]{3,2,1,0:T(8,128)(2,1)S(1)} copy-done((bf16[4,2,256,256]{3,2,1,0:T(8,128)(2,1)S(1)}, bf16[4,2,256,256]{3,2,1,0:T(8,128)(2,1)}, u32[]{:S(2)}) %copy-start.3) | copy-done | bytes 1048600
  13.8 0.9 %copy-done.12 = f32[6,6,1024]{2,1,0:T(8,128)S(1)} copy-done((f32[6,6,1024]{2,1,0:T(8,128)S(1)}, f32[6,6,1024]{2,1,0:T(8,128)}, u32[]{:S(2)}) %copy-start.12) | copy-done | bytes 147480
  14.7 1.0 %fold.1 = (f32[36,8,640]{2,1,0:T(8,128)S(1)}, f32[6,8,640]{2,1,0:T(8,128)S(1)}) custom-call(f32[6,6,1024]{2,1,0:T(8,128)S(1)} %copy-done.12, bf16[4,2,256,256]{3,2,1,0:T(8,128)(2,1)S(1)} %copy-done.3, bf16[2,2,256,256]{3,2,1,0:T(8,128)(2,1)S(1)} %copy-done.6, bf16[2,512,512]{2,1,0:T(8,128)(2,1)S(1)} %copy-done.2, f32[4,8,1024]{2,1,0:T(8,128)S(1)} %copy-done.8), custom_call_target="tpu_custom_call" | custom-call | flops 1 | bytes 1 | tf_op jit(solution)/shard_map/fold/pallas_call | solution.py:732
  15.7 0.0 copy-start.5
  15.7 0.0 collective-permute-done.near_ref
  15.7 0.0 collective-permute-done.1.next_ref
  15.7 0.0 copy-done.11
  15.7 0.1 ends.1
  15.8 1.6 %collective-permute-start.3 = (f32[104,256]{1,0:T(8,128)S(1)}, f32[104,256]{1,0:T(8,128)S(1)}, u32[]{:S(2)}, u32[]{:S(2)}) collective-permute-start(f32[104,256]{1,0:T(8,128)S(1)} %get-tuple-element.40.own_ref), channel_id=1, source_target_pairs={{0,2},{1,3},{2,0},{3,1},{4,6},{5,7},{6,4},{7,5},{8,10},{9,11},{10,... | collective-permute-start | bytes 319496 | tf_op jit(solution)/shard_map/ppermute | solution.py:724
  17.4 0.0 collective-permute-start.7
  17.4 0.0 collective-permute-done.5.across_ref
  17.4 0.6 %collective-permute-start.2 = (f32[104,256]{1,0:T(8,128)S(1)}, f32[104,256]{1,0:T(8,128)S(1)}, u32[]{:S(2)}, u32[]{:S(2)}) collective-permute-start(f32[104,256]{1,0:T(8,128)S(1)} %get-tuple-element.41.sent_ref), channel_id=1, source_target_pairs={{0,1},{1,0},{2,3},{3,2},{4,5},{5,4},{6,7},{7,6},{8,9},{9,8},{10,11... | collective-permute-start | bytes 319496 | tf_op jit(solution)/shard_map/ppermute | solution.py:724
  18.0 2.6 %collective-permute-done.6.both_ref = f32[296,256]{1,0:T(8,128)S(1)} collective-permute-done((f32[296,256]{1,0:T(8,128)}, f32[296,256]{1,0:T(8,128)S(1)}, u32[]{:S(2)}, u32[]{:S(2)}) %collective-permute-start.6) | collective-permute-done | bytes 303136 | tf_op jit(solution)/shard_map/ppermute | solution.py:724
  20.7 0.0 collective-permute-done.4.core_ref
  20.7 0.0 copy-done.4
  20.7 0.0 copy-done.7
  20.7 0.0 copy-done.5
  20.7 2.8 %transform.2 = (f32[128,128]{1,0:T(8,128)S(1)}, f32[288,384]{1,0:T(8,128)S(1)}, f32[6,48,256]{2,1,0:T(8,128)S(1)}, f32[288,384]{1,0:T(8,128)S(1)}) custom-call(f32[296,256]{1,0:T(8,128)S(1)} %copy-done.7, f32[296,256]{1,0:T(8,128)S(1)} %collective-permute-done.4.core_ref, f32[296,256]{1,0:T(8,128)S(1)} %collective-permute-done.5.across_ref, ...), custom_call_target="tpu_custom_call" | custom-call | tf_op jit(solution)/shard_map/transform/pallas_call | solution.py:675
  23.5 0.0 collective-permute-done.3.across_ref
  23.5 0.1 collective-permute-start.8
  23.6 0.5 %collective-permute-done.7.both_ref = f32[104,256]{1,0:T(8,128)S(1)} collective-permute-done((f32[104,256]{1,0:T(8,128)S(1)}, f32[104,256]{1,0:T(8,128)S(1)}, u32[]{:S(2)}, u32[]{:S(2)}) %collective-permute-start.7) | collective-permute-done | bytes 106528 | tf_op jit(solution)/shard_map/ppermute | solution.py:724
  24.1 0.0 collective-permute-done.2.core_ref
  24.1 1.2 %transform.3 = (f32[104,384]{1,0:T(8,128)S(1)}, f32[6,16,256]{2,1,0:T(8,128)S(1)}, f32[104,384]{1,0:T(8,128)S(1)}) custom-call(f32[104,256]{1,0:T(8,128)S(1)} %get-tuple-element.40.own_ref, f32[104,256]{1,0:T(8,128)S(1)} %collective-permute-done.2.core_ref, f32[104,256]{1,0:T(8,128)S(1)} %collective-permute-done.3.across_ref, ...), custom_call_target="tpu_custom_call" | custom-call | flops 45298483200 | bytes 78643200 | tf_op jit(solution)/shard_map/transform/pallas_call | solution.py:675
  25.3 0.5 %collective-permute-start.9 = (f32[104,384]{1,0:T(8,128)S(1)}, f32[104,384]{1,0:T(8,128)S(1)}, u32[]{:S(2)}, u32[]{:S(2)}) collective-permute-start(f32[104,384]{1,0:T(8,128)S(1)} %get-tuple-element.54), channel_id=1, source_target_pairs={{0,1},{1,0},{2,3},{3,2},{4,5},{5,4},{6,7},{7,6},{8,9},{9,8},{10,11... | collective-permute-start | bytes 479240 | tf_op jit(solution)/shard_map/ppermute | solution.py:724
  25.8 0.0 collective-permute-done.8.back_ref
  25.9 0.0 copy-done
  25.9 0.0 copy-done.9
  25.9 0.0 copy-done.10
  25.9 0.9 %early.1 = (f32[6,96,384]{2,1,0:T(8,128)S(1)}, f32[6,96,256]{2,1,0:T(8,128)S(1)}, f32[6,80,256]{2,1,0:T(8,128)S(1)}, f32[40,256]{1,0:T(8,128)S(1)}) custom-call(f32[6,128,256]{2,1,0:T(8,128)S(1)} %bitcast.13, s32[128,256]{1,0:T(8,128)S(1)} %copy-done.5, f32[128,128]{1,0:T(8,128)S(1)} %copy-done.10, f32[288,384]{1,0:T(8,128)S(1)} %get-tuple-element.45.own_ref, ...), custom_call_target="tpu_custom_call" | custom-call | flops 5898240 | bytes 3145728 | tf_op jit(solution)/shard_map/early/pallas_call | solution.py:755
  26.8 0.1 collective-permute-done.9.back_ref
  26.9 0.6 %late.1 = (f32[6,32,256]{2,1,0:T(8,128)S(1)}, f32[6,32,256]{2,1,0:T(8,128)S(1)}, f32[6,48,256]{2,1,0:T(8,128)S(1)}, f32[32,128]{1,0:T(8,128)S(1)}) custom-call(f32[6,128,256]{2,1,0:T(8,128)S(1)} %bitcast.14, s32[128,256]{1,0:T(8,128)S(1)} %copy-done.5, f32[128,128]{1,0:T(8,128)S(1)} %copy-done.10, f32[6,96,384]{2,1,0:T(8,128)S(1)} %get-tuple-element.52.inner_ref, ...), custom_call_target="tpu_custom_call" | custom-call | flops 1572864 | bytes 786432 | tf_op jit(solution)/shard_map/late/pallas_call | solution.py:760
  27.4 13.2 %all_to_all.11 = f32[32,1,128]{2,1,0:T(1,128)S(1)} all-to-all(f32[32,1,128]{2,1,0:T(1,128)S(1)} %bitcast.19), channel_id=1, replica_groups=mesh['ax'=8,'sec'=4] {'ax','sec'}, dimensions={0} | all-to-all | bytes 32768 | tf_op jit(solution)/shard_map/all_to_all | solution.py:765
  40.6 0.0 copy-done.1
  40.6 1.3 %update.1 = (f32[6,128,256]{2,1,0:T(8,128)}, f32[6,128,256]{2,1,0:T(8,128)}, f32[1,3]{1,0:T(1,128)}) custom-call(f32[6,128,256]{2,1,0:T(8,128)S(1)} %bitcast.17, f32[32,128]{1,0:T(8,128)S(1)} %bitcast.18, f32[6,96,384]{2,1,0:T(8,128)S(1)} %get-tuple-element.52.inner_ref, f32[6,96,256]{2,1,0:T(8,128)S(1)} %get-tuple-element.53.inner_residual_ref, ...), custom_call_target="tpu_custom_call" | custom-call | flops 786432 | bytes 4718592 | tf_op jit(solution)/shard_map/update/pallas_call | solution.py:766
  (8 shorter events, 0.0 us)
Async XLA Ops:
  3.2 9.3 %copy-start.2 = (bf16[2,512,512]{2,1,0:T(8,128)(2,1)S(1)}, bf16[2,512,512]{2,1,0:T(8,128)(2,1)}, u32[]{:S(2)}) copy-start(bf16[2,512,512]{2,1,0:T(8,128)(2,1)} %constant.10.clone.refs_2_.odd_ref) | copy-start | bytes 3145732
  3.2 9.3 %copy-start.6 = (bf16[2,2,256,256]{3,2,1,0:T(8,128)(2,1)S(1)}, bf16[2,2,256,256]{3,2,1,0:T(8,128)(2,1)}, u32[]{:S(2)}) copy-start(bf16[2,2,256,256]{3,2,1,0:T(8,128)(2,1)} %constant.9.clone.refs_1_.even_ref) | copy-start | bytes 1572868
  3.2 9.3 %copy-start.8 = (f32[4,8,1024]{2,1,0:T(8,128)S(1)}, f32[4,8,1024]{2,1,0:T(8,128)}, u32[]{:S(2)}) copy-start(f32[4,8,1024]{2,1,0:T(8,128)} %constant.11.clone.refs_3_.beyond_ref) | copy-start | bytes 393220
  3.2 14.2 %collective-permute-start.5 = (f32[296,256]{1,0:T(8,128)}, f32[296,256]{1,0:T(8,128)S(1)}, u32[]{:S(2)}, u32[]{:S(2)}) collective-permute-start(f32[296,256]{1,0:T(8,128)} %first.1.own_ref), channel_id=1, source_target_pairs={{0,2},{1,3},{2,0},{3,1},{4,6},{5,7},{6,4},{7,5},{8,10},{9,11},{10,... | collective-permute-start | bytes 909320 | tf_op jit(solution)/shard_map/ppermute | solution.py:724
  9.7 11.0 %collective-permute-start.6 = (f32[296,256]{1,0:T(8,128)}, f32[296,256]{1,0:T(8,128)S(1)}, u32[]{:S(2)}, u32[]{:S(2)}) collective-permute-start(f32[296,256]{1,0:T(8,128)} %get-tuple-element.42.sent_ref), channel_id=1, source_target_pairs={{0,3},{1,2},{2,1},{3,0},{4,7},{5,6},{6,5},{7,4},{8,11},{9,10},{10,... | collective-permute-start | bytes 909320 | tf_op jit(solution)/shard_map/ppermute | solution.py:724
  9.7 10.9 %collective-permute-start.4 = (f32[296,256]{1,0:T(8,128)}, f32[296,256]{1,0:T(8,128)S(1)}, u32[]{:S(2)}, u32[]{:S(2)}) collective-permute-start(f32[296,256]{1,0:T(8,128)} %get-tuple-element.42.sent_ref), channel_id=1, source_target_pairs={{0,1},{1,0},{2,3},{3,2},{4,5},{5,4},{6,7},{7,6},{8,9},{9,8},{10,11... | collective-permute-start | bytes 909320 | tf_op jit(solution)/shard_map/ppermute | solution.py:724
  10.0 5.7 %collective-permute-start = (f32[16,256]{1,0:T(8,128)}, f32[16,256]{1,0:T(8,128)S(1)}, u32[]{:S(2)}, u32[]{:S(2)}) collective-permute-start(f32[16,256]{1,0:T(8,128)} %get-tuple-element.38), channel_id=1, source_target_pairs={{0,4},{4,0},{8,12},{12,8},{16,20},{20,16},{24,28},{28,24},{1,5},{5... | collective-permute-start | bytes 49160 | tf_op jit(solution)/shard_map/ppermute | solution.py:730
  11.8 3.9 %collective-permute-start.1 = (f32[16,256]{1,0:T(8,128)}, f32[16,256]{1,0:T(8,128)S(1)}, u32[]{:S(2)}, u32[]{:S(2)}) collective-permute-start(f32[16,256]{1,0:T(8,128)} %get-tuple-element.39), channel_id=1, source_target_pairs={{4,8},{8,4},{12,16},{16,12},{20,24},{24,20},{5,9},{9,5},{13,17},{1... | collective-permute-start | bytes 49160 | tf_op jit(solution)/shard_map/ppermute | solution.py:731
  12.5 1.2 %copy-start.3 = (bf16[4,2,256,256]{3,2,1,0:T(8,128)(2,1)S(1)}, bf16[4,2,256,256]{3,2,1,0:T(8,128)(2,1)}, u32[]{:S(2)}) copy-start(bf16[4,2,256,256]{3,2,1,0:T(8,128)(2,1)} %constant.8.clone.refs_0_.forward_ref) | copy-start | bytes 3145732
  13.8 0.9 %copy-start.12 = (f32[6,6,1024]{2,1,0:T(8,128)S(1)}, f32[6,6,1024]{2,1,0:T(8,128)}, u32[]{:S(2)}) copy-start(f32[6,6,1024]{2,1,0:T(8,128)} %precond_ref.1) | copy-start | bytes 442372
  14.7 1.0 %copy-start.11 = (f32[2,112,256]{2,1,0:T(8,128)S(1)}, f32[2,112,256]{2,1,0:T(8,128)}, u32[]{:S(2)}) copy-start(f32[2,112,256]{2,1,0:T(8,128)} %get-tuple-element.37.ends_ref) | copy-start | bytes 688132
  14.7 6.0 %copy-start.4 = (bf16[4,2,256,256]{3,2,1,0:T(8,128)(2,1)S(1)}, bf16[4,2,256,256]{3,2,1,0:T(8,128)(2,1)}, u32[]{:S(2)}) copy-start(bf16[4,2,256,256]{3,2,1,0:T(8,128)(2,1)} %constant.8.clone.refs_0_.forward_ref) | copy-start | bytes 3145732
  14.7 6.0 %copy-start.7 = (f32[296,256]{1,0:T(8,128)S(1)}, f32[296,256]{1,0:T(8,128)}, u32[]{:S(2)}) copy-start(f32[296,256]{1,0:T(8,128)} %first.1.own_ref) | copy-start | bytes 909316
  15.7 5.0 %copy-start.5 = (s32[128,256]{1,0:T(8,128)S(1)}, s32[128,256]{1,0:T(8,128)}, u32[]{:S(2)}) copy-start(s32[128,256]{1,0:T(8,128)} %hole_ref.11) | copy-start | bytes 393220
  15.8 7.7 %collective-permute-start.3 = (f32[104,256]{1,0:T(8,128)S(1)}, f32[104,256]{1,0:T(8,128)S(1)}, u32[]{:S(2)}, u32[]{:S(2)}) collective-permute-start(f32[104,256]{1,0:T(8,128)S(1)} %get-tuple-element.40.own_ref), channel_id=1, source_target_pairs={{0,2},{1,3},{2,0},{3,1},{4,6},{5,7},{6,4},{7,5},{8,10},{9,11},{10,... | collective-permute-start | bytes 319496 | tf_op jit(solution)/shard_map/ppermute | solution.py:724
  17.4 6.6 %collective-permute-start.7 = (f32[104,256]{1,0:T(8,128)S(1)}, f32[104,256]{1,0:T(8,128)S(1)}, u32[]{:S(2)}, u32[]{:S(2)}) collective-permute-start(f32[104,256]{1,0:T(8,128)S(1)} %get-tuple-element.41.sent_ref), channel_id=1, source_target_pairs={{0,3},{1,2},{2,1},{3,0},{4,7},{5,6},{6,5},{7,4},{8,11},{9,10},{10,... | collective-permute-start | bytes 319496 | tf_op jit(solution)/shard_map/ppermute | solution.py:724
  17.4 6.6 %collective-permute-start.2 = (f32[104,256]{1,0:T(8,128)S(1)}, f32[104,256]{1,0:T(8,128)S(1)}, u32[]{:S(2)}, u32[]{:S(2)}) collective-permute-start(f32[104,256]{1,0:T(8,128)S(1)} %get-tuple-element.41.sent_ref), channel_id=1, source_target_pairs={{0,1},{1,0},{2,3},{3,2},{4,5},{5,4},{6,7},{7,6},{8,9},{9,8},{10,11... | collective-permute-start | bytes 319496 | tf_op jit(solution)/shard_map/ppermute | solution.py:724
  23.5 2.4 %collective-permute-start.8 = (f32[288,384]{1,0:T(8,128)S(1)}, f32[288,384]{1,0:T(8,128)S(1)}, u32[]{:S(2)}, u32[]{:S(2)}) collective-permute-start(f32[288,384]{1,0:T(8,128)S(1)} %get-tuple-element.50), channel_id=1, source_target_pairs={{0,1},{1,0},{2,3},{3,2},{4,5},{5,4},{6,7},{7,6},{8,9},{9,8},{10,11... | collective-permute-start | bytes 1327112 | tf_op jit(solution)/shard_map/ppermute | solution.py:724
  24.1 1.8 %copy-start = (f32[128,6,256]{2,0,1:T(8,128)S(1)}, f32[128,6,256]{2,0,1:T(8,128)}, u32[]{:S(2)}) copy-start(f32[128,6,256]{2,0,1:T(8,128)} %param.13) | copy-start | bytes 2359300
  24.1 1.8 %copy-start.9 = (f32[296,256]{1,0:T(8,128)S(1)}, f32[296,256]{1,0:T(8,128)}, u32[]{:S(2)}) copy-start(f32[296,256]{1,0:T(8,128)} %get-tuple-element.42.sent_ref) | copy-start | bytes 909316
  24.1 1.8 %copy-start.10 = (f32[128,128]{1,0:T(8,128)S(1)}, f32[128,128]{1,0:T(8,128)}, u32[]{:S(2)}) copy-start(f32[128,128]{1,0:T(8,128)} %get-tuple-element.49.factor_ref) | copy-start | bytes 196612
  25.3 1.6 %collective-permute-start.9 = (f32[104,384]{1,0:T(8,128)S(1)}, f32[104,384]{1,0:T(8,128)S(1)}, u32[]{:S(2)}, u32[]{:S(2)}) collective-permute-start(f32[104,384]{1,0:T(8,128)S(1)} %get-tuple-element.54), channel_id=1, source_target_pairs={{0,1},{1,0},{2,3},{3,2},{4,5},{5,4},{6,7},{7,6},{8,9},{9,8},{10,11... | collective-permute-start | bytes 479240 | tf_op jit(solution)/shard_map/ppermute | solution.py:724
  26.9 13.8 %copy-start.1 = (f32[128,6,256]{2,0,1:T(8,128)S(1)}, f32[128,6,256]{2,0,1:T(8,128)}, u32[]{:S(2)}) copy-start(f32[128,6,256]{2,0,1:T(8,128)} %param.12) | copy-start | bytes 2359300
